TPU v7x, 32 devices: a whole 2x2x4 slice. The times are simulated.
32 devices in a mesh: section: 2 (over x), dp: 4 (over y, core), tensor: 4 (over z).
Axes of the slice: x: 2, y: 2, z: 4, core: 2. Of those that a mesh axis runs over, the one named last changes fastest.
Arguments:
- block_input: bfloat16 [8, 1024, 768], P('dp', 'tensor'), may hold values from -6 to 6
- cotangent: bfloat16 [8, 1024, 768], P('dp', 'tensor'), may hold values from -6 to 6
- query_key_value_weights: bfloat16 [2, 3, 768, 768], P('section', None, 'dp', 'tensor'), may hold values from -0.21875 to 0.21875
- attention_output_weights: bfloat16 [2, 768, 768], P('section', 'tensor', 'dp'), may hold values from -1.75 to 1.75
- bias_table: bfloat16 [2, 32, 12], P('section'), may hold values from -6 to 6
- norm_first: bfloat16 [2, 768], P('section'), may hold values from 0.5 to 1.5
- norm_second: bfloat16 [2, 768], P('section'), may hold values from 0.5 to 1.5
- router_projection_weights: bfloat16 [2, 768, 4], P('section'), may hold values from -0.15625 to 0.15625
- expert_up: bfloat16 [2, 4, 768, 3072], P('section', 'dp', None, 'tensor'), may hold values from -0.21875 to 0.21875
- expert_down: bfloat16 [2, 4, 3072, 768], P('section', 'dp', 'tensor'), may hold values from -0.4375 to 0.4375
- routes: int32 [2, 8, 1024, 1], P('section', 'dp'), may hold values from 0 to 3; in each aligned block of 1024 rows (0 to 1023, 1024 to 2047, ..., all dimensions but the last counted through in order) at most 320 rows name the same one
- prefix_lengths: int32 [8], P('dp'), may hold values from 1 to 1024
- relative_buckets: int32 [2047], replicated, may hold values from 0 to 31
Outputs:
- layer_outputs: bfloat16 [2, 8, 1024, 768], P('section', 'dp', 'tensor')
- input_grads: bfloat16 [2, 8, 1024, 768], P('section', 'dp', 'tensor')
- input_weights_grad: float32 [2, 3, 768, 768], P('section', None, 'dp', 'tensor')
- output_weights_grad: float32 [2, 768, 768], P('section', 'tensor', 'dp')
- bias_table_grad: float32 [2, 32, 12], P('section')
- norm_first_grad: float32 [2, 768], P('section')
- norm_second_grad: float32 [2, 768], P('section')
- router_weights_grad: float32 [2, 768, 4], P('section')
- expert_up_grad: float32 [2, 4, 768, 3072], P('section', 'dp', None, 'tensor')
- expert_down_grad: float32 [2, 4, 3072, 768], P('section', 'dp', 'tensor')
Inputs may be any that keep to these rules, and one draw needn't show every extreme that they name: `routes`: in every aligned block of 1024 rows (one micro-batch of one index of dp) no expert is named by more than 320 rows, and in some block one expert is named by exactly 320 rows.
All inputs are finite; a program needn't handle non-finite values.
Results may differ from a plain program's by a relative error of at most 0.034.
Values may be sent and summed in bfloat16 or wider, within the bound.
No kernel may reach another device: no remote copies, remote signals or barrier semaphores. Data moves between devices by JAX's collectives and lax.ppermute only.
A program may use at most 256 MiB of HBM per device.

v0:
```python
import jax
import jax.numpy as jnp
from jax import lax
from jax.sharding import PartitionSpec as P

HEADS = 12
HEAD_DIM = 64
SEQ_MB = 1
MICRO = 2


EPSILON = 1e-06
MASKED = -1000000000.0
MATMUL_PRECISION = lax.Precision.HIGHEST


def passed_along(block, axis, distance):
    devices = range(lax.axis_size(axis))
    route = [(i - distance, i) for i in devices if i - distance in devices]
    return lax.ppermute(block, axis, route)


def row_norm(values, gain):
    scale = lax.rsqrt(jnp.mean(values * values, -1, keepdims=True) + EPSILON)
    return (scale, (values * scale * gain).astype(jnp.bfloat16))


def norm_backward(values, scale, gain, grad_normed):
    scaled = grad_normed * gain
    grad_values = scale * scaled - values * scale * scale * scale * jnp.mean(
        scaled * values, -1, keepdims=True
    )
    grad_gain = jnp.sum(grad_normed * values * scale, axis=(0, 1))
    return (grad_values, grad_gain)


def gather_rows(values):
    return lax.all_gather(values, "tensor", axis=1, tiled=True)


def sum_rows(values):
    return lax.psum_scatter(
        values.astype(jnp.bfloat16), "tensor", scatter_dimension=1, tiled=True
    ).astype(jnp.float32)


def fetch_heads(query_key_value_weights, attention_output_weights):
    return (
        lax.all_gather(query_key_value_weights[0], "dp", axis=1, tiled=True),
        lax.all_gather(attention_output_weights[0], "dp", axis=1, tiled=True),
    )


def to_experts(buffers):
    return lax.all_to_all(buffers, "dp", split_axis=0, concat_axis=1, tiled=True)


def from_experts(produced):
    return lax.all_to_all(
        produced.astype(jnp.bfloat16), "dp", split_axis=1, concat_axis=0, tiled=True
    ).astype(produced.dtype)


def reduce_heads(grad_in, grad_out):
    return (
        lax.psum_scatter(
            grad_in.astype(jnp.bfloat16), "dp", scatter_dimension=1, tiled=True
        ).astype(jnp.float32),
        lax.psum_scatter(
            grad_out.astype(jnp.bfloat16), "dp", scatter_dimension=1, tiled=True
        ).astype(jnp.float32),
    )


def bias_block(rel_rows, row_start, block_rows, seq_len):
    heads_local = rel_rows.shape[0]
    width = seq_len + block_rows - 1
    window = lax.dynamic_slice_in_dim(rel_rows, seq_len - block_rows - row_start, width, 1)
    tiled = jnp.broadcast_to(window[:, None, :], (heads_local, block_rows, width)).reshape(
        heads_local, block_rows * width
    )
    skewed = tiled[:, block_rows - 1 : block_rows - 1 + block_rows * (width - 1)].reshape(
        heads_local, block_rows, width - 1
    )
    return skewed[:, :, :seq_len]


def block_scores(query_rows, key_rows, row_start, prefix_one, rel_rows):
    heads_local, block_rows, head_dim = query_rows.shape
    seq_len = key_rows.shape[1]
    key_pos = jnp.arange(seq_len, dtype=jnp.int32)
    row_pos = row_start + jnp.arange(block_rows, dtype=jnp.int32)
    scores = jnp.einsum(
        "hbd,hld->hbl", query_rows, key_rows, preferred_element_type=jnp.float32
    ) * head_dim ** (-0.5)
    scores = scores + bias_block(rel_rows, row_start, block_rows, seq_len)
    allowed = (key_pos[None, :] <= row_pos[:, None]) | (key_pos[None, :] < prefix_one)
    return jnp.where(allowed[None], scores, MASKED)


def diagonal_sums(values):
    heads_local, block_rows, key_len = values.shape
    width = key_len + block_rows
    padded = jnp.pad(values, ((0, 0), (0, 0), (block_rows, 0)))
    flat = jnp.pad(padded.reshape(heads_local, block_rows * width), ((0, 0), (0, block_rows)))
    return jnp.sum(flat.reshape(heads_local, block_rows, width + 1), 1)


def attend(queries, key_rows, value_rows, prefix_one, rel_rows):
    heads_local, seq_len, head_dim = queries.shape
    block_rows = min(512, seq_len)

    def one_block(row_start):
        query_rows = lax.dynamic_slice_in_dim(queries, row_start, block_rows, 1)
        scores = block_scores(query_rows, key_rows, row_start, prefix_one, rel_rows)
        top_score = jnp.max(scores, -1, keepdims=True)
        weights = jnp.exp(scores - top_score)
        totals = jnp.sum(weights, -1, keepdims=True)
        weights_low = (weights / totals).astype(jnp.bfloat16)
        output = jnp.einsum(
            "hbl,hld->hbd", weights_low, value_rows, preferred_element_type=jnp.float32
        )
        return (output.astype(jnp.bfloat16), (top_score + jnp.log(totals))[..., 0])

    starts = jnp.arange(seq_len // block_rows, dtype=jnp.int32) * block_rows
    outputs, log_sums = lax.map(one_block, starts)
    return (jnp.transpose(outputs, (1, 0, 2, 3)).reshape(queries.shape), log_sums)


def attend_backward(queries, key_rows, value_rows, prefix_one, rel_rows, log_sums, grad_output):
    heads_local, seq_len, head_dim = queries.shape
    block_rows = min(512, seq_len)
    scaling = head_dim ** (-0.5)
    span = seq_len + block_rows + 1

    def one_block(running, element):
        grad_keys, grad_values, diag_total = running
        row_start, lse_block = element
        query_rows = lax.dynamic_slice_in_dim(queries, row_start, block_rows, 1)
        grad_rows = lax.dynamic_slice_in_dim(grad_output, row_start, block_rows, 1)
        scores = block_scores(query_rows, key_rows, row_start, prefix_one, rel_rows)
        weights = jnp.exp(scores - lse_block[..., None])
        grad_weights = jnp.einsum(
            "hbd,hld->hbl", grad_rows, value_rows, preferred_element_type=jnp.float32
        )
        grad_scores = (
            weights * (grad_weights - jnp.sum(weights * grad_weights, -1, keepdims=True))
        ).astype(jnp.bfloat16)
        grad_query = (
            jnp.einsum("hbl,hld->hbd", grad_scores, key_rows, preferred_element_type=jnp.float32)
            * scaling
        ).astype(jnp.bfloat16)
        grad_keys = (
            grad_keys
            + jnp.einsum(
                "hbl,hbd->hld", grad_scores, query_rows, preferred_element_type=jnp.float32
            )
            * scaling
        )
        grad_values = grad_values + jnp.einsum(
            "hbl,hbd->hld",
            weights.astype(jnp.bfloat16),
            grad_rows,
            preferred_element_type=jnp.float32,
        )
        sums = diagonal_sums(grad_scores.astype(jnp.float32))
        start = seq_len - block_rows - row_start
        current = lax.dynamic_slice_in_dim(diag_total, start, span, 1)
        diag_total = lax.dynamic_update_slice_in_dim(diag_total, current + sums, start, 1)
        return ((grad_keys, grad_values, diag_total), grad_query)

    starts = jnp.arange(seq_len // block_rows, dtype=jnp.int32) * block_rows
    zeros_rows = jnp.zeros(queries.shape, jnp.float32)
    diag_zero = jnp.zeros((heads_local, 2 * seq_len + 1), jnp.float32)
    final, grad_queries = lax.scan(
        one_block, (zeros_rows, zeros_rows, diag_zero), (starts, log_sums)
    )
    grad_keys, grad_values, diag_total = final
    grad_rel = diag_total[:, 1 : 2 * seq_len]
    grad_queries = jnp.transpose(grad_queries, (1, 0, 2, 3)).reshape(queries.shape)
    return (
        grad_queries,
        grad_keys.astype(jnp.bfloat16),
        grad_values.astype(jnp.bfloat16),
        grad_rel,
    )


def route_slots(routes_flat, experts_all, capacity):
    count_rows = routes_flat.shape[0]
    onehot = (routes_flat[:, None] == jnp.arange(experts_all, dtype=jnp.int32)[None, :]).astype(
        jnp.int32
    )
    slot_index = jnp.sum((jnp.cumsum(onehot, 0) - 1) * onehot, 1)
    target = routes_flat * capacity + slot_index
    source = (
        jnp.full((experts_all * capacity,), count_rows, jnp.int32)
        .at[target]
        .set(jnp.arange(count_rows, dtype=jnp.int32))
    )
    return (target, source)


def dispatch(rows_all, source):
    padded = jnp.concatenate([rows_all, jnp.zeros((1, rows_all.shape[1]), rows_all.dtype)], 0)
    return jnp.take(padded, source, axis=0)


def expert_forward(buffers, up_used, down_used):
    arrived = to_experts(buffers)
    hidden = jnp.einsum("ecd,edf->ecf", arrived, up_used, preferred_element_type=jnp.float32)
    activated = jax.nn.gelu(hidden).astype(jnp.bfloat16)
    produced = jnp.einsum("ecf,efd->ecd", activated, down_used, preferred_element_type=jnp.float32)
    produced = from_experts(produced)
    return (arrived, hidden, activated, produced)


def expert_backward(arrived, hidden, activated, grad_buffers, up_used, down_used):
    grad_arrived = to_experts(grad_buffers)
    grad_down = jnp.einsum(
        "ecf,ecd->efd", activated, grad_arrived, preferred_element_type=jnp.float32
    )
    grad_active = jnp.einsum(
        "ecd,efd->ecf", grad_arrived, down_used, preferred_element_type=jnp.float32
    )
    grad_hidden = jax.vjp(jax.nn.gelu, hidden)[1](grad_active)[0].astype(jnp.bfloat16)
    grad_up = jnp.einsum("ecd,ecf->edf", arrived, grad_hidden, preferred_element_type=jnp.float32)
    grad_rows = jnp.einsum("ecf,edf->ecd", grad_hidden, up_used, preferred_element_type=jnp.float32)
    grad_rows = from_experts(grad_rows)
    return (grad_up, grad_down, grad_rows)


def layer_forward(section_in, params, head_used, expert_used, routes_mb, prefix_mb, rel_onehot):
    gain_one, bias_table, gain_two, router_projection_weights = params
    input_weight_slice, output_weight_slice = head_used
    up_used, down_used = expert_used
    tensor_id = lax.axis_index("tensor")
    sequences, piece_rows, model_width = section_in.shape
    seq_len = routes_mb.shape[1]
    heads_local = input_weight_slice.shape[2] // HEAD_DIM
    table_local = lax.dynamic_slice_in_dim(bias_table, tensor_id * heads_local, heads_local, 1)
    rel_rows = jnp.dot(table_local.T, rel_onehot.T, precision=MATMUL_PRECISION)
    scale_one, first_norm_output = row_norm(section_in, gain_one)
    collected_first_rows = gather_rows(first_norm_output)
    projected_rows = jnp.einsum(
        "trx,vxj->vtrj",
        collected_first_rows,
        input_weight_slice,
        preferred_element_type=jnp.float32,
    ).astype(jnp.bfloat16)
    shaped = projected_rows.reshape(3, sequences, seq_len, heads_local, HEAD_DIM)
    heads_major = jnp.transpose(shaped, (0, 1, 3, 2, 4))
    attended, log_sums = lax.map(
        lambda element: attend(element[0], element[1], element[2], element[3], rel_rows),
        (heads_major[0], heads_major[1], heads_major[2], prefix_mb),
    )
    merged_heads = jnp.transpose(attended, (0, 2, 1, 3)).reshape(
        sequences, seq_len, heads_local * HEAD_DIM
    )
    middle = section_in + sum_rows(
        jnp.einsum(
            "ubz,zv->ubv", merged_heads, output_weight_slice, preferred_element_type=jnp.float32
        )
    )
    scale_two, second_norm_output = row_norm(middle, gain_two)
    router_scores = jnp.dot(
        second_norm_output.reshape(-1, model_width),
        router_projection_weights,
        preferred_element_type=jnp.float32,
    )
    experts_all = router_scores.shape[1]
    router_probs = jax.nn.softmax(router_scores, -1)
    local_routes = lax.dynamic_slice_in_dim(
        routes_mb, tensor_id * piece_rows, piece_rows, 1
    ).reshape(-1)
    chosen = (local_routes[:, None] == jnp.arange(experts_all, dtype=jnp.int32)[None, :]).astype(
        jnp.float32
    )
    gates = jnp.sum(router_probs * chosen, 1).reshape(sequences, piece_rows, 1)
    capacity = (5 * sequences * seq_len + 4 * experts_all - 1) // (4 * experts_all)
    target, source = route_slots(routes_mb.reshape(-1), experts_all, capacity)
    gathered_two = gather_rows(second_norm_output).reshape(-1, model_width)
    buffers = dispatch(gathered_two, source).reshape(experts_all, capacity, model_width)
    arrived, hidden, activated, produced = expert_forward(buffers, up_used, down_used)
    combined = jnp.take(produced.reshape(-1, model_width), target, axis=0).reshape(
        sequences, seq_len, model_width
    )
    expert_out = sum_rows(combined)
    result = middle + gates * expert_out
    saved = (
        scale_one,
        collected_first_rows,
        heads_major,
        log_sums,
        merged_heads,
        output_weight_slice,
        middle,
        scale_two,
        second_norm_output,
        chosen,
        gates,
        target,
        source,
        arrived,
        hidden,
        activated,
        expert_out,
        rel_rows,
    )
    return (result, router_probs, saved)


def layer_backward(
    section_in, grad_result, params, head_used, expert_used, routes_mb, prefix_mb, rel_onehot
):
    gain_one, bias_table, gain_two, router_projection_weights = params
    input_weight_slice, output_weight_slice = head_used
    up_used, down_used = expert_used
    tensor_id = lax.axis_index("tensor")
    sequences, piece_rows, model_width = section_in.shape
    seq_len = routes_mb.shape[1]
    heads_local = input_weight_slice.shape[2] // HEAD_DIM
    result, router_probs, saved = layer_forward(
        section_in, params, head_used, expert_used, routes_mb, prefix_mb, rel_onehot
    )
    (
        scale_one,
        collected_first_rows,
        heads_major,
        log_sums,
        merged_head_rows,
        out_full,
        middle,
        scale_two,
        second_norm_output,
        chosen,
        gates,
        target,
        source,
        arrived,
        hidden,
        activated,
        expert_out,
        rel_rows,
    ) = saved
    experts_all = router_probs.shape[1]
    capacity = (5 * sequences * seq_len + 4 * experts_all - 1) // (4 * experts_all)
    grad_expert = (gates * grad_result).astype(jnp.bfloat16)
    grad_gates = jnp.sum(grad_result * expert_out, -1).reshape(-1, 1)
    grad_gathered = gather_rows(grad_expert).reshape(-1, model_width)
    grad_buffers = dispatch(grad_gathered, source).reshape(experts_all, capacity, model_width)
    grad_up, grad_down, grad_rows = expert_backward(
        arrived, hidden, activated, grad_buffers, up_used, down_used
    )
    grad_combined = jnp.take(grad_rows.reshape(-1, model_width), target, axis=0).reshape(
        sequences, seq_len, model_width
    )
    grad_normed_two = sum_rows(grad_combined)
    grad_probs = chosen * grad_gates
    grad_logits = (
        router_probs * (grad_probs - jnp.sum(router_probs * grad_probs, 1, keepdims=True))
    ).astype(jnp.bfloat16)
    flat_two = second_norm_output.reshape(-1, model_width)
    grad_router = jnp.dot(flat_two.T, grad_logits, preferred_element_type=jnp.float32)
    grad_normed_two = grad_normed_two + jnp.dot(
        grad_logits, router_projection_weights.T, preferred_element_type=jnp.float32
    ).reshape(sequences, piece_rows, model_width)
    grad_middle, grad_gain_two = norm_backward(middle, scale_two, gain_two, grad_normed_two)
    grad_middle = grad_middle + grad_result
    grad_low = grad_middle.astype(jnp.bfloat16)
    residual_branch_grad = gather_rows(grad_low)
    grad_out_proj = jnp.einsum(
        "vjo,vjt->ot", merged_head_rows, residual_branch_grad, preferred_element_type=jnp.float32
    )
    grad_merged = jnp.einsum(
        "cgz,oz->cgo", residual_branch_grad, output_weight_slice, preferred_element_type=jnp.float32
    ).astype(jnp.bfloat16)
    grad_heads = jnp.transpose(
        grad_merged.reshape(sequences, seq_len, heads_local, HEAD_DIM), (0, 2, 1, 3)
    )
    grad_queries, grad_keys, grad_values, grad_rel = lax.map(
        lambda element: attend_backward(
            element[0], element[1], element[2], element[3], rel_rows, element[4], element[5]
        ),
        (heads_major[0], heads_major[1], heads_major[2], prefix_mb, log_sums, grad_heads),
    )
    stacked_grads = jnp.stack([grad_queries, grad_keys, grad_values])
    projected_rows_grad = jnp.transpose(stacked_grads, (0, 1, 3, 2, 4)).reshape(
        3, sequences, seq_len, heads_local * HEAD_DIM
    )
    grad_in_proj = jnp.einsum(
        "get,pgen->ptn",
        collected_first_rows,
        projected_rows_grad,
        preferred_element_type=jnp.float32,
    )
    grad_normed_one = sum_rows(
        jnp.einsum(
            "ehvr,efr->hvf",
            projected_rows_grad,
            input_weight_slice,
            preferred_element_type=jnp.float32,
        )
    )
    grad_input, grad_gain_one = norm_backward(section_in, scale_one, gain_one, grad_normed_one)
    grad_input = grad_input + grad_middle
    grad_table_local = jnp.dot(jnp.sum(grad_rel, 0), rel_onehot, precision=MATMUL_PRECISION).T
    grad_table = lax.dynamic_update_slice_in_dim(
        jnp.zeros((rel_onehot.shape[1], HEADS), jnp.float32),
        grad_table_local,
        tensor_id * heads_local,
        1,
    )
    return (
        grad_input,
        (grad_in_proj, grad_out_proj),
        (grad_up, grad_down),
        (grad_gain_one, grad_table, grad_gain_two, grad_router),
    )


def accumulate(running, addition, is_valid):
    masked = jax.tree.map(lambda member: jnp.where(is_valid, member, 0.0), addition)
    if running is None:
        return masked
    return jax.tree.map(jnp.add, running, masked)


def per_device(
    block_input,
    cotangent,
    query_key_value_weights,
    attention_output_weights,
    bias_table,
    norm_first,
    norm_second,
    router_projection_weights,
    expert_up,
    expert_down,
    routes,
    prefix_lengths,
    relative_buckets,
):
    section_id = lax.axis_index("section")
    local_seqs, piece_rows, model_width = block_input.shape
    params = (
        norm_first[0].astype(jnp.float32),
        bias_table[0].astype(jnp.float32),
        norm_second[0].astype(jnp.float32),
        router_projection_weights[0],
    )
    section_routes = routes[0, :, :, 0]
    rel_onehot = (
        relative_buckets[:, None] == jnp.arange(bias_table.shape[1], dtype=jnp.int32)[None, :]
    ).astype(jnp.float32)
    expert_pair = (expert_up[0], expert_down[0])

    def heads_now():
        return fetch_heads(query_key_value_weights, attention_output_weights)

    received = jnp.zeros((SEQ_MB, piece_rows, model_width), jnp.bfloat16)
    stashed = jnp.zeros((MICRO, SEQ_MB, piece_rows, model_width), jnp.bfloat16)
    outputs_all = jnp.zeros_like(stashed)
    for tick_index in range(MICRO + 1):
        offset = tick_index - section_id
        index_mb = jnp.clip(offset, 0, MICRO - 1)
        is_valid = (offset >= 0) & (offset < MICRO)
        first_row = min(tick_index, MICRO - 1) * SEQ_MB
        fresh_rows = block_input[first_row : first_row + SEQ_MB]
        section_in = jnp.where(section_id == 0, fresh_rows, received)
        stashed = jnp.where(
            is_valid,
            lax.dynamic_update_slice_in_dim(stashed, section_in[None], index_mb, 0),
            stashed,
        )
        routes_mb = lax.dynamic_slice_in_dim(section_routes, index_mb * SEQ_MB, SEQ_MB, 0)
        prefix_mb = lax.dynamic_slice_in_dim(prefix_lengths, index_mb * SEQ_MB, SEQ_MB, 0)
        result, router_probs, saved = layer_forward(
            section_in.astype(jnp.float32),
            params,
            heads_now(),
            expert_pair,
            routes_mb,
            prefix_mb,
            rel_onehot,
        )
        sent_rows = result.astype(jnp.bfloat16)
        outputs_all = jnp.where(
            is_valid,
            lax.dynamic_update_slice_in_dim(outputs_all, sent_rows[None], index_mb, 0),
            outputs_all,
        )
        if tick_index < MICRO:
            received = passed_along(sent_rows, "section", 1)
    grad_received = jnp.zeros_like(received)
    grads_in_all = jnp.zeros_like(stashed)
    head_sum = None
    expert_sum = None
    small_sum = None
    for tick_index in range(MICRO + 1):
        offset = MICRO - tick_index - section_id
        index_mb = jnp.clip(offset, 0, MICRO - 1)
        is_valid = (offset >= 0) & (offset < MICRO)
        first_row = max(MICRO - 1 - tick_index, 0) * SEQ_MB
        upstream = cotangent[first_row : first_row + SEQ_MB]
        grad_result = jnp.where(section_id == 1, upstream, grad_received).astype(jnp.float32)
        section_in = lax.dynamic_index_in_dim(stashed, index_mb, 0, keepdims=False).astype(
            jnp.float32
        )
        routes_mb = lax.dynamic_slice_in_dim(section_routes, index_mb * SEQ_MB, SEQ_MB, 0)
        prefix_mb = lax.dynamic_slice_in_dim(prefix_lengths, index_mb * SEQ_MB, SEQ_MB, 0)
        grad_input, head_grads, expert_grads, small_grads = layer_backward(
            section_in,
            grad_result,
            params,
            heads_now(),
            expert_pair,
            routes_mb,
            prefix_mb,
            rel_onehot,
        )
        head_grads = reduce_heads(head_grads[0], head_grads[1])
        head_sum = accumulate(head_sum, head_grads, is_valid)
        expert_sum = accumulate(expert_sum, expert_grads, is_valid)
        small_sum = accumulate(small_sum, small_grads, is_valid)
        grad_sent = grad_input.astype(jnp.bfloat16)
        grads_in_all = jnp.where(
            is_valid,
            lax.dynamic_update_slice_in_dim(grads_in_all, grad_sent[None], index_mb, 0),
            grads_in_all,
        )
        if tick_index < MICRO:
            grad_received = passed_along(grad_sent, "section", -1)
    gain_one_grad, table_grad, gain_two_grad, router_grad = lax.psum(
        (small_sum[0], small_sum[1], small_sum[2], small_sum[3]), ("dp", "tensor")
    )
    return (
        outputs_all.reshape(1, local_seqs, piece_rows, model_width),
        grads_in_all.reshape(1, local_seqs, piece_rows, model_width),
        head_sum[0][None],
        head_sum[1][None],
        table_grad[None],
        gain_one_grad[None],
        gain_two_grad[None],
        router_grad[None],
        expert_sum[0][None],
        expert_sum[1][None],
    )


def solution(mesh):
    in_specs = (
        P("dp", "tensor", None),
        P("dp", "tensor", None),
        P("section", None, "dp", "tensor"),
        P("section", "tensor", "dp"),
        P("section", None, None),
        P("section", None),
        P("section", None),
        P("section", None, None),
        P("section", "dp", None, "tensor"),
        P("section", "dp", "tensor", None),
        P("section", "dp", None, None),
        P("dp"),
        P(),
    )
    out_specs = (
        P("section", "dp", "tensor", None),
        P("section", "dp", "tensor", None),
        P("section", None, "dp", "tensor"),
        P("section", "tensor", "dp"),
        P("section", None, None),
        P("section", None),
        P("section", None),
        P("section", None, None),
        P("section", "dp", None, "tensor"),
        P("section", "dp", "tensor", None),
    )
    return jax.shard_map(
        per_device, mesh=mesh, in_specs=in_specs, out_specs=out_specs, check_vma=False
    )
```

profile of v0, /device:TPU:0, one launch (start us, length us, event | category | flops | bytes accessed | tf_op | source)
XLA Modules:
  0.0 4139.4 jit_solution(5723676483602623866)
XLA Ops:
  55.5 210.7 %while.222 = (s32[]{:T(128)}, bf16[2,3,512,64]{2,3,1,0:T(8,128)(2,1)S(1)}, s32[2]{0:T(128)S(1)}, s32[]{:T(128)}, bf16[3,1024,64]{1,2,0:T(8,128)(2,1)S(1)}, /*ind...) while((s32[]{:T(128)}, ...), condition=%wide.region_4.5_spmd, body=%wide.region_1.4_spmd.sunk | while | flops 416388096 | bytes 164204784 | solution.py:126
  268.8 34.2 reduce-scatter.37.cloned.1.call-done
  312.9 29.5 all-gather.23.cloned.1.call-done
  350.7 26.8 all_to_all.72
  412.7 24.2 all-to-all-done.1
  452.2 32.3 reduce-scatter.39.cloned.1.call-done
  502.2 37.3 all-gather.25.cloned.1.call-done
  543.3 194.2 %while.223 = (s32[]{:T(128)}, bf16[2,3,512,64]{2,3,1,0:T(8,128)(2,1)S(1)}, s32[2]{0:T(128)S(1)}, s32[]{:T(128)}, bf16[3,1024,64]{1,2,0:T(8,128)(2,1)S(1)}, /*ind...) while((s32[]{:T(128)}, ...), condition=%wide.region_19.22_spmd, body=%wide.region_16.21_spmd.sunk | while | flops 416388096 | bytes 164204784 | solution.py:126
  553.9 15.3 reshape.2867
  646.8 15.3 reshape.2867
  740.1 34.2 reduce-scatter.41.cloned.1.call-done
  785.8 28.0 all-gather.27.cloned.1.call-done
  822.0 26.8 all_to_all.73
  884.6 23.0 all-to-all-done.3
  923.5 32.0 reduce-scatter.43.cloned.1.call-done
  975.8 36.7 all-gather.29.cloned.1.call-done
  1016.2 202.6 %while.224 = (s32[]{:T(128)}, bf16[2,3,512,64]{2,3,1,0:T(8,128)(2,1)S(1)}, s32[2]{0:T(128)S(1)}, s32[]{:T(128)}, bf16[3,1024,64]{1,2,0:T(8,128)(2,1)S(1)}, /*ind...) while((s32[]{:T(128)}, ...), condition=%wide.region_34.37_spmd, body=%wide.region_31.36_spmd.sunk | while | flops 416388096 | bytes 164204784 | solution.py:126
  1026.7 15.3 reshape.2871
  1119.2 15.2 reshape.2871
  1226.3 172.8 %while.225 = (s32[]{:T(128)}, bf16[2,3,512,64]{2,3,1,0:T(8,128)(2,1)}, f32[2,3,512]{2,1,0:T(4,128)}, s32[2]{0:T(128)S(1)}, s32[]{:T(128)}, /*index=5*/bf16[3,102...) while((s32[]{:T(128)}, ...), condition=%wide.region_49.52_spmd, body=%wide.region_46.51_spmd.sunk | while | flops 417955840 | bytes 131211464 | solution.py:126
  1236.6 15.2 reshape.2875
  1322.8 15.2 reshape.2875
  1406.0 33.0 reduce-scatter.49.cloned.1.call-done
  1448.4 31.7 all-gather.37.cloned.1.call-done
  1488.4 27.0 all_to_all.74
  1550.5 27.9 all_to_all.75
  1594.1 31.6 reduce-scatter.53.cloned.1.call-done
  1629.6 34.2 all-gather.31.cloned.1.call-done
  1670.6 31.2 all-gather.41.cloned.1.call-done
  1705.7 34.0 all-gather.35.cloned.1.call-done
  1756.3 168.7 %while.226 = (s32[]{:T(128)}, bf16[2,3,512,64]{2,3,1,0:T(8,128)(2,1)}, f32[2,3,512]{2,1,0:T(4,128)S(1)}, s32[2]{0:T(128)S(1)}, s32[]{:T(128)}, /*index=5*/bf16[3...) while((s32[]{:T(128)}, ...), condition=%wide.region_70.73_spmd, body=%wide.region_67.72_spmd.sunk | while | flops 417955840 | bytes 135938336 | solution.py:126
  1985.0 170.1 %while.227 = (s32[]{:T(128)}, bf16[2,3,512,64]{2,3,1,0:T(8,128)(2,1)}, f32[2,3,512]{2,1,0:T(4,128)S(1)}, s32[2]{0:T(128)S(1)}, s32[]{:T(128)}, /*index=5*/bf16[3...) while((s32[]{:T(128)}, ...), condition=%wide.region_91.94_spmd, body=%wide.region_88.93_spmd.sunk | while | flops 417955840 | bytes 134365440 | solution.py:126
  2238.2 32.9 reduce-scatter.51.cloned.1.call-done
  2278.1 35.5 all-gather.45.cloned.1.call-done
  2327.7 24.0 all-gather.39.cloned.1.call-done
  2354.6 301.4 %while.228 = (s32[]{:T(128)}, f32[3,1024,64]{1,2,0:T(8,128)}, f32[3,1024,64]{1,2,0:T(8,128)}, f32[3,2049]{1,0:T(4,128)S(1)}, bf16[2,3,512,64]{2,3,1,0:T(8,128)(2...) while((s32[]{:T(128)}, f32[3,1024,64]{1,2,0:T(8,128)}, ...), condition=%wide.region_63.66_spmd.clone, body=%wide.region_60.65_spmd.clone.sunk | while | flops 1029311488 | bytes 277025472 | solution.py:175
  2372.0 15.2 reshape.2888
  2479.8 16.5 reshape.2893
  2518.7 15.2 reshape.2888
  2626.7 16.7 reshape.2893
  2698.3 28.3 all_to_all.76
  2758.4 15.5 reduce-scatter.61.cloned.1.call-done
  2776.1 36.2 all-gather.43.cloned.1.call-done
  2820.7 26.8 all_to_all.77
  2882.6 28.0 all_to_all.78
  2925.3 32.6 reduce-scatter.59.cloned.1.call-done
  2962.6 33.0 all-gather.53.cloned.1.call-done
  3009.9 23.9 all-gather.47.cloned.1.call-done
  3036.6 298.0 %while.229 = (s32[]{:T(128)}, f32[3,1024,64]{1,2,0:T(8,128)}, f32[3,1024,64]{1,2,0:T(8,128)}, f32[3,2049]{1,0:T(4,128)S(1)}, bf16[2,3,512,64]{2,3,1,0:T(8,128)(2...) while((s32[]{:T(128)}, f32[3,1024,64]{1,2,0:T(8,128)}, ...), condition=%wide.region_84.87_spmd.clone, body=%wide.region_81.86_spmd.clone.sunk | while | flops 1029311488 | bytes 278598368 | solution.py:175
  3160.1 16.5 reshape.2900
  3305.2 16.7 reshape.2900
  3376.9 28.3 all_to_all.79
  3425.5 26.9 reduce-scatter.69.cloned.1.call-done
  3454.7 36.2 all-gather.51.cloned.1.call-done
  3499.3 26.8 all_to_all.80
  3561.1 28.0 all_to_all.81
  3603.1 33.3 reduce-scatter.67.cloned.1.call-done
  3680.8 299.5 %while.230 = (s32[]{:T(128)}, f32[3,1024,64]{1,2,0:T(8,128)}, f32[3,1024,64]{1,2,0:T(8,128)}, f32[3,2049]{1,0:T(4,128)}, bf16[2,3,512,64]{2,3,1,0:T(8,128)(2,1)}...) while((s32[]{:T(128)}, f32[3,1024,64]{1,2,0:T(8,128)}, ...), condition=%wide.region_105.108_spmd.clone, body=%wide.region_102.107_spmd.clone.sunk | while | flops 1029311488 | bytes 278598368 | solution.py:175
  3696.7 15.4 reshape.2902
  3804.7 16.7 reshape.2907
  3844.0 15.4 reshape.2902
  3951.9 16.5 reshape.2907
  4047.7 20.4 reduce-scatter.71.cloned.1.call-done
  4070.2 59.5 %all-reduce.15 = (f32[1,32,12]{1,2,0:T(8,128)S(1)}, f32[1,768]{1,0:T(1,128)}, f32[1,768]{1,0:T(1,128)}, f32[1,768,4]{1,2,0:T(4,128)}) all-reduce(f32[1,32,12]{1,2,0:T(8,128)S(1)} %copy-done.172, f32[1,768]{1,0:T(1,128)S(1)} %broadcast_in_dim.582, ...), channel_id=1, replica_groups=mesh['section'=2,'dp'=4,'tensor'=4] {'dp','tensor'}, use_global_device_ids=true, to_apply=%region_114.117 | all-reduce | flops 4992 | bytes 39936 | tf_op jit(solution)/shard_map/psum | solution.py:534
  (1371 shorter events, 2539.7 us)
Async XLA Ops:
  7.2 370.4 %copy-start = (bf16[1,1,768,768]{3,2,1,0:T(8,128)(2,1)S(1)}, bf16[1,1,768,768]{3,2,1,0:T(8,128)(2,1)}, u32[]{:S(2)}) copy-start(bf16[1,1,768,768]{3,2,1,0:T(8,128)(2,1)} %param.44) | copy-start | bytes 3538948
  7.2 44.5 %all-gather.21.cloned.1.call-start = ((), (), s32[]{:S(2)}) async-start(), calls=%async_computation.42 | async-start | bytes 1966080 | tf_op jit(solution)/shard_map/all_gather | solution.py:38
  11.7 291.3 %reduce-scatter.37.cloned.1.call-start = ((), (), s32[]{:S(2)}) async-start(), calls=%async_computation.43 | async-start | bytes 1966080 | tf_op jit(solution)/shard_map/reduce_scatter | solution.py:42
  55.5 211.4 %copy-start.26 = (bf16[1,192,768]{2,1,0:T(8,128)(2,1)S(1)}, bf16[1,192,768]{2,1,0:T(8,128)(2,1)}, u32[]{:S(2)}) copy-start(bf16[1,192,768]{2,1,0:T(8,128)(2,1)} %copy.93) | copy-start | bytes 884740
  268.7 73.7 %all-gather.23.cloned.1.call-start = ((), (), s32[]{:S(2)}) async-start(), calls=%async_computation.44 | async-start | bytes 1966080 | tf_op jit(solution)/shard_map/all_gather | solution.py:38
  268.8 80.0 %copy-start.143 = (f32[768]{0:T(1024)}, f32[768]{0:T(1024)S(1)}, u32[]{:S(2)}) copy-start(f32[768]{0:T(1024)S(1)} %convert_reduce_fusion) | copy-start | bytes 9220
  409.0 27.9 all-to-all-start.1
  412.6 71.9 %reduce-scatter.39.cloned.1.call-start = ((), (), s32[]{:S(2)}) async-start(), calls=%async_computation.45 | async-start | bytes 1966080 | tf_op jit(solution)/shard_map/reduce_scatter | solution.py:42
  451.2 88.3 %all-gather.25.cloned.1.call-start = ((), (), s32[]{:S(2)}) async-start(), calls=%async_computation.46 | async-start | bytes 1966080 | tf_op jit(solution)/shard_map/all_gather | solution.py:38
  486.6 11.9 collective-permute-start
  502.1 272.2 %reduce-scatter.41.cloned.1.call-start = ((), (), s32[]{:S(2)}) async-start(), calls=%async_computation.47 | async-start | bytes 1966080 | tf_op jit(solution)/shard_map/reduce_scatter | solution.py:42
  543.3 195.0 %copy-start.27 = (bf16[1,192,768]{2,1,0:T(8,128)(2,1)S(1)}, bf16[1,192,768]{2,1,0:T(8,128)(2,1)}, u32[]{:S(2)}) copy-start(bf16[1,192,768]{2,1,0:T(8,128)(2,1)} %copy.93) | copy-start | bytes 884740
  740.0 73.7 %all-gather.27.cloned.1.call-start = ((), (), s32[]{:S(2)}) async-start(), calls=%async_computation.48 | async-start | bytes 1966080 | tf_op jit(solution)/shard_map/all_gather | solution.py:38
  879.8 27.9 all-to-all-start.3
  883.4 72.1 %reduce-scatter.43.cloned.1.call-start = ((), (), s32[]{:S(2)}) async-start(), calls=%async_computation.49 | async-start | bytes 1966080 | tf_op jit(solution)/shard_map/reduce_scatter | solution.py:42
  922.1 90.5 %all-gather.29.cloned.1.call-start = ((), (), s32[]{:S(2)}) async-start(), calls=%async_computation.50 | async-start | bytes 1966080 | tf_op jit(solution)/shard_map/all_gather | solution.py:38
  957.7 11.9 collective-permute-start.1
  975.2 246.1 %all-gather.33.cloned.1.call-start = ((), (), s32[]{:S(2)}) async-start(), calls=%async_computation.54 | async-start | bytes 1966080 | tf_op jit(solution)/shard_map/all_gather | solution.py:38
  975.8 428.9 %reduce-scatter.45.cloned.1.call-start = ((), (), s32[]{:S(2)}) async-start(), calls=%async_computation.51 | async-start | bytes 1966080 | tf_op jit(solution)/shard_map/reduce_scatter | solution.py:42
  1016.2 203.3 %copy-start.28 = (bf16[1,192,768]{2,1,0:T(8,128)(2,1)S(1)}, bf16[1,192,768]{2,1,0:T(8,128)(2,1)}, u32[]{:S(2)}) copy-start(bf16[1,192,768]{2,1,0:T(8,128)(2,1)} %copy.93) | copy-start | bytes 884740
  1221.3 217.7 %reduce-scatter.49.cloned.1.call-start = ((), (), s32[]{:S(2)}) async-start(), calls=%async_computation.55 | async-start | bytes 1966080 | tf_op jit(solution)/shard_map/reduce_scatter | solution.py:42
  1226.3 176.6 %copy-start.29 = (bf16[1,192,768]{2,1,0:T(8,128)(2,1)S(1)}, bf16[1,192,768]{2,1,0:T(8,128)(2,1)}, u32[]{:S(2)}) copy-start(bf16[1,192,768]{2,1,0:T(8,128)(2,1)} %copy.93) | copy-start | bytes 884740
  1404.7 75.4 %all-gather.37.cloned.1.call-start = ((), (), s32[]{:S(2)}) async-start(), calls=%async_computation.57 | async-start | bytes 1966080 | tf_op jit(solution)/shard_map/all_gather | solution.py:38
  1443.8 181.8 %reduce-scatter.53.cloned.1.call-start = ((), (), s32[]{:S(2)}) async-start(), calls=%async_computation.59 | async-start | bytes 1966080 | tf_op jit(solution)/shard_map/reduce_scatter | solution.py:42
  1592.3 71.5 %all-gather.31.cloned.1.call-start = ((), (), s32[]{:S(2)}) async-start(), calls=%async_computation.52 | async-start | bytes 1966080 | tf_op jit(solution)/shard_map/all_gather | solution.py:38
  1592.9 108.9 %all-gather.41.cloned.1.call-start = ((), (), s32[]{:S(2)}) async-start(), calls=%async_computation.62 | async-start | bytes 1966080 | tf_op jit(solution)/shard_map/all_gather | solution.py:38
  1593.5 146.3 %all-gather.35.cloned.1.call-start = ((), (), s32[]{:S(2)}) async-start(), calls=%async_computation.56 | async-start | bytes 1966080 | tf_op jit(solution)/shard_map/all_gather | solution.py:38
  1629.0 299.7 %all-gather.49.cloned.1.call-start = ((), (), s32[]{:S(2)}) async-start(), calls=%async_computation.70 | async-start | bytes 1966080 | tf_op jit(solution)/shard_map/all_gather | solution.py:38
  1750.8 181.9 %all-to-all-start.6 = ((bf16[4,320,768]{2,1,0:T(8,128)(2,1)}), bf16[4,320,768]{2,1,0:T(8,128)(2,1)}, u32[]{:S(2)}, u32[]{:S(2)}) async-start(bf16[4,320,768]{2,1,0:T(8,128)(2,1)} %bitcast.1114), calls=%async_computation.13 | async-start | bytes 3932160 | tf_op jit(solution)/shard_map/all_to_all | solution.py:55
  1755.4 482.7 %reduce-scatter.57.cloned.1.call-start = ((), (), s32[]{:S(2)}) async-start(), calls=%async_computation.63 | async-start | bytes 1966080 | tf_op jit(solution)/shard_map/reduce_scatter | solution.py:42
  1756.3 170.6 %copy-start.30 = (bf16[1,192,768]{2,1,0:T(8,128)(2,1)S(1)}, bf16[1,192,768]{2,1,0:T(8,128)(2,1)}, u32[]{:S(2)}) copy-start(bf16[1,192,768]{2,1,0:T(8,128)(2,1)} %copy.93) | copy-start | bytes 884740
  1932.7 47.0 %all-to-all-start.4 = ((bf16[4,320,768]{2,1,0:T(8,128)(2,1)}), bf16[4,320,768]{2,1,0:T(8,128)(2,1)}, u32[]{:S(2)}, u32[]{:S(2)}) async-start(bf16[4,320,768]{2,1,0:T(8,128)(2,1)} %bitcast.130), calls=%async_computation.9 | async-start | bytes 3932160 | tf_op jit(solution)/shard_map/all_to_all | solution.py:55
  1979.7 212.5 %all-to-all-start.8 = ((bf16[4,2,122880]{2,1,0:T(2,128)(2,1)}), bf16[4,2,122880]{2,1,0:T(2,128)(2,1)}, u32[]{:S(2)}, u32[]{:S(2)}) async-start(bf16[4,2,122880]{2,1,0:T(2,128)(2,1)} %reshape.2808), calls=%async_computation.15 | async-start | bytes 3932160 | tf_op jit(solution)/shard_map/all_to_all | solution.py:59
  1984.1 254.0 %reduce-scatter.65.cloned.1.call-start = ((), (), s32[]{:S(2)}) async-start(), calls=%async_computation.71 | async-start | bytes 1966080 | tf_op jit(solution)/shard_map/reduce_scatter | solution.py:42
  1985.0 173.8 %copy-start.31 = (bf16[1,192,768]{2,1,0:T(8,128)(2,1)S(1)}, bf16[1,192,768]{2,1,0:T(8,128)(2,1)}, u32[]{:S(2)}) copy-start(bf16[1,192,768]{2,1,0:T(8,128)(2,1)} %copy.93) | copy-start | bytes 884740
  2192.2 28.8 all-to-all-start.5
  2196.6 74.5 %reduce-scatter.51.cloned.1.call-start = ((), (), s32[]{:S(2)}) async-start(), calls=%async_computation.58 | async-start | bytes 1966080 | tf_op jit(solution)/shard_map/reduce_scatter | solution.py:42
  2237.8 75.7 %all-gather.45.cloned.1.call-start = ((), (), s32[]{:S(2)}) async-start(), calls=%async_computation.65 | async-start | bytes 1966080 | tf_op jit(solution)/shard_map/all_gather | solution.py:38
  2277.3 74.4 %all-gather.39.cloned.1.call-start = ((), (), s32[]{:S(2)}) async-start(), calls=%async_computation.60 | async-start | bytes 1966080 | tf_op jit(solution)/shard_map/all_gather | solution.py:38
  2323.2 339.8 %all-to-all-start.11 = ((bf16[4,320,768]{2,1,0:T(8,128)(2,1)}), bf16[4,320,768]{2,1,0:T(8,128)(2,1)}, u32[]{:S(2)}, u32[]{:S(2)}) async-start(bf16[4,320,768]{2,1,0:T(8,128)(2,1)} %bitcast.1105), calls=%async_computation.22 | async-start | bytes 3932160 | tf_op jit(solution)/shard_map/all_to_all | solution.py:55
  2327.6 412.9 %reduce-scatter.55.cloned.1.call-start = ((), (), s32[]{:S(2)}) async-start(), calls=%async_computation.61 | async-start | bytes 1966080 | tf_op jit(solution)/shard_map/reduce_scatter | solution.py:42
  2662.9 111.0 %reduce-scatter.61.cloned.1.call-start = ((), (), s32[]{:S(2)}) async-start(), calls=%async_computation.67 | async-start | bytes 1966080 | tf_op jit(solution)/shard_map/reduce_scatter | solution.py:42
  2740.5 71.8 %all-gather.43.cloned.1.call-start = ((), (), s32[]{:S(2)}) async-start(), calls=%async_computation.64 | async-start | bytes 1966080 | tf_op jit(solution)/shard_map/all_gather | solution.py:38
  2746.0 12.4 collective-permute-start.2
  2776.1 181.8 %reduce-scatter.59.cloned.1.call-start = ((), (), s32[]{:S(2)}) async-start(), calls=%async_computation.66 | async-start | bytes 1966080 | tf_op jit(solution)/shard_map/reduce_scatter | solution.py:42
  2924.5 71.1 %all-gather.53.cloned.1.call-start = ((), (), s32[]{:S(2)}) async-start(), calls=%async_computation.73 | async-start | bytes 1966080 | tf_op jit(solution)/shard_map/all_gather | solution.py:38
  2925.3 108.5 %all-gather.47.cloned.1.call-start = ((), (), s32[]{:S(2)}) async-start(), calls=%async_computation.68 | async-start | bytes 1966080 | tf_op jit(solution)/shard_map/all_gather | solution.py:38
  2925.3 71.8 %copy-start.203 = (bf16[256,4]{0,1:T(4,128)(2,1)}, bf16[256,4]{0,1:T(4,128)(2,1)S(1)}, u32[]{:S(2)}) copy-start(bf16[256,4]{0,1:T(4,128)(2,1)S(1)} %fusion.452) | copy-start | bytes 6148
  3005.2 336.3 %all-to-all-start.15 = ((bf16[4,320,768]{2,1,0:T(8,128)(2,1)}), bf16[4,320,768]{2,1,0:T(8,128)(2,1)}, u32[]{:S(2)}, u32[]{:S(2)}) async-start(bf16[4,320,768]{2,1,0:T(8,128)(2,1)} %bitcast.1106), calls=%async_computation.30 | async-start | bytes 3932160 | tf_op jit(solution)/shard_map/all_to_all | solution.py:55
  3009.8 409.3 %reduce-scatter.63.cloned.1.call-start = ((), (), s32[]{:S(2)}) async-start(), calls=%async_computation.69 | async-start | bytes 1966080 | tf_op jit(solution)/shard_map/reduce_scatter | solution.py:42
  3341.5 110.9 %reduce-scatter.69.cloned.1.call-start = ((), (), s32[]{:S(2)}) async-start(), calls=%async_computation.75 | async-start | bytes 1966080 | tf_op jit(solution)/shard_map/reduce_scatter | solution.py:42
  3419.0 71.8 %all-gather.51.cloned.1.call-start = ((), (), s32[]{:S(2)}) async-start(), calls=%async_computation.72 | async-start | bytes 1966080 | tf_op jit(solution)/shard_map/all_gather | solution.py:38
  3423.7 28.7 collective-permute-start.3
  3454.6 181.8 %reduce-scatter.67.cloned.1.call-start = ((), (), s32[]{:S(2)}) async-start(), calls=%async_computation.74 | async-start | bytes 1966080 | tf_op jit(solution)/shard_map/reduce_scatter | solution.py:42
  3603.0 74.3 %all-gather.55.cloned.1.call-start = ((), (), s32[]{:S(2)}) async-start(), calls=%async_computation.76 | async-start | bytes 1966080 | tf_op jit(solution)/shard_map/all_gather | solution.py:38
  3641.0 360.4 %reduce-scatter.47.cloned.1.call-start = ((), (), s32[]{:S(2)}) async-start(), calls=%async_computation.53 | async-start | bytes 1966080 | tf_op jit(solution)/shard_map/reduce_scatter | solution.py:42
  3641.8 363.7 %reduce-scatter.79.cloned.1.call-start = ((), (), s32[]{:S(2)}) async-start(), calls=%async_computation.81 | async-start | bytes 491520
  3644.7 361.8 %reduce-scatter.73.cloned.1.call-start = ((), (), s32[]{:S(2)}) async-start(), calls=%async_computation.78 | async-start | bytes 1228800
  3655.9 368.7 %reduce-scatter.81.cloned.1.call-start = ((), (), s32[]{:S(2)}) async-start(), calls=%async_computation.82 | async-start | bytes 491520
  3660.5 365.1 %reduce-scatter.75.cloned.1.call-start = ((), (), s32[]{:S(2)}) async-start(), calls=%async_computation.79 | async-start | bytes 1228800
  3674.4 368.9 %reduce-scatter.83.cloned.1.call-start = ((), (), s32[]{:S(2)}) async-start(), calls=%async_computation.83 | async-start | bytes 491520
  3983.5 61.5 %reduce-scatter.77.cloned.1.call-start = ((), (), s32[]{:S(2)}) async-start(), calls=%async_computation.80 | async-start | bytes 1228800
  3996.6 71.4 %reduce-scatter.71.cloned.1.call-start = ((), (), s32[]{:S(2)}) async-start(), calls=%async_computation.77 | async-start | bytes 1966080 | tf_op jit(solution)/shard_map/reduce_scatter | solution.py:42
  4039.9 90.4 %copy-start.86 = (f32[1,256,768]{2,1,0:T(8,128)S(1)}, f32[1,256,768]{2,1,0:T(8,128)}, u32[]{:S(2)}) copy-start(f32[1,256,768]{2,1,0:T(8,128)} %get-tuple-element.1794) | copy-start | bytes 2359300
  (273 other events, 3830.8 us)
Sparse Core Ops, SparseCore 0:
  11.8 39.7 all-gather.20
  268.9 34.1 reduce-scatter.36
  306.4 36.0 all-gather.22
  451.3 33.2 reduce-scatter.38
  502.2 37.1 all-gather.24
  740.2 34.1 reduce-scatter.40
  777.6 36.1 all-gather.26
  922.2 33.2 reduce-scatter.42
  975.3 37.1 all-gather.28
  1014.5 35.9 all-gather.32
  1221.4 34.1 reduce-scatter.44
  1404.8 34.1 reduce-scatter.48
  1444.0 36.0 all-gather.36
  1592.4 33.2 reduce-scatter.52
  1627.7 36.0 all-gather.30
  1665.8 35.9 all-gather.40
  1703.8 35.9 all-gather.34
  1741.8 35.9 all-gather.48
  1928.8 34.4 reduce-scatter.56
  2160.7 34.4 reduce-scatter.64
  2237.9 33.1 reduce-scatter.50
  2277.4 36.0 all-gather.44
  2315.7 35.9 all-gather.38
  2663.0 34.1 reduce-scatter.54
  2740.6 33.2 reduce-scatter.60
  2776.2 36.0 all-gather.42
  2924.6 33.2 reduce-scatter.58
  2959.5 36.0 all-gather.52
  2997.7 35.9 all-gather.46
  3341.6 34.1 reduce-scatter.62
  3419.1 33.2 reduce-scatter.68
  3454.7 36.0 all-gather.50
  3603.1 33.2 reduce-scatter.66
  3641.2 36.0 all-gather.54
  3679.6 34.1 reduce-scatter.46
  3716.1 19.7 reduce-scatter.78
  3738.4 24.4 reduce-scatter.72
  3765.5 20.8 reduce-scatter.80
  3789.0 24.4 reduce-scatter.74
  3983.6 19.5 reduce-scatter.82
  4005.8 24.4 reduce-scatter.76
  4032.7 35.2 reduce-scatter.70
where the time goes:
time: 4160 us; the launch traced here: 4140 us
  local copies, waits for them, and re-layouts  1940 us (47%)
  waiting for transfers between devices  912 us (22%)
  matrix products  371 us (9%)
  blocking collectives  357 us (9%)
  other arithmetic  354 us (9%)
  loops' own time  138 us (3%)
  starting transfers between devices  45.6 us (1%)
    while x226, local copies, waits for them, and re-layouts  664 us
    all_gather x18, waiting for transfers between devices, gather_rows(): return lax.all_gather(values, 'tensor', axis=1, tiled=True)  463 us
    reduce_scatter x18, waiting for transfers between devices, sum_rows(): lax.psum_scatter(values.astype(jnp.bfloat16), 'tensor', scatter_dimension...  359 us
    slice x18, local copies, waits for them, and re-layouts, bias_block(): tiled[:, block_rows - 1:block_rows - 1 + block_rows * (width - 1)]  242 us
    reshape x18, local copies, waits for them, and re-layouts, bias_block(): jnp.broadcast_to(window[:, None, :], (heads_local, block_rows, width))  237 us
    reshape x18, local copies, waits for them, and re-layouts, bias_block(): tiled[:, block_rows - 1:block_rows - 1 + block_rows * (width - 1)]  200 us
    all_to_all x5, blocking collectives, from_experts(): lax.all_to_all(produced.astype(jnp.bfloat16), 'dp', split_axis=1, concat_...  140 us
    all_to_all x5, blocking collectives, to_experts(): lax.all_to_all(buffers, 'dp', split_axis=0, concat_axis=1, tiled=True)  134 us
  transfers between devices with their start and end apart: 54, of which 34 were waited for; matrix products, arithmetic and copies ran while one was open for 47% of the time, Pallas kernels for 0%

commit v1 on v0

v1 whole, which is shorter than its diff:
```python
import functools

import jax
import jax.numpy as jnp
from jax import lax
from jax.experimental import pallas as pl
from jax.experimental.pallas import tpu as pltpu
from jax.sharding import PartitionSpec as P

HEAD_DIM = 64
EPSILON = 1e-06
MASKED = -1000000000.0
AXES = ("section", "dp", "tensor")
BLOCK = 128
DIRECT = 8
BF16 = jnp.bfloat16
F32 = jnp.float32


def send(value, to):
    sections, width, depth = (lax.axis_size(name) for name in AXES)

    def number(x, h, c, t):
        return (x * width + 2 * h + c) * depth + t

    pairs = []
    for x in range(sections):
        for d in range(width):
            for t in range(depth):
                target = to(x, d // 2, d % 2, t)
                if target is not None:
                    pairs.append((number(x, d // 2, d % 2, t), number(*target)))
    return lax.ppermute(value, AXES, pairs)


def core_swap(value):
    return send(value, lambda x, h, c, t: (x, h, 1 - c, t))


def section_swap(value):
    return send(value, lambda x, h, c, t: (1 - x, h, c, t))


def tensor_swap(value, j):
    return send(value, lambda x, h, c, t: (x, h, c, t ^ j))


def host_swap(value, j):
    return send(value, lambda x, h, c, t: (x, h ^ j, c, t))


def expert_swap(value, j):
    def to(x, h, c, t):
        e = (2 * h + (t & 1)) ^ j
        return (x, e >> 1, c, (t & 2) | (e & 1))

    return send(value, to)


def expert_exchange(values):
    count, bit = values.shape[0], 1
    while bit < count:
        parts = values.reshape(count // (2 * bit), 2, bit, *values.shape[1:])
        other = expert_swap(parts[:, 1], bit)
        values = jnp.stack([parts[:, 0], other], 1).reshape(values.shape)
        bit *= 2
    return values


def place():
    d = lax.axis_index("dp")
    return lax.axis_index("section"), d // 2, d % 2, lax.axis_index("tensor")


def ordered(flag, own, other, axis):
    first = jnp.where(flag == 0, own, other)
    second = jnp.where(flag == 0, other, own)
    return jnp.concatenate([first, second], axis)


def at(values, index):
    return lax.dynamic_index_in_dim(values, index, 0, keepdims=False)


def rows_over_hosts(value, axis):
    _, h, _, _ = place()
    bit = 1
    while bit < lax.axis_size("dp") // 2:
        other = host_swap(value, bit)
        value = ordered((h // bit) % 2, value, other, axis)
        bit *= 2
    return value


def to_groups(rows):
    _, _, c, t = place()
    count, piece, width = rows.shape
    parts = rows.reshape(count, 2, piece // 2, width)
    keep = jnp.where(c == 0, parts[:, 0], parts[:, 1])
    give = jnp.where(c == 0, parts[:, 1], parts[:, 0])
    four = ordered(c, keep, core_swap(give), 0)
    got = jnp.stack([at(four, t)] + [tensor_swap(at(four, t ^ j), j) for j in (1, 2, 3)])
    halves = jnp.stack([at(got, t ^ p) for p in range(4)])
    whole = ordered(c, halves[:, None], core_swap(halves)[:, None], 1)
    return whole.reshape(4 * piece, width)


def from_groups(rows):
    _, _, c, t = place()
    length, width = rows.shape
    half = length // 8
    parts = rows.reshape(4, 2, half, width)
    mine = jnp.where(c == 0, parts[:, 0], parts[:, 1])
    got = jnp.stack([at(mine, t)] + [tensor_swap(at(mine, t ^ j), j) for j in (1, 2, 3)])
    four = jnp.stack([at(got, t ^ p) for p in range(4)])
    keep = jnp.where(c == 0, four[:2], four[2:])
    give = jnp.where(c == 0, four[2:], four[:2])
    whole = ordered(c, keep[:, None], core_swap(give)[:, None], 1)
    return whole.reshape(2, 2 * half, width)


def head_lanes(width, head):
    lane = lax.broadcasted_iota(jnp.int32, (1, width), 1)
    return (lane // HEAD_DIM) == head


def attend_kernel(heads, prefix_ref, q_ref, k_ref, v_ref, base_ref, o_ref, a_ref, strip):
    block = pl.program_id(0)
    rows, width = q_ref.shape
    length = k_ref.shape[0]
    span = base_ref.shape[1]

    @pl.when(block == 0)
    def _():
        sub = lax.broadcasted_iota(jnp.int32, (8, span), 0)
        for head in range(heads):
            part = jnp.broadcast_to(base_ref[head : head + 1, :], (8, span))
            for bit in (1, 2, 4):
                part = jnp.where((sub & bit) != 0, pltpu.roll(part, bit, 1), part)
            size = 8
            while size < rows:
                part = jnp.concatenate([part, pltpu.roll(part, size, 1)], 0)
                size *= 2
            strip[head] = part

    start = pl.multiple_of((length // rows - 1 - block) * rows, rows)
    row = block * rows + lax.broadcasted_iota(jnp.int32, (rows, length), 0)
    col = lax.broadcasted_iota(jnp.int32, (rows, length), 1)
    allowed = (col <= row) | (col < prefix_ref[0])
    queries, keys, values = q_ref[...], k_ref[...], v_ref[...]
    out = jnp.zeros((rows, width), F32)
    for head in range(heads):
        lanes = head_lanes(width, head)
        own = jnp.where(lanes, queries, jnp.zeros_like(queries))
        scores = lax.dot_general(own, keys, (((1,), (1,)), ((), ())), preferred_element_type=F32)
        scores = scores * HEAD_DIM ** (-0.5) + strip[head, :, pl.ds(start, length)]
        scores = jnp.where(allowed, scores, MASKED)
        weights = jnp.exp(scores - jnp.max(scores, -1, keepdims=True))
        weights = weights / jnp.sum(weights, -1, keepdims=True)
        low = weights.astype(BF16)
        a_ref[head] = low
        out = jnp.where(lanes, jnp.dot(low, values, preferred_element_type=F32), out)
    o_ref[...] = out.astype(BF16)


def attend(qkv, base, prefix):
    _, length, width = qkv.shape
    heads = width // HEAD_DIM
    span = base.shape[1]
    return pl.pallas_call(
        functools.partial(attend_kernel, heads),
        grid=(length // BLOCK,),
        in_specs=[
            pl.BlockSpec(memory_space=pltpu.SMEM),
            pl.BlockSpec((None, BLOCK, width), lambda i: (0, i, 0)),
            pl.BlockSpec((None, length, width), lambda i: (1, 0, 0)),
            pl.BlockSpec((None, length, width), lambda i: (2, 0, 0)),
            pl.BlockSpec((heads, span), lambda i: (0, 0)),
        ],
        out_specs=[
            pl.BlockSpec((BLOCK, width), lambda i: (i, 0)),
            pl.BlockSpec((heads, BLOCK, length), lambda i: (0, i, 0)),
        ],
        out_shape=[
            jax.ShapeDtypeStruct((length, width), BF16),
            jax.ShapeDtypeStruct((heads, length, length), BF16),
        ],
        scratch_shapes=[pltpu.VMEM((heads, BLOCK, span), F32)],
        compiler_params=pltpu.CompilerParams(vmem_limit_bytes=40 * 2**20),
    )(prefix, qkv, qkv, qkv, base)


def attend_back_kernel(
    heads, q_ref, k_ref, v_ref, a_ref, do_ref, dq_ref, dk_ref, dv_ref, diag_ref, dk, dv, strip
):
    block = pl.program_id(0)
    rows, width = q_ref.shape
    length = k_ref.shape[0]
    span = strip.shape[2]
    scaling = HEAD_DIM ** (-0.5)

    @pl.when(block == 0)
    def _():
        dk[...] = jnp.zeros_like(dk)
        dv[...] = jnp.zeros_like(dv)
        strip[...] = jnp.zeros_like(strip)

    start = pl.multiple_of((length // rows - 1 - block) * rows, rows)
    queries, keys, values, grads = q_ref[...], k_ref[...], v_ref[...], do_ref[...]
    dq = jnp.zeros((rows, width), F32)
    for head in range(heads):
        lanes = head_lanes(width, head)
        low = a_ref[head]
        own_grad = jnp.where(lanes, grads, jnp.zeros_like(grads))
        own_query = jnp.where(lanes, queries, jnp.zeros_like(queries))
        weights = low.astype(F32)
        da = lax.dot_general(own_grad, values, (((1,), (1,)), ((), ())), preferred_element_type=F32)
        ds = weights * (da - jnp.sum(weights * da, -1, keepdims=True))
        ds = ds.astype(BF16)
        dq = jnp.where(lanes, jnp.dot(ds, keys, preferred_element_type=F32), dq)
        dk[...] += lax.dot_general(
            ds, own_query, (((0,), (0,)), ((), ())), preferred_element_type=F32
        )
        dv[...] += lax.dot_general(
            low, own_grad, (((0,), (0,)), ((), ())), preferred_element_type=F32
        )
        strip[head, :, pl.ds(start, length)] += ds.astype(F32)
    dq_ref[...] = (dq * scaling).astype(BF16)

    @pl.when(block == length // rows - 1)
    def _():
        dk_ref[...] = (dk[...] * scaling).astype(BF16)
        dv_ref[...] = dv[...].astype(BF16)
        sub = lax.broadcasted_iota(jnp.int32, (8, span), 0)
        for head in range(heads):
            part = strip[head]
            size = rows // 2
            while size >= 8:
                part = part[:size] + pltpu.roll(part[size:], span - size, 1)
                size //= 2
            for bit in (4, 2, 1):
                part = jnp.where((sub & bit) != 0, pltpu.roll(part, span - bit, 1), part)
            diag_ref[head : head + 1, :] = jnp.sum(part, 0, keepdims=True)


def attend_back(qkv, weights, grads):
    _, length, width = qkv.shape
    heads = width // HEAD_DIM
    span = 2 * length
    whole = jax.ShapeDtypeStruct((length, width), BF16)
    return pl.pallas_call(
        functools.partial(attend_back_kernel, heads),
        grid=(length // BLOCK,),
        in_specs=[
            pl.BlockSpec((None, BLOCK, width), lambda i: (0, i, 0)),
            pl.BlockSpec((None, length, width), lambda i: (1, 0, 0)),
            pl.BlockSpec((None, length, width), lambda i: (2, 0, 0)),
            pl.BlockSpec((heads, BLOCK, length), lambda i: (0, i, 0)),
            pl.BlockSpec((BLOCK, width), lambda i: (i, 0)),
        ],
        out_specs=[
            pl.BlockSpec((BLOCK, width), lambda i: (i, 0)),
            pl.BlockSpec((length, width), lambda i: (0, 0)),
            pl.BlockSpec((length, width), lambda i: (0, 0)),
            pl.BlockSpec((heads, span), lambda i: (0, 0)),
        ],
        out_shape=[whole, whole, whole, jax.ShapeDtypeStruct((heads, span), F32)],
        scratch_shapes=[
            pltpu.VMEM((length, width), F32),
            pltpu.VMEM((length, width), F32),
            pltpu.VMEM((heads, BLOCK, span), F32),
        ],
        compiler_params=pltpu.CompilerParams(vmem_limit_bytes=40 * 2**20),
    )(qkv, qkv, qkv, weights, grads)


def norm(values, gain):
    scale = lax.rsqrt(jnp.mean(values * values, -1, keepdims=True) + EPSILON)
    return scale, (values * scale * gain).astype(BF16)


def norm_back(values, scale, gain, grad):
    scaled = grad * gain
    mean = jnp.mean(scaled * values, -1, keepdims=True)
    return (
        scale * scaled - values * (scale * scale * scale) * mean,
        jnp.sum(grad * values * scale, axis=0),
    )


def attention_weights(pieces):
    x, h, c, t = place()
    quarter = x + 2 * c
    both = ordered(c, pieces[:3], core_swap(pieces[:3]), 1)
    arrived = None
    for j in (1, 2, 3):

        def to(x, h, c, t, j=j):
            return (x, h, c, t ^ j) if t == x + 2 * c else None

        part = send(both, to)
        arrived = part if arrived is None else arrived + part
    qkv = rows_over_hosts(jnp.where(t == quarter, both, arrived)[:, None], 1)
    qkv = qkv.reshape(3, -1, pieces.shape[2])
    out = pieces[3]
    got = jnp.stack([out] + [tensor_swap(out, j) for j in (1, 2, 3)])
    four = jnp.stack([at(got, t ^ p) for p in range(4)])
    four = rows_over_hosts(four[:, None], 1)
    four = ordered(c, four[:, :, None], core_swap(four)[:, :, None], 2)
    out = jnp.transpose(four, (1, 2, 3, 0, 4)).reshape(qkv.shape[1], -1)
    return qkv, out


def weights_out(i):
    def to(x, h, c, t):
        return (x, h, t >> 1, c + 2 * (i ^ (t & 1)))

    return to


def weights_home(i):
    def to(x, h, c, t):
        return (x, h, t & 1, 2 * c + (i ^ (t >> 1)))

    return to


def expert_weights(up, down):
    up = jnp.concatenate([send(up, weights_out(i)) for i in range(2)], 1)
    down = jnp.concatenate([send(down, weights_out(i)) for i in range(2)], 0)
    return up, down


def expert_grads_home(layer, grad_up, grad_down):
    half = grad_up.shape[1] // 2

    def home(first, second):
        first = send(first.astype(BF16), weights_home(0)).astype(F32)
        return first + send(second.astype(BF16), weights_home(1)).astype(F32)

    grad_up = home(grad_up[:, :half], grad_up[:, half:])
    grad_down = home(grad_down[:half], grad_down[half:])

    def across(value):
        return send(
            value.astype(BF16), lambda x, h, c, t: (layer, h, c, t) if x != layer else None
        ).astype(F32)

    return (grad_up, across(grad_up)), (grad_down, across(grad_down))


def to_expert(selection, rows, experts):
    _, _, c, _ = place()
    half = rows.shape[1] // 2
    own = jnp.where(c == 0, rows[:, :half], rows[:, half:])
    buffers = jnp.dot(selection, own, preferred_element_type=F32).astype(BF16)
    buffers = buffers.reshape(experts, -1, half)
    if experts > DIRECT:
        arrived = expert_exchange(buffers).reshape(-1, half)
    else:
        arrived = jnp.concatenate(
            [buffers[0]] + [expert_swap(buffers[j], j) for j in range(1, experts)], 0
        )
    return ordered(c, arrived, core_swap(arrived), 1)


def from_expert(selection, partial, experts):
    _, _, c, _ = place()
    half = partial.shape[1] // 2
    keep = jnp.where(c == 0, partial[:, :half], partial[:, half:])
    give = jnp.where(c == 0, partial[:, half:], partial[:, :half])
    chip = (keep + core_swap(give.astype(BF16)).astype(F32)).astype(BF16)
    chip = chip.reshape(experts, -1, half)
    if experts > DIRECT:
        total = (chip.astype(F32) + section_swap(chip).astype(F32)).astype(BF16)
        produced = expert_exchange(total).reshape(-1, half)
    else:
        back = [None] * experts
        for j in range(experts - 1, -1, -1):
            total = (chip[j].astype(F32) + section_swap(chip[j]).astype(F32)).astype(BF16)
            back[j] = total if j == 0 else expert_swap(total, j)
        produced = jnp.concatenate(back, 0)
    rows = lax.dot_general(
        selection, produced, (((0,), (0,)), ((), ())), preferred_element_type=F32
    ).astype(BF16)
    return ordered(c, rows, core_swap(rows), 1)


def layer_forward(rows, params, attention, expert, table, experts):
    gain_one, base, prefix, gain_two, router, chosen, selection = params
    qkv_weights, out_weights = attention
    up, down = expert
    x, _, c, _ = place()
    values = rows.astype(F32)
    scale_one, normed = norm(values, gain_one)
    qkv = jnp.einsum("rx,vxj->vrj", normed, qkv_weights, preferred_element_type=F32).astype(BF16)
    own, weights = attend(qkv, base, prefix)
    pair = ordered(x, own, section_swap(own), 1)
    merged = ordered(c, pair, core_swap(pair), 1)
    middle = values + lax.dot_general(
        merged, out_weights, (((1,), (1,)), ((), ())), preferred_element_type=F32
    )
    scale_two, normed_two = norm(middle, gain_two)
    logits = jnp.dot(normed_two, router, preferred_element_type=F32)
    probs = jax.nn.softmax(logits, -1)
    gates = jnp.sum(probs * chosen, 1, keepdims=True)
    arrived = to_expert(selection, normed_two, experts)
    hidden = jnp.dot(arrived, up, preferred_element_type=F32)
    active = jax.nn.gelu(hidden).astype(BF16)
    partial = jnp.dot(active, down, preferred_element_type=F32)
    produced = from_expert(selection, partial, experts).astype(F32)
    result = middle + gates * produced
    saved = (
        values,
        scale_one,
        normed,
        qkv,
        own,
        weights,
        middle,
        scale_two,
        normed_two,
        probs,
        gates,
        arrived,
        hidden,
        active,
        produced,
    )
    return result.astype(BF16), saved


def layer_backward(layer, grad, saved, params, attention, expert, experts):
    gain_one, base, prefix, gain_two, router, chosen, selection = params
    qkv_weights, out_weights = attention
    up, down = expert
    (
        values,
        scale_one,
        normed,
        qkv,
        own,
        weights,
        middle,
        scale_two,
        normed_two,
        probs,
        gates,
        arrived,
        hidden,
        active,
        produced,
    ) = saved
    x, h, c, t = place()
    grad = grad.astype(F32)
    grad_expert = (gates * grad).astype(BF16)
    grad_gates = jnp.sum(grad * produced, -1, keepdims=True)
    grad_arrived = to_expert(selection, grad_expert, experts)
    grad_active = lax.dot_general(
        grad_arrived, down, (((1,), (1,)), ((), ())), preferred_element_type=F32
    )
    grad_hidden = jax.vjp(jax.nn.gelu, hidden)[1](grad_active)[0].astype(BF16)
    partial = lax.dot_general(
        grad_hidden, up, (((1,), (1,)), ((), ())), preferred_element_type=F32
    )
    over_rows = (((0,), (0,)), ((), ()))
    grad_up = lax.dot_general(arrived, grad_hidden, over_rows, preferred_element_type=F32)
    grad_down = lax.dot_general(active, grad_arrived, over_rows, preferred_element_type=F32)
    expert_grads = expert_grads_home(layer, grad_up, grad_down)
    grad_normed_two = from_expert(selection, partial, experts).astype(F32)
    grad_probs = chosen * grad_gates
    grad_logits = (
        probs * (grad_probs - jnp.sum(probs * grad_probs, 1, keepdims=True))
    ).astype(BF16)
    grad_router = lax.dot_general(
        normed_two, grad_logits, over_rows, preferred_element_type=F32
    )
    grad_normed_two = grad_normed_two + lax.dot_general(
        grad_logits, router, (((1,), (1,)), ((), ())), preferred_element_type=F32
    )
    grad_middle, grad_gain_two = norm_back(middle, scale_two, gain_two, grad_normed_two)
    grad_middle = grad_middle + grad
    grad_low = grad_middle.astype(BF16)
    width = own.shape[1]
    own_weights = lax.dynamic_slice_in_dim(out_weights, (x + 2 * c) * width, width, 1)
    grad_own = jnp.dot(grad_low, own_weights, preferred_element_type=F32).astype(BF16)
    dq, dk, dv, diagonal = attend_back(qkv, weights, grad_own)
    dp = jnp.stack([dq, dk, dv])
    partial = jnp.einsum("vrj,vxj->rx", dp, qkv_weights, preferred_element_type=F32)
    half = partial.shape[1] // 2
    keep = jnp.where(c == 0, partial[:, :half], partial[:, half:])
    give = jnp.where(c == 0, partial[:, half:], partial[:, :half])
    chip = (keep + core_swap(give.astype(BF16)).astype(F32)).astype(BF16)
    total = (chip.astype(F32) + section_swap(chip).astype(F32)).astype(BF16)
    grad_normed = ordered(c, total, core_swap(total), 1).astype(F32)
    grad_rows, grad_gain_one = norm_back(values, scale_one, gain_one, grad_normed)
    grad_rows = (grad_rows + grad_middle).astype(BF16)
    grad_in = jnp.einsum("rx,vrj->xvj", normed, dp, preferred_element_type=F32)
    grad_out = lax.dot_general(grad_low, own, over_rows, preferred_element_type=F32)
    head_grads = jnp.concatenate([grad_in, grad_out[:, None]], 1)
    head_grads = head_grads.reshape(head_grads.shape[0], -1)
    small = (grad_gain_one, grad_gain_two, grad_router, diagonal)
    return grad_rows, expert_grads, head_grads_home(layer, head_grads), small


def head_grads_home(layer, grads):
    _, h, _, t = place()
    groups = 2 * lax.axis_size("dp")
    pieces = grads.astype(BF16).reshape(groups, -1, grads.shape[1])
    mine = 4 * h + t

    def swap(value, j):
        def to(x, h, c, t):
            n = (4 * h + t) ^ j
            return (x, n >> 2, c, n & 3)

        return send(value, to)

    if groups > DIRECT:
        bit = groups // 2
        while bit:
            pair = pieces.reshape(2, bit, *pieces.shape[1:])
            upper = (mine & bit) != 0
            keep = jnp.where(upper, pair[1], pair[0]).astype(F32)
            give = jnp.where(upper, pair[0], pair[1]).astype(BF16)
            pieces = keep + swap(give, bit).astype(F32)
            bit //= 2
        total = pieces[0].astype(BF16)
    else:
        total = at(pieces, mine).astype(F32)
        for j in range(1, groups):
            total = total + swap(at(pieces, mine ^ j), j).astype(F32)
        total = total.astype(BF16)
    parts = []
    for i in range(2):

        def home(x, h, c, t, i=i):
            return (layer, h, t >> 1, x + 2 * c) if t & 1 == i else None

        parts.append(send(total, home))
    whole = jnp.concatenate(parts, 0).astype(F32)
    return whole.reshape(whole.shape[0], 4, -1)


def pick(flag, first, second):
    return jax.tree.map(lambda a, b: jnp.where(flag == 0, a, b), first, second)


def per_device(
    block_input,
    cotangent,
    query_key_value_weights,
    attention_output_weights,
    bias_table,
    norm_first,
    norm_second,
    router_projection_weights,
    expert_up,
    expert_down,
    routes,
    prefix_lengths,
    relative_buckets,
):
    x, h, c, t = place()
    _, piece, width = block_input.shape
    length = routes.shape[2]
    buckets, head_count = bias_table.shape[1:]
    experts = router_projection_weights.shape[2]
    heads = head_count // 4
    capacity = (5 * length + 4 * experts - 1) // (4 * experts)

    pieces = jnp.concatenate(
        [query_key_value_weights[0], attention_output_weights[0].T[None]], 0
    )
    other = section_swap(pieces)
    pieces = pick(x, (pieces, other), (other, pieces))
    scale = 32
    packed = jnp.concatenate(
        [
            routes[0, :, :, 0].reshape(-1),
            prefix_lengths // scale,
            prefix_lengths % scale,
        ]
    ).astype(BF16)
    both = ordered(c, packed[None], core_swap(packed)[None], 0)
    lower = at(both, t >> 1)
    route = lax.dynamic_slice_in_dim(lower, (t & 1) * length, length, 0)
    numbers = lower[2 * length :].astype(F32).astype(jnp.int32)
    prefix = lax.dynamic_slice_in_dim(numbers[:2] * scale + numbers[2:], t & 1, 1, 0)
    packed = jnp.concatenate(
        [
            route,
            norm_first[0],
            norm_second[0],
            router_projection_weights[0].reshape(-1),
            bias_table[0].reshape(-1),
        ]
    )
    other = section_swap(packed)
    packed = pick(x, (packed, other), (other, packed))

    half = expert_up.shape[3] // 2
    up, down = expert_up[0, 0], expert_down[0, 0]
    give = jnp.where(x == 0, up[:, half:], up[:, :half])
    keep = jnp.where(x == 0, up[:, :half], up[:, half:])
    other = section_swap(give)
    ups = pick(x, (keep, other), (other, keep))
    give = jnp.where(x == 0, down[half:], down[:half])
    keep = jnp.where(x == 0, down[:half], down[half:])
    other = section_swap(give)
    downs = pick(x, (keep, other), (other, keep))

    rows = to_groups(block_input)
    top = to_groups(cotangent)

    bucket_onehot = (
        relative_buckets[:, None] == jnp.arange(buckets, dtype=jnp.int32)[None, :]
    ).astype(BF16)
    earlier = (
        jnp.arange(length, dtype=jnp.int32)[None, :] < jnp.arange(length, dtype=jnp.int32)[:, None]
    ).astype(BF16)
    expert_ids = jnp.arange(experts, dtype=jnp.int32)

    def unpack(vector):
        route = vector[:length].astype(F32).astype(jnp.int32)
        at_one = length
        gain_one = vector[at_one : at_one + width].astype(F32)
        at_two = at_one + width
        gain_two = vector[at_two : at_two + width].astype(F32)
        at_router = at_two + width
        router = vector[at_router : at_router + width * experts].reshape(width, experts)
        table = vector[at_router + width * experts :].reshape(buckets, head_count)
        own = lax.dynamic_slice_in_dim(table, (x + 2 * c) * heads, heads, 1)
        rel = lax.dot_general(
            own, bucket_onehot, (((0,), (1,)), ((), ())), preferred_element_type=F32
        )
        base = jnp.roll(jnp.pad(rel, ((0, 0), (0, 1))), -(BLOCK - 1), axis=1)
        chosen = route[:, None] == expert_ids[None, :]
        rank = jnp.dot(earlier, chosen.astype(BF16), preferred_element_type=F32)
        rank = jnp.sum(jnp.where(chosen, rank, 0.0), 1).astype(jnp.int32)
        slot = (route ^ (2 * h + (t & 1))) * capacity + rank
        selection = (
            slot[None, :] == jnp.arange(experts * capacity, dtype=jnp.int32)[:, None]
        ).astype(BF16)
        return (gain_one, base, prefix, gain_two, router, chosen.astype(F32), selection)

    params = [unpack(vector) for vector in packed]
    attention = [attention_weights(part) for part in pieces]
    expert = [expert_weights(*pair) for pair in zip(ups, downs)]

    first, saved_first = layer_forward(rows, params[0], attention[0], expert[0], None, experts)
    second, saved_second = layer_forward(first, params[1], attention[1], expert[1], None, experts)
    outputs = from_groups(jnp.where(x == 0, first, second))

    grads_one = layer_backward(
        1, top, saved_second, params[1], attention[1], expert[1], experts
    )
    grads_zero = layer_backward(
        0, grads_one[0], saved_first, params[0], attention[0], expert[0], experts
    )
    grad_rows = from_groups(jnp.where(x == 0, grads_zero[0], grads_one[0]))

    def halves(zero, one, axis):
        own = jnp.where(x == 0, zero[0], one[0])
        other = jnp.where(x == 0, zero[1], one[1])
        return ordered(x, own, other, axis)

    grad_up = halves(grads_zero[1][0], grads_one[1][0], 1)
    grad_down = halves(grads_zero[1][1], grads_one[1][1], 0)
    heads_grad = jnp.where(x == 0, grads_zero[2], grads_one[2])
    grad_in = jnp.transpose(heads_grad[:, :3], (1, 0, 2))
    grad_out = heads_grad[:, 3].T

    def flat(small):
        gain_one, gain_two, router, diagonal = small
        total = jnp.roll(diagonal, BLOCK - 1, axis=1)[:, : 2 * length - 1]
        table = lax.dot_general(
            bucket_onehot.astype(F32),
            total,
            (((0,), (1,)), ((), ())),
            precision=lax.Precision.HIGHEST,
        )
        whole = lax.dynamic_update_slice_in_dim(
            jnp.zeros((buckets, head_count), F32), table, (x + 2 * c) * heads, 1
        )
        return jnp.concatenate([gain_one, gain_two, router.reshape(-1)]), whole.reshape(-1)

    shared = [flat(small) for small in (grads_zero[3], grads_one[3])]
    size = shared[0][0].shape[0]
    everything = jnp.concatenate([shared[0][0], shared[1][0], shared[0][1], shared[1][1]])
    for j in (1, 2):
        everything = everything + tensor_swap(everything, j)
    bit = 1
    while bit < lax.axis_size("dp") // 2:
        everything = everything + host_swap(everything, bit)
        bit *= 2
    tables = everything[2 * size :]
    tables = tables + core_swap(tables)
    tables = tables + section_swap(tables)
    table_grad = at(tables.reshape(2, buckets, head_count), x)
    own = lax.dynamic_slice_in_dim(everything, x * size, size, 0)
    return (
        outputs[None],
        grad_rows[None],
        grad_in[None],
        grad_out[None],
        table_grad[None],
        own[:width][None],
        own[width : 2 * width][None],
        own[2 * width :].reshape(width, experts)[None],
        grad_up[None, None],
        grad_down[None, None],
    )


def solution(mesh):
    in_specs = (
        P("dp", "tensor", None),
        P("dp", "tensor", None),
        P("section", None, "dp", "tensor"),
        P("section", "tensor", "dp"),
        P("section", None, None),
        P("section", None),
        P("section", None),
        P("section", None, None),
        P("section", "dp", None, "tensor"),
        P("section", "dp", "tensor", None),
        P("section", "dp", None, None),
        P("dp"),
        P(),
    )
    out_specs = (
        P("section", "dp", "tensor", None),
        P("section", "dp", "tensor", None),
        P("section", None, "dp", "tensor"),
        P("section", "tensor", "dp"),
        P("section", None, None),
        P("section", None),
        P("section", None),
        P("section", None, None),
        P("section", "dp", None, "tensor"),
        P("section", "dp", "tensor", None),
    )
    return jax.shard_map(
        per_device, mesh=mesh, in_specs=in_specs, out_specs=out_specs, check_vma=False
    )
```

time: 4160 us -> 960 us (0.23)
  local copies, waits for them, and re-layouts: 1940 us -> 99 us
  waiting for transfers between devices: 912 us -> 335 us
  blocking collectives: 357 us -> 0 us
  matrix products: 371 us -> 73.5 us
  other arithmetic: 354 us -> 123 us
  starting transfers between devices: 45.6 us -> 232 us
  loops' own time: 138 us -> 0 us
  Pallas kernels: 0 us -> 82.1 us
    while x226 -> x0, local copies, waits for them, and re-layouts: 664 us -> none
    reshape x42 -> x11, local copies, waits for them, and re-layouts: 536 us -> 11.3 us  [the longest x2 8.01 us: attention_weights(): out = jnp.transpose(four, (1, 2, 3, 0, 4)).reshape(qkv.shape[1], -1)]
    all_gather x18 -> x0, waiting for transfers between devices: 463 us -> none  [gather_rows(): return lax.all_gather(values, 'tensor', axis=1, tiled=True)]
    reduce_scatter x18 -> x0, waiting for transfers between devices: 359 us -> none  [sum_rows(): lax.psum_scatter(values.astype(jnp.bfloat16), 'tensor', scatter_dimension...]
    ppermute x4 -> x148, waiting for transfers between devices: 25.8 us -> 335 us  [send(): return lax.ppermute(value, AXES, pairs)]
    dot_general x109 -> x42, matrix products: 355 us -> 69.8 us  [the longest x4 10.7 us: from_expert(): lax.dot_general(selection, produced, (((0,), (0,)), ((), ())), preferred_...]
    all_to_all x10 -> x0, blocking collectives: 275 us -> none  [the longest x5 140 us: from_experts(): lax.all_to_all(produced.astype(jnp.bfloat16), 'dp', split_axis=1, concat_...]
    slice x18 -> x30, local copies, waits for them, and re-layouts: 242 us -> 8.38 us  [the longest x4 2.83 us: unpack(): vector[at_router:at_router + width * experts].reshape(width, experts)]
  transfers between devices with their start and end apart: 54 -> 148, of which waited for: 34 -> 71; matrix products, arithmetic and copies ran while one was open for 47% -> 22% of each run, Pallas kernels for 0% -> 6%
where the time goes in v1:
time: 960 us; the launch traced here: 950 us
  waiting for transfers between devices  335 us (35%)
  starting transfers between devices  232 us (24%)
  other arithmetic  123 us (13%)
  local copies, waits for them, and re-layouts  99 us (10%)
  Pallas kernels  82.1 us (9%)
  matrix products  73.5 us (8%)
    ppermute x148, waiting for transfers between devices, send(): return lax.ppermute(value, AXES, pairs)  335 us
    ppermute x148, starting transfers between devices, send(): return lax.ppermute(value, AXES, pairs)  232 us
    pallas_call x2, Pallas kernels, attend_back(): pl.pallas_call(functools.partial(attend_back_kernel, heads), grid=(length...  44.8 us
    unnamed x400, local copies, waits for them, and re-layouts  43 us
    pallas_call x2, Pallas kernels, attend(): pl.pallas_call(functools.partial(attend_kernel, heads), grid=(length // B...  37.3 us
    select_n x28, other arithmetic, ordered(): first = jnp.where(flag == 0, own, other)  29.1 us
  transfers between devices with their start and end apart: 148, of which 71 were waited for; matrix products, arithmetic and copies ran while one was open for 22% of the time, Pallas kernels for 6%

profile of v1, /device:TPU:0, one launch (start us, length us, event | category | flops | bytes accessed | tf_op | source)
XLA Modules:
  0.0 949.8 jit_solution(734644341994883922)
XLA Ops:
  22.7 5.3 collective-permute-start.48
  35.9 6.5 collective-permute-done.1
  42.4 11.1 %collective-permute-done.2 = bf16[128,768]{1,0:T(8,128)(2,1)S(1)} collective-permute-done((bf16[128,768]{1,0:T(8,128)(2,1)S(1)}, bf16[128,768]{1,0:T(8,128)(2,1)S(1)}, u32[]{:S(2)}, u32[]{:S(2)}) %collective-permute-start.2) | collective-permute-done | bytes 196640 | tf_op jit(solution)/shard_map/ppermute | solution.py:33
  54.3 3.8 collective-permute-start.16
  59.9 4.3 collective-permute-start.10
  82.6 13.0 %collective-permute-done.11 = bf16[3,1,384,192]{2,3,1,0:T(8,128)(2,1)S(1)} collective-permute-done((bf16[3,1,384,192]{2,3,1,0:T(8,128)(2,1)S(1)}, bf16[3,1,384,192]{2,3,1,0:T(8,128)(2,1)S(1)}, u32[]{:S(2)}, u32[]{:S(2)}) %collective-permute-start.11) | collective-permute-done | bytes 442400 | tf_op jit(solution)/shard_map/ppermute | solution.py:33
  100.8 18.7 %shard_map.204 = (bf16[1024,192]{1,0:T(8,128)(2,1)S(1)}, bf16[3,1024,1024]{2,1,0:T(8,128)(2,1)S(1)}) custom-call(s32[1]{0:T(128)} %bitcast.15.prefix_ref, bf16[3,1024,192]{2,1,0:T(8,128)(2,1)S(1)} %bitcast.372, bf16[3,1024,192]{2,1,0:T(8,128)(2,1)S(1)} %bitcast.373, bf16[3,1024,192]{2,1,0:T(8,128)(2,1)S(1)} %bitcast.374, ...), custom_call_target="tpu_custom_call" | custom-call | tf_op jit(solution)/shard_map/pallas_call | solution.py:170
  124.1 11.3 %collective-permute-done.13 = bf16[1024,192]{1,0:T(8,128)(2,1)S(1)} collective-permute-done((bf16[1024,192]{1,0:T(8,128)(2,1)S(1)}, bf16[1024,192]{1,0:T(8,128)(2,1)S(1)}, u32[]{:S(2)}, u32[]{:S(2)}) %collective-permute-start.13) | collective-permute-done | bytes 393248 | tf_op jit(solution)/shard_map/ppermute | solution.py:33
  138.4 4.0 copy.444
  142.4 4.0 reshape.410
  160.6 6.0 collective-permute-start.28
  175.9 6.0 collective-permute-start.25
  184.6 13.8 %collective-permute-done.29 = bf16[384,768]{1,0:T(8,128)(2,1)} collective-permute-done((bf16[384,768]{1,0:T(8,128)(2,1)}, bf16[384,768]{1,0:T(8,128)(2,1)}, u32[]{:S(2)}, u32[]{:S(2)}) %collective-permute-start.29) | collective-permute-done | bytes 589856 | tf_op jit(solution)/shard_map/ppermute | solution.py:33
  199.5 13.4 %collective-permute-done.26 = bf16[768,384]{1,0:T(8,128)(2,1)} collective-permute-done((bf16[768,384]{1,0:T(8,128)(2,1)}, bf16[768,384]{1,0:T(8,128)(2,1)}, u32[]{:S(2)}, u32[]{:S(2)}) %collective-permute-start.26) | collective-permute-done | bytes 589856 | tf_op jit(solution)/shard_map/ppermute | solution.py:33
  221.8 7.6 collective-permute-start.30
  241.5 4.7 collective-permute-done.41
  246.2 4.7 collective-permute-done.40
  252.2 4.6 collective-permute-done.34
  284.9 18.7 %shard_map.205 = (bf16[1024,192]{1,0:T(8,128)(2,1)S(1)}, bf16[3,1024,1024]{2,1,0:T(8,128)(2,1)S(1)}) custom-call(s32[1]{0:T(128)} %bitcast.15.prefix_ref, bf16[3,1024,192]{2,1,0:T(8,128)(2,1)S(1)} %bitcast.378, bf16[3,1024,192]{2,1,0:T(8,128)(2,1)S(1)} %bitcast.379, bf16[3,1024,192]{2,1,0:T(8,128)(2,1)S(1)} %bitcast.380, ...), custom_call_target="tpu_custom_call" | custom-call | tf_op jit(solution)/shard_map/pallas_call | solution.py:170
  309.7 11.0 %collective-permute-done.44 = bf16[1024,192]{1,0:T(8,128)(2,1)S(1)} collective-permute-done((bf16[1024,192]{1,0:T(8,128)(2,1)S(1)}, bf16[1024,192]{1,0:T(8,128)(2,1)S(1)}, u32[]{:S(2)}, u32[]{:S(2)}) %collective-permute-start.44) | collective-permute-done | bytes 393248 | tf_op jit(solution)/shard_map/ppermute | solution.py:33
  324.1 4.0 copy.451
  328.1 4.0 reshape.413
  344.9 4.8 collective-permute-done.53
  349.7 5.0 collective-permute-done.52
  359.0 5.1 collective-permute-start.58
  366.7 11.2 %collective-permute-done.58 = bf16[384,768]{1,0:T(8,128)(2,1)S(1)} collective-permute-done((bf16[384,768]{1,0:T(8,128)(2,1)S(1)}, bf16[384,768]{1,0:T(8,128)(2,1)S(1)}, u32[]{:S(2)}, u32[]{:S(2)}) %collective-permute-start.58) | collective-permute-done | bytes 589856 | tf_op jit(solution)/shard_map/ppermute | solution.py:33
  378.0 12.6 %collective-permute-done.56 = bf16[768,384]{1,0:T(8,128)(2,1)S(1)} collective-permute-done((bf16[768,384]{1,0:T(8,128)(2,1)S(1)}, bf16[768,384]{1,0:T(8,128)(2,1)S(1)}, u32[]{:S(2)}, u32[]{:S(2)}) %collective-permute-start.56) | collective-permute-done | bytes 589856 | tf_op jit(solution)/shard_map/ppermute | solution.py:33
  396.8 13.0 %collective-permute-start.59 = (bf16[1280,384]{1,0:T(8,128)(2,1)S(1)}, bf16[1280,384]{1,0:T(8,128)(2,1)S(1)}, u32[]{:S(2)}, u32[]{:S(2)}) collective-permute-start(bf16[1280,384]{1,0:T(8,128)(2,1)S(1)} %select_convert_fusion.2), channel_id=1, source_target_pairs={{0,4},{1,5},{2,6},{3,7},{4,0},{5,1},{6,2},{7,3},{8,12},{9,13},{10,... | collective-permute-start | bytes 2949128 | tf_op jit(solution)/shard_map/ppermute | solution.py:33
  414.6 6.3 collective-permute-done.73
  420.9 7.3 collective-permute-done.74
  437.7 5.3 collective-permute-done.65
  443.0 5.3 collective-permute-done.63
  452.8 4.9 collective-permute-start.62
  464.9 4.8 collective-permute-done.64
  485.6 6.2 collective-permute-done.79
  491.8 4.8 collective-permute-done.78
  527.0 4.0 collective-permute-done.87
  531.3 4.9 collective-permute-done.85
  536.3 4.7 collective-permute-done.83
  545.0 5.2 collective-permute-done.84
  550.3 3.8 collective-permute-done.88
  577.9 22.5 %shard_map.206 = (bf16[1024,192]{1,0:T(8,128)(2,1)S(1)}, bf16[1024,192]{1,0:T(8,128)(2,1)S(1)}, bf16[1024,192]{1,0:T(8,128)(2,1)S(1)}, f32[3,2048]{1,0:T(4,128)S(1)}) custom-call(bf16[3,1024,192]{2,1,0:T(8,128)(2,1)S(1)} %bitcast.381, bf16[3,1024,192]{2,1,0:T(8,128)(2,1)S(1)} %bitcast.382, bf16[3,1024,192]{2,1,0:T(8,128)(2,1)S(1)} %bitcast.383, ...), custom_call_target="tpu_custom_call" | custom-call | tf_op jit(solution)/shard_map/pallas_call | solution.py:251
  613.9 6.0 collective-permute-start.138
  619.9 6.0 collective-permute-done.91
  627.0 12.3 %collective-permute-done.145 = bf16[384,768]{1,0:T(8,128)(2,1)S(1)} collective-permute-done((bf16[384,768]{1,0:T(8,128)(2,1)S(1)}, bf16[384,768]{1,0:T(8,128)(2,1)S(1)}, u32[]{:S(2)}, u32[]{:S(2)}) %collective-permute-start.145) | collective-permute-done | bytes 589856 | tf_op jit(solution)/shard_map/ppermute | solution.py:33
  680.9 5.1 collective-permute-done.123
  688.8 9.6 %collective-permute-start.122 = (bf16[96,768]{0,1:T(8,128)(2,1)S(1)}, bf16[96,768]{0,1:T(8,128)(2,1)S(1)}, u32[]{:S(2)}, u32[]{:S(2)}) collective-permute-start(bf16[96,768]{0,1:T(8,128)(2,1)S(1)} %bitcast.442), channel_id=1, source_target_pairs={{0,1},{1,0},{2,3},{3,2},{4,5},{5,4},{6,7},{7,6},{8,9},{9,8},{10,11... | collective-permute-start | bytes 442376 | tf_op jit(solution)/shard_map/ppermute | solution.py:33
  708.3 3.8 collective-permute-start.129
  716.3 4.6 collective-permute-done.129
  735.6 6.0 collective-permute-start.142
  751.4 5.3 collective-permute-done.103
  756.7 4.3 collective-permute-done.101
  768.6 4.3 collective-permute-done.100
  772.9 6.0 collective-permute-start.136
  782.3 4.5 collective-permute-start.147
  792.4 9.9 %collective-permute-done.137 = bf16[768,384]{1,0:T(8,128)(2,1)} collective-permute-done((bf16[768,384]{1,0:T(8,128)(2,1)}, bf16[768,384]{1,0:T(8,128)(2,1)}, u32[]{:S(2)}, u32[]{:S(2)}) %collective-permute-start.137) | collective-permute-done | bytes 589856 | tf_op jit(solution)/shard_map/ppermute | solution.py:33
  817.0 22.3 %shard_map.207 = (bf16[1024,192]{1,0:T(8,128)(2,1)S(1)}, bf16[1024,192]{1,0:T(8,128)(2,1)S(1)}, bf16[1024,192]{1,0:T(8,128)(2,1)S(1)}, f32[3,2048]{1,0:T(4,128)S(1)}) custom-call(bf16[3,1024,192]{2,1,0:T(8,128)(2,1)S(1)} %bitcast.375, bf16[3,1024,192]{2,1,0:T(8,128)(2,1)S(1)} %bitcast.376, bf16[3,1024,192]{2,1,0:T(8,128)(2,1)S(1)} %bitcast.377, ...), custom_call_target="tpu_custom_call" | custom-call | tf_op jit(solution)/shard_map/pallas_call | solution.py:251
  846.7 3.9 fusion.94
  868.1 3.7 collective-permute-start.117
  871.8 4.1 collective-permute-done.107
  884.0 9.2 collective-permute-start.113
  906.0 7.7 collective-permute-done.121
  929.0 4.9 collective-permute-done.132
  938.0 5.6 collective-permute-done.110
  (950 shorter events, 474.3 us)
Async XLA Ops:
  4.7 26.3 %collective-permute-start = (bf16[2,128,768]{2,1,0:T(8,128)(2,1)}, bf16[2,128,768]{2,1,0:T(8,128)(2,1)S(1)}, u32[]{:S(2)}, u32[]{:S(2)}) collective-permute-start(bf16[2,128,768]{2,1,0:T(8,128)(2,1)} %fusion.156), channel_id=1, source_target_pairs={{0,4},{1,5},{2,6},{3,7},{4,0},{5,1},{6,2},{7,3},{8,12},{9,13},{10,... | collective-permute-start | bytes 1179656 | tf_op jit(solution)/shard_map/ppermute | solution.py:33
  22.7 35.7 %collective-permute-start.48 = (bf16[192,192]{0,1:T(8,128)(2,1)S(1)}, bf16[192,192]{0,1:T(8,128)(2,1)S(1)}, u32[]{:S(2)}, u32[]{:S(2)}) collective-permute-start(bf16[192,192]{0,1:T(8,128)(2,1)S(1)} %get-tuple-element.286), channel_id=1, source_target_pairs={{0,3},{1,2},{2,1},{3,0},{4,7},{5,6},{6,5},{7,4},{8,11},{9,10},{10,... | collective-permute-start | bytes 221192 | tf_op jit(solution)/shard_map/ppermute | solution.py:33
  28.0 30.6 %collective-permute-start.47 = (bf16[192,192]{0,1:T(8,128)(2,1)S(1)}, bf16[192,192]{0,1:T(8,128)(2,1)S(1)}, u32[]{:S(2)}, u32[]{:S(2)}) collective-permute-start(bf16[192,192]{0,1:T(8,128)(2,1)S(1)} %get-tuple-element.286), channel_id=1, source_target_pairs={{0,2},{1,3},{2,0},{3,1},{4,6},{5,7},{6,4},{7,5},{8,10},{9,11},{10,... | collective-permute-start | bytes 221192 | tf_op jit(solution)/shard_map/ppermute | solution.py:33
  32.9 20.5 %collective-permute-start.2 = (bf16[128,768]{1,0:T(8,128)(2,1)S(1)}, bf16[128,768]{1,0:T(8,128)(2,1)S(1)}, u32[]{:S(2)}, u32[]{:S(2)}) collective-permute-start(bf16[128,768]{1,0:T(8,128)(2,1)S(1)} %get-tuple-element.275), channel_id=1, source_target_pairs={{0,2},{1,3},{2,0},{3,1},{4,6},{5,7},{6,4},{7,5},{8,10},{9,11},{10,... | collective-permute-start | bytes 589832 | tf_op jit(solution)/shard_map/ppermute | solution.py:33
  33.5 20.8 %collective-permute-start.3 = (bf16[128,768]{1,0:T(8,128)(2,1)S(1)}, bf16[128,768]{1,0:T(8,128)(2,1)S(1)}, u32[]{:S(2)}, u32[]{:S(2)}) collective-permute-start(bf16[128,768]{1,0:T(8,128)(2,1)S(1)} %get-tuple-element.276), channel_id=1, source_target_pairs={{0,3},{1,2},{2,1},{3,0},{4,7},{5,6},{6,5},{7,4},{8,11},{9,10},{10,... | collective-permute-start | bytes 589832 | tf_op jit(solution)/shard_map/ppermute | solution.py:33
  42.4 17.5 %collective-permute-start.46 = (bf16[192,192]{0,1:T(8,128)(2,1)S(1)}, bf16[192,192]{0,1:T(8,128)(2,1)S(1)}, u32[]{:S(2)}, u32[]{:S(2)}) collective-permute-start(bf16[192,192]{0,1:T(8,128)(2,1)S(1)} %get-tuple-element.286), channel_id=1, source_target_pairs={{0,1},{1,0},{2,3},{3,2},{4,5},{5,4},{6,7},{7,6},{8,9},{9,8},{10,11... | collective-permute-start | bytes 221192 | tf_op jit(solution)/shard_map/ppermute | solution.py:33
  58.4 22.9 %collective-permute-start.4 = (bf16[4,128,768]{2,1,0:T(8,128)(2,1)S(1)}, bf16[4,128,768]{2,1,0:T(8,128)(2,1)S(1)}, u32[]{:S(2)}, u32[]{:S(2)}) collective-permute-start(bf16[4,128,768]{2,1,0:T(8,128)(2,1)S(1)} %pad_maximum_fusion.30), channel_id=1, source_target_pairs={{0,4},{1,5},{2,6},{3,7},{4,0},{5,1},{6,2},{7,3},{8,12},{9,13},{10,... | collective-permute-start | bytes 2359304 | tf_op jit(solution)/shard_map/ppermute | solution.py:33
  67.5 90.9 %collective-permute-start.27 = (bf16[384,768]{1,0:T(8,128)(2,1)}, bf16[384,768]{1,0:T(8,128)(2,1)}, u32[]{:S(2)}, u32[]{:S(2)}) collective-permute-start(bf16[384,768]{1,0:T(8,128)(2,1)} %select_bitcast_fusion.8), channel_id=1, source_target_pairs={{0,16},{1,17},{2,18},{3,19},{4,20},{5,21},{6,22},{7,23},{8,24},{9,... | collective-permute-start | bytes 1769480 | tf_op jit(solution)/shard_map/ppermute | solution.py:33
  70.3 103.4 %collective-permute-start.24 = (bf16[768,384]{1,0:T(8,128)(2,1)}, bf16[768,384]{1,0:T(8,128)(2,1)}, u32[]{:S(2)}, u32[]{:S(2)}) collective-permute-start(bf16[768,384]{1,0:T(8,128)(2,1)} %broadcast_select_fusion.27), channel_id=1, source_target_pairs={{0,16},{1,17},{2,18},{3,19},{4,20},{5,21},{6,22},{7,23},{8,24},{9,... | collective-permute-start | bytes 1769480 | tf_op jit(solution)/shard_map/ppermute | solution.py:33
  74.7 48.0 %collective-permute-start.18 = (bf16[4,1,192,192]{2,3,0,1:T(8,128)(2,1)}, bf16[4,1,192,192]{2,3,0,1:T(8,128)(2,1)}, u32[]{:S(2)}, u32[]{:S(2)}) collective-permute-start(bf16[4,1,192,192]{2,3,0,1:T(8,128)(2,1)} %maximum_bitcast_fusion.6), channel_id=1, source_target_pairs={{0,8},{1,9},{2,10},{3,11},{4,12},{5,13},{6,14},{7,15},{8,0},{9,1},... | collective-permute-start | bytes 884744 | tf_op jit(solution)/shard_map/ppermute | solution.py:33
  160.6 21.6 %collective-permute-start.28 = (bf16[384,768]{1,0:T(8,128)(2,1)}, bf16[384,768]{1,0:T(8,128)(2,1)}, u32[]{:S(2)}, u32[]{:S(2)}) collective-permute-start(bf16[384,768]{1,0:T(8,128)(2,1)} %get-tuple-element.126), channel_id=1, source_target_pairs={{0,0},{1,2},{2,4},{3,6},{4,1},{5,3},{6,5},{7,7},{8,8},{9,10},{10,1... | collective-permute-start | bytes 1769480 | tf_op jit(solution)/shard_map/ppermute | solution.py:33
  173.6 40.5 %collective-permute-start.23 = (bf16[1280,384]{1,0:T(8,128)(2,1)}, bf16[1280,384]{1,0:T(8,128)(2,1)}, u32[]{:S(2)}, u32[]{:S(2)}) collective-permute-start(bf16[1280,384]{1,0:T(8,128)(2,1)} %pad_maximum_fusion.25), channel_id=1, source_target_pairs={{0,4},{1,5},{2,6},{3,7},{4,0},{5,1},{6,2},{7,3},{8,12},{9,13},{10,... | collective-permute-start | bytes 2949128 | tf_op jit(solution)/shard_map/ppermute | solution.py:33
  181.9 16.5 %collective-permute-start.29 = (bf16[384,768]{1,0:T(8,128)(2,1)}, bf16[384,768]{1,0:T(8,128)(2,1)}, u32[]{:S(2)}, u32[]{:S(2)}) collective-permute-start(bf16[384,768]{1,0:T(8,128)(2,1)} %get-tuple-element.126), channel_id=1, source_target_pairs={{0,2},{1,0},{2,6},{3,4},{4,3},{5,1},{6,7},{7,5},{8,10},{9,8},{10,1... | collective-permute-start | bytes 1769480 | tf_op jit(solution)/shard_map/ppermute | solution.py:33
  181.9 31.0 %collective-permute-start.26 = (bf16[768,384]{1,0:T(8,128)(2,1)}, bf16[768,384]{1,0:T(8,128)(2,1)}, u32[]{:S(2)}, u32[]{:S(2)}) collective-permute-start(bf16[768,384]{1,0:T(8,128)(2,1)} %get-tuple-element.124), channel_id=1, source_target_pairs={{0,2},{1,0},{2,6},{3,4},{4,3},{5,1},{6,7},{7,5},{8,10},{9,8},{10,1... | collective-permute-start | bytes 1769480 | tf_op jit(solution)/shard_map/ppermute | solution.py:33
  221.8 16.6 %collective-permute-start.30 = (bf16[1280,384]{1,0:T(8,128)(2,1)S(1)}, bf16[1280,384]{1,0:T(8,128)(2,1)S(1)}, u32[]{:S(2)}, u32[]{:S(2)}) collective-permute-start(bf16[1280,384]{1,0:T(8,128)(2,1)S(1)} %select_convert_fusion.3), channel_id=1, source_target_pairs={{0,4},{1,5},{2,6},{3,7},{4,0},{5,1},{6,2},{7,3},{8,12},{9,13},{10,... | collective-permute-start | bytes 2949128 | tf_op jit(solution)/shard_map/ppermute | solution.py:33
  252.0 22.2 %collective-permute-start.43 = (bf16[3,1,384,192]{2,3,1,0:T(8,128)(2,1)}, bf16[3,1,384,192]{2,3,1,0:T(8,128)(2,1)}, u32[]{:S(2)}, u32[]{:S(2)}) collective-permute-start(bf16[3,1,384,192]{2,3,1,0:T(8,128)(2,1)} %bitcast.39), channel_id=1, source_target_pairs={{0,8},{1,9},{2,10},{3,11},{4,12},{5,13},{6,14},{7,15},{8,0},{9,1},... | collective-permute-start | bytes 1327112 | tf_op jit(solution)/shard_map/ppermute | solution.py:33
  266.4 41.7 %collective-permute-start.49 = (bf16[4,1,192,192]{2,3,0,1:T(8,128)(2,1)}, bf16[4,1,192,192]{2,3,0,1:T(8,128)(2,1)}, u32[]{:S(2)}, u32[]{:S(2)}) collective-permute-start(bf16[4,1,192,192]{2,3,0,1:T(8,128)(2,1)} %maximum_bitcast_fusion.7), channel_id=1, source_target_pairs={{0,8},{1,9},{2,10},{3,11},{4,12},{5,13},{6,14},{7,15},{8,0},{9,1},... | collective-permute-start | bytes 884744 | tf_op jit(solution)/shard_map/ppermute | solution.py:33
  344.2 20.6 %collective-permute-start.57 = (bf16[384,768]{1,0:T(8,128)(2,1)S(1)}, bf16[384,768]{1,0:T(8,128)(2,1)S(1)}, u32[]{:S(2)}, u32[]{:S(2)}) collective-permute-start(bf16[384,768]{1,0:T(8,128)(2,1)S(1)} %copy-done.112), channel_id=1, source_target_pairs={{0,0},{1,2},{2,4},{3,6},{4,1},{5,3},{6,5},{7,7},{8,8},{9,10},{10,1... | collective-permute-start | bytes 1769480 | tf_op jit(solution)/shard_map/ppermute | solution.py:33
  358.2 32.5 %collective-permute-start.54 = (bf16[1280,384]{1,0:T(8,128)(2,1)S(1)}, bf16[1280,384]{1,0:T(8,128)(2,1)S(1)}, u32[]{:S(2)}, u32[]{:S(2)}) collective-permute-start(bf16[1280,384]{1,0:T(8,128)(2,1)S(1)} %pad_maximum_fusion.26), channel_id=1, source_target_pairs={{0,4},{1,5},{2,6},{3,7},{4,0},{5,1},{6,2},{7,3},{8,12},{9,13},{10,... | collective-permute-start | bytes 2949128 | tf_op jit(solution)/shard_map/ppermute | solution.py:33
  359.0 18.9 %collective-permute-start.58 = (bf16[384,768]{1,0:T(8,128)(2,1)S(1)}, bf16[384,768]{1,0:T(8,128)(2,1)S(1)}, u32[]{:S(2)}, u32[]{:S(2)}) collective-permute-start(bf16[384,768]{1,0:T(8,128)(2,1)S(1)} %copy-done.112), channel_id=1, source_target_pairs={{0,2},{1,0},{2,6},{3,4},{4,3},{5,1},{6,7},{7,5},{8,10},{9,8},{10,1... | collective-permute-start | bytes 1769480 | tf_op jit(solution)/shard_map/ppermute | solution.py:33
  364.1 26.5 %collective-permute-start.56 = (bf16[768,384]{1,0:T(8,128)(2,1)S(1)}, bf16[768,384]{1,0:T(8,128)(2,1)S(1)}, u32[]{:S(2)}, u32[]{:S(2)}) collective-permute-start(bf16[768,384]{1,0:T(8,128)(2,1)S(1)} %copy-done.113), channel_id=1, source_target_pairs={{0,2},{1,0},{2,6},{3,4},{4,3},{5,1},{6,7},{7,5},{8,10},{9,8},{10,1... | collective-permute-start | bytes 1769480 | tf_op jit(solution)/shard_map/ppermute | solution.py:33
  364.8 45.0 %collective-permute-start.72 = (bf16[2,128,768]{2,1,0:T(8,128)(2,1)S(1)}, bf16[2,128,768]{2,1,0:T(8,128)(2,1)S(1)}, u32[]{:S(2)}, u32[]{:S(2)}) collective-permute-start(bf16[2,128,768]{2,1,0:T(8,128)(2,1)S(1)} %select_bitcast_fusion.11), channel_id=1, source_target_pairs={{0,4},{1,5},{2,6},{3,7},{4,0},{5,1},{6,2},{7,3},{8,12},{9,13},{10,... | collective-permute-start | bytes 1179656 | tf_op jit(solution)/shard_map/ppermute | solution.py:33
  396.8 31.6 %collective-permute-start.59 = (bf16[1280,384]{1,0:T(8,128)(2,1)S(1)}, bf16[1280,384]{1,0:T(8,128)(2,1)S(1)}, u32[]{:S(2)}, u32[]{:S(2)}) collective-permute-start(bf16[1280,384]{1,0:T(8,128)(2,1)S(1)} %select_convert_fusion.2), channel_id=1, source_target_pairs={{0,4},{1,5},{2,6},{3,7},{4,0},{5,1},{6,2},{7,3},{8,12},{9,13},{10,... | collective-permute-start | bytes 2949128 | tf_op jit(solution)/shard_map/ppermute | solution.py:33
  410.8 17.4 %collective-permute-start.74 = (bf16[128,768]{1,0:T(8,128)(2,1)S(1)}, bf16[128,768]{1,0:T(8,128)(2,1)S(1)}, u32[]{:S(2)}, u32[]{:S(2)}) collective-permute-start(bf16[128,768]{1,0:T(8,128)(2,1)S(1)} %get-tuple-element.261), channel_id=1, source_target_pairs={{0,2},{1,3},{2,0},{3,1},{4,6},{5,7},{6,4},{7,5},{8,10},{9,11},{10,... | collective-permute-start | bytes 589832 | tf_op jit(solution)/shard_map/ppermute | solution.py:33
  430.8 17.4 %collective-permute-start.63 = (bf16[320,384]{1,0:T(8,128)(2,1)S(1)}, bf16[320,384]{1,0:T(8,128)(2,1)S(1)}, u32[]{:S(2)}, u32[]{:S(2)}) collective-permute-start(bf16[320,384]{1,0:T(8,128)(2,1)S(1)} %get-tuple-element.217), channel_id=1, source_target_pairs={{0,16},{1,17},{2,18},{3,19},{4,20},{5,21},{6,22},{7,23},{8,24},{9,... | collective-permute-start | bytes 737288 | tf_op jit(solution)/shard_map/ppermute | solution.py:33
  431.6 20.0 %collective-permute-start.61 = (bf16[320,384]{1,0:T(8,128)(2,1)S(1)}, bf16[320,384]{1,0:T(8,128)(2,1)S(1)}, u32[]{:S(2)}, u32[]{:S(2)}) collective-permute-start(bf16[320,384]{1,0:T(8,128)(2,1)S(1)} %get-tuple-element.218), channel_id=1, source_target_pairs={{0,16},{1,17},{2,18},{3,19},{4,20},{5,21},{6,22},{7,23},{8,24},{9,... | collective-permute-start | bytes 737288 | tf_op jit(solution)/shard_map/ppermute | solution.py:33
  434.6 38.1 %collective-permute-start.76 = (bf16[4,128,768]{2,1,0:T(8,128)(2,1)}, bf16[4,128,768]{2,1,0:T(8,128)(2,1)}, u32[]{:S(2)}, u32[]{:S(2)}) collective-permute-start(bf16[4,128,768]{2,1,0:T(8,128)(2,1)} %pad_maximum_fusion.38), channel_id=1, source_target_pairs={{0,4},{1,5},{2,6},{3,7},{4,0},{5,1},{6,2},{7,3},{8,12},{9,13},{10,... | collective-permute-start | bytes 2359304 | tf_op jit(solution)/shard_map/ppermute | solution.py:33
  519.0 17.3 %collective-permute-start.85 = (bf16[320,384]{1,0:T(8,128)(2,1)S(1)}, bf16[320,384]{1,0:T(8,128)(2,1)S(1)}, u32[]{:S(2)}, u32[]{:S(2)}) collective-permute-start(bf16[320,384]{1,0:T(8,128)(2,1)S(1)} %get-tuple-element.205), channel_id=1, source_target_pairs={{0,16},{1,17},{2,18},{3,19},{4,20},{5,21},{6,22},{7,23},{8,24},{9,... | collective-permute-start | bytes 737288 | tf_op jit(solution)/shard_map/ppermute | solution.py:33
  519.8 21.2 %collective-permute-start.83 = (bf16[320,384]{1,0:T(8,128)(2,1)S(1)}, bf16[320,384]{1,0:T(8,128)(2,1)S(1)}, u32[]{:S(2)}, u32[]{:S(2)}) collective-permute-start(bf16[320,384]{1,0:T(8,128)(2,1)S(1)} %get-tuple-element.206), channel_id=1, source_target_pairs={{0,16},{1,17},{2,18},{3,19},{4,20},{5,21},{6,22},{7,23},{8,24},{9,... | collective-permute-start | bytes 737288 | tf_op jit(solution)/shard_map/ppermute | solution.py:33
  521.2 21.9 %collective-permute-start.70 = (bf16[128,768]{1,0:T(8,128)(2,1)S(1)}, bf16[128,768]{1,0:T(8,128)(2,1)S(1)}, u32[]{:S(2)}, u32[]{:S(2)}) collective-permute-start(bf16[128,768]{1,0:T(8,128)(2,1)S(1)} %get-tuple-element.252), channel_id=1, source_target_pairs={{0,3},{1,2},{2,1},{3,0},{4,7},{5,6},{6,5},{7,4},{8,11},{9,10},{10,... | collective-permute-start | bytes 589832 | tf_op jit(solution)/shard_map/ppermute | solution.py:33
  525.7 19.1 %collective-permute-start.69 = (bf16[128,768]{1,0:T(8,128)(2,1)S(1)}, bf16[128,768]{1,0:T(8,128)(2,1)S(1)}, u32[]{:S(2)}, u32[]{:S(2)}) collective-permute-start(bf16[128,768]{1,0:T(8,128)(2,1)S(1)} %get-tuple-element.253), channel_id=1, source_target_pairs={{0,2},{1,3},{2,0},{3,1},{4,6},{5,7},{6,4},{7,5},{8,10},{9,11},{10,... | collective-permute-start | bytes 589832 | tf_op jit(solution)/shard_map/ppermute | solution.py:33
  606.4 19.5 %collective-permute-start.91 = (bf16[1024,384]{1,0:T(8,128)(2,1)S(1)}, bf16[1024,384]{1,0:T(8,128)(2,1)S(1)}, u32[]{:S(2)}, u32[]{:S(2)}) collective-permute-start(bf16[1024,384]{1,0:T(8,128)(2,1)S(1)} %add_convert_fusion.8), channel_id=1, source_target_pairs={{0,16},{1,17},{2,18},{3,19},{4,20},{5,21},{6,22},{7,23},{8,24},{9,... | collective-permute-start | bytes 2359304 | tf_op jit(solution)/shard_map/ppermute | solution.py:33
  607.3 19.7 %collective-permute-start.144 = (bf16[384,768]{1,0:T(8,128)(2,1)S(1)}, bf16[384,768]{1,0:T(8,128)(2,1)S(1)}, u32[]{:S(2)}, u32[]{:S(2)}) collective-permute-start(bf16[384,768]{1,0:T(8,128)(2,1)S(1)} %get-tuple-element.169), channel_id=1, source_target_pairs={{0,0},{1,4},{2,1},{3,5},{4,2},{5,6},{6,3},{7,7},{8,8},{9,12},{10,9... | collective-permute-start | bytes 1769480 | tf_op jit(solution)/shard_map/ppermute | solution.py:33
  608.0 31.2 %collective-permute-start.145 = (bf16[384,768]{1,0:T(8,128)(2,1)S(1)}, bf16[384,768]{1,0:T(8,128)(2,1)S(1)}, u32[]{:S(2)}, u32[]{:S(2)}) collective-permute-start(bf16[384,768]{1,0:T(8,128)(2,1)S(1)} %get-tuple-element.170), channel_id=1, source_target_pairs={{0,1},{1,5},{2,0},{3,4},{4,3},{5,7},{6,2},{7,6},{8,9},{9,13},{10,8... | collective-permute-start | bytes 1769480 | tf_op jit(solution)/shard_map/ppermute | solution.py:33
  613.9 64.2 %collective-permute-start.138 = (bf16[768,384]{1,0:T(8,128)(2,1)}, bf16[768,384]{1,0:T(8,128)(2,1)}, u32[]{:S(2)}, u32[]{:S(2)}) collective-permute-start(bf16[768,384]{1,0:T(8,128)(2,1)} %get-tuple-element.173), channel_id=1, source_target_pairs={{0,0},{1,4},{2,1},{3,5},{4,2},{5,6},{6,3},{7,7},{8,8},{9,12},{10,9... | collective-permute-start | bytes 1769480 | tf_op jit(solution)/shard_map/ppermute | solution.py:33
  619.9 58.6 %collective-permute-start.139 = (bf16[768,384]{1,0:T(8,128)(2,1)}, bf16[768,384]{1,0:T(8,128)(2,1)}, u32[]{:S(2)}, u32[]{:S(2)}) collective-permute-start(bf16[768,384]{1,0:T(8,128)(2,1)} %get-tuple-element.174), channel_id=1, source_target_pairs={{0,1},{1,5},{2,0},{3,4},{4,3},{5,7},{6,2},{7,6},{8,9},{9,13},{10,8... | collective-permute-start | bytes 1769480 | tf_op jit(solution)/shard_map/ppermute | solution.py:33
  627.0 22.0 %collective-permute-start.92 = (bf16[1024,384]{1,0:T(8,128)(2,1)}, bf16[1024,384]{1,0:T(8,128)(2,1)}, u32[]{:S(2)}, u32[]{:S(2)}) collective-permute-start(bf16[1024,384]{1,0:T(8,128)(2,1)} %add_convert_fusion.7), channel_id=1, source_target_pairs={{0,4},{1,5},{2,6},{3,7},{4,0},{5,1},{6,2},{7,3},{8,12},{9,13},{10,... | collective-permute-start | bytes 2359304 | tf_op jit(solution)/shard_map/ppermute | solution.py:33
  658.4 16.8 %collective-permute-start.93 = (bf16[320,384]{1,0:T(8,128)(2,1)}, bf16[320,384]{1,0:T(8,128)(2,1)}, u32[]{:S(2)}, u32[]{:S(2)}) collective-permute-start(bf16[320,384]{1,0:T(8,128)(2,1)} %get-tuple-element.198), channel_id=1, source_target_pairs={{0,1},{1,0},{2,3},{3,2},{4,5},{5,4},{6,7},{7,6},{8,9},{9,8},{10,11... | collective-permute-start | bytes 737288 | tf_op jit(solution)/shard_map/ppermute | solution.py:33
  670.5 18.3 %collective-permute-start.124 = (bf16[96,768]{0,1:T(8,128)(2,1)S(1)}, bf16[96,768]{0,1:T(8,128)(2,1)S(1)}, u32[]{:S(2)}, u32[]{:S(2)}) collective-permute-start(bf16[96,768]{0,1:T(8,128)(2,1)S(1)} %bitcast.451), channel_id=1, source_target_pairs={{0,3},{1,2},{2,1},{3,0},{4,7},{5,6},{6,5},{7,4},{8,11},{9,10},{10,... | collective-permute-start | bytes 442376 | tf_op jit(solution)/shard_map/ppermute | solution.py:33
  675.3 23.1 %collective-permute-start.125 = (bf16[96,768]{0,1:T(8,128)(2,1)S(1)}, bf16[96,768]{0,1:T(8,128)(2,1)S(1)}, u32[]{:S(2)}, u32[]{:S(2)}) collective-permute-start(bf16[96,768]{0,1:T(8,128)(2,1)S(1)} %bitcast.449), channel_id=1, source_target_pairs={{0,8},{1,9},{2,10},{3,11},{4,12},{5,13},{6,14},{7,15},{8,0},{9,1},... | collective-permute-start | bytes 442376 | tf_op jit(solution)/shard_map/ppermute | solution.py:33
  678.1 22.5 %collective-permute-start.126 = (bf16[96,768]{0,1:T(8,128)(2,1)S(1)}, bf16[96,768]{0,1:T(8,128)(2,1)S(1)}, u32[]{:S(2)}, u32[]{:S(2)}) collective-permute-start(bf16[96,768]{0,1:T(8,128)(2,1)S(1)} %bitcast.446), channel_id=1, source_target_pairs={{0,9},{1,8},{2,11},{3,10},{4,13},{5,12},{6,15},{7,14},{8,1},{9,0},... | collective-permute-start | bytes 442376 | tf_op jit(solution)/shard_map/ppermute | solution.py:33
  678.5 24.1 %collective-permute-start.127 = (bf16[96,768]{0,1:T(8,128)(2,1)S(1)}, bf16[96,768]{0,1:T(8,128)(2,1)S(1)}, u32[]{:S(2)}, u32[]{:S(2)}) collective-permute-start(bf16[96,768]{0,1:T(8,128)(2,1)S(1)} %bitcast.444), channel_id=1, source_target_pairs={{0,10},{1,11},{2,8},{3,9},{4,14},{5,15},{6,12},{7,13},{8,2},{9,3},... | collective-permute-start | bytes 442376 | tf_op jit(solution)/shard_map/ppermute | solution.py:33
  686.0 16.6 %collective-permute-start.128 = (bf16[96,768]{0,1:T(8,128)(2,1)S(1)}, bf16[96,768]{0,1:T(8,128)(2,1)S(1)}, u32[]{:S(2)}, u32[]{:S(2)}) collective-permute-start(bf16[96,768]{0,1:T(8,128)(2,1)S(1)} %bitcast.443), channel_id=1, source_target_pairs={{0,11},{1,10},{2,9},{3,8},{4,15},{5,14},{6,13},{7,12},{8,3},{9,2},... | collective-permute-start | bytes 442376 | tf_op jit(solution)/shard_map/ppermute | solution.py:33
  688.8 17.3 %collective-permute-start.122 = (bf16[96,768]{0,1:T(8,128)(2,1)S(1)}, bf16[96,768]{0,1:T(8,128)(2,1)S(1)}, u32[]{:S(2)}, u32[]{:S(2)}) collective-permute-start(bf16[96,768]{0,1:T(8,128)(2,1)S(1)} %bitcast.442), channel_id=1, source_target_pairs={{0,1},{1,0},{2,3},{3,2},{4,5},{5,4},{6,7},{7,6},{8,9},{9,8},{10,11... | collective-permute-start | bytes 442376 | tf_op jit(solution)/shard_map/ppermute | solution.py:33
  698.4 26.3 %collective-permute-start.96 = (bf16[1280,384]{1,0:T(8,128)(2,1)}, bf16[1280,384]{1,0:T(8,128)(2,1)}, u32[]{:S(2)}, u32[]{:S(2)}) collective-permute-start(bf16[1280,384]{1,0:T(8,128)(2,1)} %pad_maximum_fusion.28), channel_id=1, source_target_pairs={{0,4},{1,5},{2,6},{3,7},{4,0},{5,1},{6,2},{7,3},{8,12},{9,13},{10,... | collective-permute-start | bytes 2949128 | tf_op jit(solution)/shard_map/ppermute | solution.py:33
  735.6 46.7 %collective-permute-start.142 = (bf16[384,768]{1,0:T(8,128)(2,1)}, bf16[384,768]{1,0:T(8,128)(2,1)}, u32[]{:S(2)}, u32[]{:S(2)}) collective-permute-start(bf16[384,768]{1,0:T(8,128)(2,1)} %get-tuple-element.167), channel_id=1, source_target_pairs={{0,0},{1,4},{2,1},{3,5},{4,2},{5,6},{6,3},{7,7},{8,8},{9,12},{10,9... | collective-permute-start | bytes 1769480 | tf_op jit(solution)/shard_map/ppermute | solution.py:33
  746.6 17.0 %collective-permute-start.99 = (bf16[320,384]{1,0:T(8,128)(2,1)S(1)}, bf16[320,384]{1,0:T(8,128)(2,1)S(1)}, u32[]{:S(2)}, u32[]{:S(2)}) collective-permute-start(bf16[320,384]{1,0:T(8,128)(2,1)S(1)} %get-tuple-element.194), channel_id=1, source_target_pairs={{0,16},{1,17},{2,18},{3,19},{4,20},{5,21},{6,22},{7,23},{8,24},{9,... | collective-permute-start | bytes 737288 | tf_op jit(solution)/shard_map/ppermute | solution.py:33
  751.4 35.4 %collective-permute-start.143 = (bf16[384,768]{1,0:T(8,128)(2,1)}, bf16[384,768]{1,0:T(8,128)(2,1)}, u32[]{:S(2)}, u32[]{:S(2)}) collective-permute-start(bf16[384,768]{1,0:T(8,128)(2,1)} %get-tuple-element.168), channel_id=1, source_target_pairs={{0,1},{1,5},{2,0},{3,4},{4,3},{5,7},{6,2},{7,6},{8,9},{9,13},{10,8... | collective-permute-start | bytes 1769480 | tf_op jit(solution)/shard_map/ppermute | solution.py:33
  772.9 18.3 %collective-permute-start.136 = (bf16[768,384]{1,0:T(8,128)(2,1)}, bf16[768,384]{1,0:T(8,128)(2,1)}, u32[]{:S(2)}, u32[]{:S(2)}) collective-permute-start(bf16[768,384]{1,0:T(8,128)(2,1)} %get-tuple-element.171), channel_id=1, source_target_pairs={{0,0},{1,4},{2,1},{3,5},{4,2},{5,6},{6,3},{7,7},{8,8},{9,12},{10,9... | collective-permute-start | bytes 1769480 | tf_op jit(solution)/shard_map/ppermute | solution.py:33
  778.8 23.5 %collective-permute-start.137 = (bf16[768,384]{1,0:T(8,128)(2,1)}, bf16[768,384]{1,0:T(8,128)(2,1)}, u32[]{:S(2)}, u32[]{:S(2)}) collective-permute-start(bf16[768,384]{1,0:T(8,128)(2,1)} %get-tuple-element.172), channel_id=1, source_target_pairs={{0,1},{1,5},{2,0},{3,4},{4,3},{5,7},{6,2},{7,6},{8,9},{9,13},{10,8... | collective-permute-start | bytes 1769480 | tf_op jit(solution)/shard_map/ppermute | solution.py:33
  781.5 24.7 %collective-permute-start.105 = (bf16[1024,384]{1,0:T(8,128)(2,1)}, bf16[1024,384]{1,0:T(8,128)(2,1)}, u32[]{:S(2)}, u32[]{:S(2)}) collective-permute-start(bf16[1024,384]{1,0:T(8,128)(2,1)} %fusion.79), channel_id=1, source_target_pairs={{0,4},{1,5},{2,6},{3,7},{4,0},{5,1},{6,2},{7,3},{8,12},{9,13},{10,... | collective-permute-start | bytes 2359304 | tf_op jit(solution)/shard_map/ppermute | solution.py:33
  782.3 59.6 %collective-permute-start.147 = (bf16[384,768]{1,0:T(8,128)(2,1)}, bf16[384,768]{1,0:T(8,128)(2,1)}, u32[]{:S(2)}, u32[]{:S(2)}) collective-permute-start(bf16[384,768]{1,0:T(8,128)(2,1)} %fusion.97), channel_id=1, source_target_pairs={{0,16},{1,17},{2,18},{3,19},{4,20},{5,21},{6,22},{7,23},{8,24},{9,... | collective-permute-start | bytes 1769480 | tf_op jit(solution)/shard_map/ppermute | solution.py:33
  786.8 59.8 %collective-permute-start.141 = (bf16[768,384]{1,0:T(8,128)(2,1)}, bf16[768,384]{1,0:T(8,128)(2,1)}, u32[]{:S(2)}, u32[]{:S(2)}) collective-permute-start(bf16[768,384]{1,0:T(8,128)(2,1)} %fusion.92), channel_id=1, source_target_pairs={{0,16},{1,17},{2,18},{3,19},{4,20},{5,21},{6,22},{7,23},{8,24},{9,... | collective-permute-start | bytes 1769480 | tf_op jit(solution)/shard_map/ppermute | solution.py:33
  791.1 50.8 %collective-permute-start.146 = (bf16[384,768]{1,0:T(8,128)(2,1)}, bf16[384,768]{1,0:T(8,128)(2,1)}, u32[]{:S(2)}, u32[]{:S(2)}) collective-permute-start(bf16[384,768]{1,0:T(8,128)(2,1)} %fusion.95), channel_id=1, source_target_pairs={{16,0},{17,1},{18,2},{19,3},{20,4},{21,5},{22,6},{23,7},{24,8},{25... | collective-permute-start | bytes 1769480 | tf_op jit(solution)/shard_map/ppermute | solution.py:33
  804.6 42.0 %collective-permute-start.140 = (bf16[768,384]{1,0:T(8,128)(2,1)}, bf16[768,384]{1,0:T(8,128)(2,1)}, u32[]{:S(2)}, u32[]{:S(2)}) collective-permute-start(bf16[768,384]{1,0:T(8,128)(2,1)} %fusion.90), channel_id=1, source_target_pairs={{16,0},{17,1},{18,2},{19,3},{20,4},{21,5},{22,6},{23,7},{24,8},{25... | collective-permute-start | bytes 1769480 | tf_op jit(solution)/shard_map/ppermute | solution.py:33
  855.0 21.0 %collective-permute-start.107 = (bf16[1024,384]{1,0:T(8,128)(2,1)}, bf16[1024,384]{1,0:T(8,128)(2,1)}, u32[]{:S(2)}, u32[]{:S(2)}) collective-permute-start(bf16[1024,384]{1,0:T(8,128)(2,1)} %add_convert_fusion.6), channel_id=1, source_target_pairs={{0,16},{1,17},{2,18},{3,19},{4,20},{5,21},{6,22},{7,23},{8,24},{9,... | collective-permute-start | bytes 2359304 | tf_op jit(solution)/shard_map/ppermute | solution.py:33
  866.9 17.1 %collective-permute-start.115 = (bf16[96,768]{0,1:T(8,128)(2,1)S(1)}, bf16[96,768]{0,1:T(8,128)(2,1)S(1)}, u32[]{:S(2)}, u32[]{:S(2)}) collective-permute-start(bf16[96,768]{0,1:T(8,128)(2,1)S(1)} %bitcast.454), channel_id=1, source_target_pairs={{0,3},{1,2},{2,1},{3,0},{4,7},{5,6},{6,5},{7,4},{8,11},{9,10},{10,... | collective-permute-start | bytes 442376 | tf_op jit(solution)/shard_map/ppermute | solution.py:33
  867.0 26.2 %collective-permute-start.116 = (bf16[96,768]{0,1:T(8,128)(2,1)S(1)}, bf16[96,768]{0,1:T(8,128)(2,1)S(1)}, u32[]{:S(2)}, u32[]{:S(2)}) collective-permute-start(bf16[96,768]{0,1:T(8,128)(2,1)S(1)} %bitcast.452), channel_id=1, source_target_pairs={{0,8},{1,9},{2,10},{3,11},{4,12},{5,13},{6,14},{7,15},{8,0},{9,1},... | collective-permute-start | bytes 442376 | tf_op jit(solution)/shard_map/ppermute | solution.py:33
  868.1 26.8 %collective-permute-start.117 = (bf16[96,768]{0,1:T(8,128)(2,1)S(1)}, bf16[96,768]{0,1:T(8,128)(2,1)S(1)}, u32[]{:S(2)}, u32[]{:S(2)}) collective-permute-start(bf16[96,768]{0,1:T(8,128)(2,1)S(1)} %bitcast.450), channel_id=1, source_target_pairs={{0,9},{1,8},{2,11},{3,10},{4,13},{5,12},{6,15},{7,14},{8,1},{9,0},... | collective-permute-start | bytes 442376 | tf_op jit(solution)/shard_map/ppermute | solution.py:33
  875.9 21.3 %collective-permute-start.118 = (bf16[96,768]{0,1:T(8,128)(2,1)S(1)}, bf16[96,768]{0,1:T(8,128)(2,1)S(1)}, u32[]{:S(2)}, u32[]{:S(2)}) collective-permute-start(bf16[96,768]{0,1:T(8,128)(2,1)S(1)} %bitcast.448), channel_id=1, source_target_pairs={{0,10},{1,11},{2,8},{3,9},{4,14},{5,15},{6,12},{7,13},{8,2},{9,3},... | collective-permute-start | bytes 442376 | tf_op jit(solution)/shard_map/ppermute | solution.py:33
  880.9 16.4 %collective-permute-start.119 = (bf16[96,768]{0,1:T(8,128)(2,1)S(1)}, bf16[96,768]{0,1:T(8,128)(2,1)S(1)}, u32[]{:S(2)}, u32[]{:S(2)}) collective-permute-start(bf16[96,768]{0,1:T(8,128)(2,1)S(1)} %bitcast.447), channel_id=1, source_target_pairs={{0,11},{1,10},{2,9},{3,8},{4,15},{5,14},{6,13},{7,12},{8,3},{9,2},... | collective-permute-start | bytes 442376 | tf_op jit(solution)/shard_map/ppermute | solution.py:33
  884.0 16.9 %collective-permute-start.113 = (bf16[96,768]{0,1:T(8,128)(2,1)S(1)}, bf16[96,768]{0,1:T(8,128)(2,1)S(1)}, u32[]{:S(2)}, u32[]{:S(2)}) collective-permute-start(bf16[96,768]{0,1:T(8,128)(2,1)S(1)} %bitcast.445), channel_id=1, source_target_pairs={{0,1},{1,0},{2,3},{3,2},{4,5},{5,4},{6,7},{7,6},{8,9},{9,8},{10,11... | collective-permute-start | bytes 442376 | tf_op jit(solution)/shard_map/ppermute | solution.py:33
  893.2 21.1 %collective-permute-start.108 = (bf16[1024,384]{1,0:T(8,128)(2,1)S(1)}, bf16[1024,384]{1,0:T(8,128)(2,1)}, u32[]{:S(2)}, u32[]{:S(2)}) collective-permute-start(bf16[1024,384]{1,0:T(8,128)(2,1)S(1)} %add_convert_fusion.5), channel_id=1, source_target_pairs={{0,4},{1,5},{2,6},{3,7},{4,0},{5,1},{6,2},{7,3},{8,12},{9,13},{10,... | collective-permute-start | bytes 2359304 | tf_op jit(solution)/shard_map/ppermute | solution.py:33
  927.3 16.4 %collective-permute-start.110 = (bf16[128,768]{1,0:T(8,128)(2,1)S(1)}, bf16[128,768]{1,0:T(8,128)(2,1)S(1)}, u32[]{:S(2)}, u32[]{:S(2)}) collective-permute-start(bf16[128,768]{1,0:T(8,128)(2,1)S(1)} %get-tuple-element.245), channel_id=1, source_target_pairs={{0,2},{1,3},{2,0},{3,1},{4,6},{5,7},{6,4},{7,5},{8,10},{9,11},{10,... | collective-permute-start | bytes 589832 | tf_op jit(solution)/shard_map/ppermute | solution.py:33
  (273 other events, 2886.7 us)

commit v2 on v1

v2 whole, which is shorter than its diff:
```python
import functools

import jax
import jax.numpy as jnp
from jax import lax
from jax.experimental import pallas as pl
from jax.experimental.pallas import tpu as pltpu
from jax.sharding import PartitionSpec as P

HEAD_DIM = 64
EPSILON = 1e-06
MASKED = -1000000000.0
AXES = ("section", "dp", "tensor")
BLOCK = 128
DIRECT = 8
LONG = 10**11
BF16 = jnp.bfloat16
F32 = jnp.float32


def send(value, to):
    sections, width, depth = (lax.axis_size(name) for name in AXES)

    def number(x, h, c, t):
        return (x * width + 2 * h + c) * depth + t

    pairs = []
    for x in range(sections):
        for d in range(width):
            for t in range(depth):
                target = to(x, d // 2, d % 2, t)
                if target is not None:
                    pairs.append((number(x, d // 2, d % 2, t), number(*target)))
    return lax.ppermute(value, AXES, pairs)


def core_swap(value):
    return send(value, lambda x, h, c, t: (x, h, 1 - c, t))


def section_swap(value):
    return send(value, lambda x, h, c, t: (1 - x, h, c, t))


def tensor_swap(value, j):
    return send(value, lambda x, h, c, t: (x, h, c, t ^ j))


def host_swap(value, j):
    return send(value, lambda x, h, c, t: (x, h ^ j, c, t))


def expert_swap(value, j):
    def to(x, h, c, t):
        e = (2 * h + (t & 1)) ^ j
        return (x, e >> 1, c, (t & 2) | (e & 1))

    return send(value, to)


def expert_exchange(values):
    count, bit = values.shape[0], 1
    while bit < count:
        parts = values.reshape(count // (2 * bit), 2, bit, *values.shape[1:])
        other = expert_swap(parts[:, 1], bit)
        values = jnp.stack([parts[:, 0], other], 1).reshape(values.shape)
        bit *= 2
    return values


def place():
    d = lax.axis_index("dp")
    return lax.axis_index("section"), d // 2, d % 2, lax.axis_index("tensor")


def ordered(flag, own, other, axis):
    first = jnp.where(flag == 0, own, other)
    second = jnp.where(flag == 0, other, own)
    return jnp.concatenate([first, second], axis)


def at(values, index):
    return lax.dynamic_index_in_dim(values, index, 0, keepdims=False)


def rows_over_hosts(value, axis):
    _, h, _, _ = place()
    bit = 1
    while bit < lax.axis_size("dp") // 2:
        other = host_swap(value, bit)
        value = ordered((h // bit) % 2, value, other, axis)
        bit *= 2
    return value


def to_groups(rows):
    _, _, _, t = place()
    got = []
    for i in range(2):

        def to(x, h, c, t, i=i):
            return (x, h, 1 - (t >> 1), 2 * c + (i ^ (t & 1)))

        got.append(send(at(rows, i ^ (t & 1)), to))
    return got + [core_swap(part) for part in got]


def piece_order():
    c, low = which_core(), lax.axis_index("tensor") & 1
    return [2 * (1 - c) + low, 2 * (1 - c) + (1 - low), 2 * c + low, 2 * c + (1 - low)]


def whole_rows(pieces):
    order = piece_order()
    return jnp.concatenate([at_place(pieces, order, place) for place in range(4)], 0)


def at_place(pieces, order, place):
    value = pieces[3]
    for piece, number in zip(pieces[:3], order[:3]):
        value = jnp.where(number == place, piece, value)
    return value


def from_groups(rows):
    _, _, c, t = place()
    length, width = rows.shape
    pieces = rows.reshape(4, length // 4, width)
    got = []
    for i in range(2):

        def to(x, h, c, t, i=i):
            return (x, h, t >> 1, 2 * (1 - c) + (i ^ (t & 1)))

        got.append(send(at(pieces, 2 * (1 - c) + (i ^ (t & 1))), to))
    low = t & 1
    return jnp.stack([jnp.where(low == 0, got[0], got[1]), jnp.where(low == 0, got[1], got[0])])


def head_lanes(width, head):
    lane = lax.broadcasted_iota(jnp.int32, (1, width), 1)
    return (lane // HEAD_DIM) == head


def dot(a, b, contract=(1, 0)):
    dims = (((contract[0],), (contract[1],)), ((), ()))
    return lax.dot_general(a, b, dims, preferred_element_type=F32)


def which_core():
    return lax.rem(lax.axis_index("dp"), 2)


def which_member():
    return lax.axis_index("section") + 2 * which_core()


def half_at(index, half):
    return pl.ds(pl.multiple_of(index * half, half), half)


def row_scale(values):
    return lax.rsqrt(jnp.mean(values * values, -1, keepdims=True) + EPSILON)


def call(kernel, inputs, outputs, grid=(1,), scratch=(), vmem=24, flops=10**9):
    def spec(item):
        value, given = item
        if given is not None:
            return given
        return pl.BlockSpec(value.shape, lambda i, n=len(value.shape): (0,) * n)

    return pl.pallas_call(
        kernel,
        grid=grid,
        in_specs=[spec(item) for item in inputs],
        out_specs=[spec(item) for item in outputs],
        out_shape=[item[0] for item in outputs],
        scratch_shapes=list(scratch),
        cost_estimate=pl.CostEstimate(flops=flops, bytes_accessed=1000, transcendentals=0),
        compiler_params=pltpu.CompilerParams(vmem_limit_bytes=vmem * 2**20),
    )(*[item[0] for item in inputs])


def shape_of(*dims, dtype=BF16):
    return jax.ShapeDtypeStruct(dims, dtype)


SMEM = pl.BlockSpec(memory_space=pltpu.SMEM)


def attend_kernel(heads, mix, parts, *refs):
    if mix:
        middle_ref, gate_ref, own_ref, other_ref, *refs = refs
    else:
        row_refs, refs = refs[:4], refs[4:]
    part_refs, refs = refs[:parts], refs[parts:]
    prefix_ref, gain_ref, base_ref, x_ref, normed_ref, qkv_ref, w_ref, *refs = refs
    o_ref, a_ref, strip, causal, scores_ref = refs
    block = pl.program_id(0)
    length, width = x_ref.shape
    rows = o_ref.shape[0]
    span = base_ref.shape[1]
    lanes_all = o_ref.shape[1]

    @pl.when(block == 0)
    def _():
        step = 256
        for j, ref in enumerate(part_refs):
            count = ref.shape[1]
            first = (lax.axis_index("dp") ^ j) * count if parts > 1 else 0
            first = pl.multiple_of(first, 8) if parts > 1 else 0
            for v in range(3):
                w_ref[v, pl.ds(first, count), :] = ref[v]
        if not mix:
            for ref, piece in zip(row_refs, piece_order()):
                count = ref.shape[0]
                x_ref[pl.ds(pl.multiple_of(piece * count, count), count), :] = ref[...]
        for at_row in range(0, length, step):
            part = pl.ds(at_row, step)
            if mix:
                half = width // 2
                core = which_core()
                for ref, side in ((own_ref, core), (other_ref, 1 - core)):
                    lanes = half_at(side, half)
                    value = middle_ref[part, lanes] + gate_ref[part, :] * ref[part, :].astype(F32)
                    x_ref[part, lanes] = value.astype(BF16)
            values = x_ref[part, :].astype(F32)
            normed = (values * row_scale(values) * gain_ref[...]).astype(BF16)
            normed_ref[part, :] = normed
            for v in range(3):
                qkv_ref[v, part, :] = dot(normed, w_ref[v]).astype(BF16)
        sub = lax.broadcasted_iota(jnp.int32, (8, span), 0)
        for head in range(heads):
            part = jnp.broadcast_to(base_ref[head : head + 1, :], (8, span))
            for bit in (1, 2, 4):
                part = jnp.where((sub & bit) != 0, pltpu.roll(part, bit, 1), part)
            size = 8
            while size < rows:
                part = jnp.concatenate([part, pltpu.roll(part, size, 1)], 0)
                size *= 2
            strip[head] = part
            ahead = lax.broadcasted_iota(jnp.int32, (rows, span), 1) - lax.broadcasted_iota(
                jnp.int32, (rows, span), 0
            )
            causal[head] = jnp.where(ahead > length - rows, MASKED, part)

    start = pl.multiple_of((length // rows - 1 - block) * rows, rows)
    here = pl.ds(pl.multiple_of(block * rows, rows), rows)
    col = lax.broadcasted_iota(jnp.int32, (1, length), 1)
    inside = col < prefix_ref[0]
    queries, keys, values = qkv_ref[0, here, :], qkv_ref[1], qkv_ref[2]
    queries = queries * jnp.asarray(HEAD_DIM ** (-0.5), BF16)
    step = 32
    for head in range(heads):
        own = jnp.where(head_lanes(lanes_all, head), queries, jnp.zeros_like(queries))
        scores_ref[head] = dot(own, keys, (1, 1))
    out = jnp.zeros((rows, lanes_all), F32)
    for head in range(heads):
        for at_row in range(0, rows, step):
            part = pl.ds(at_row, step)
            across = pl.ds(start, length)
            bias = jnp.where(inside, strip[head, part, across], causal[head, part, across])
            scores = scores_ref[head, part, :] + bias
            weights = jnp.exp(scores - jnp.max(scores, -1, keepdims=True))
            weights = weights * (1.0 / jnp.sum(weights, -1, keepdims=True))
            a_ref[head, part, :] = weights.astype(BF16)
        out = jnp.where(head_lanes(lanes_all, head), dot(a_ref[head], values), out)
    o_ref[...] = out.astype(BF16)


def attend(source, mix, prefix, gain, weights, base):
    width = gain.shape[1]
    length = source[0].shape[0] * (1 if mix else 4)
    lanes = weights[0].shape[2]
    heads = lanes // HEAD_DIM
    span = base.shape[1]
    inputs = [(part, None) for part in (*source, *weights)]
    inputs += [(prefix, SMEM), (gain, None), (base, None)]
    return call(
        functools.partial(attend_kernel, heads, mix, len(weights)),
        inputs,
        [
            (shape_of(length, width), None),
            (shape_of(length, width), None),
            (shape_of(3, length, lanes), None),
            (shape_of(3, width, lanes), None),
            (shape_of(length, lanes), pl.BlockSpec((BLOCK, lanes), lambda i: (i, 0))),
            (
                shape_of(heads, length, length),
                pl.BlockSpec((heads, BLOCK, length), lambda i: (0, i, 0)),
            ),
        ],
        grid=(length // BLOCK,),
        scratch=[
            pltpu.VMEM((heads, BLOCK, span), F32),
            pltpu.VMEM((heads, BLOCK, span), F32),
            pltpu.VMEM((heads, BLOCK, length), F32),
        ],
        vmem=58,
        flops=LONG,
    )


def pieces_of(experts):
    return experts if experts <= DIRECT else 1


def selection_block(slot_ref, first, count):
    ids = first + lax.broadcasted_iota(jnp.int32, (count, slot_ref.shape[1]), 0)
    return jnp.where(ids == slot_ref[...], 1.0, 0.0).astype(BF16)


def dispatch_blocks(step, steps, slot_ref, rows_ref, buffer_refs):
    half = rows_ref.shape[1] // 2
    total = sum(ref.shape[0] for ref in buffer_refs) if len(buffer_refs) > 1 else None
    lanes = half_at(which_core(), half)
    if total is None:

        @pl.when(step >= steps)
        def _():
            count = buffer_refs[0].shape[0]
            chosen = selection_block(slot_ref, (step - steps) * count, count)
            buffer_refs[0][...] = dot(chosen, rows_ref[:, lanes]).astype(BF16)

        return
    first = 0
    for index, ref in enumerate(buffer_refs):

        @pl.when(step == steps + index)
        def _(ref=ref, first=first):
            chosen = selection_block(slot_ref, first, ref.shape[0])
            ref[...] = dot(chosen, rows_ref[:, lanes]).astype(BF16)

        first += ref.shape[0]


def buffer_outputs(experts, rows, half, steps):
    count = pieces_of(experts)
    if count > 1:
        return [(shape_of(rows // count, half), None)] * count, steps + count
    blocks = 4
    spec = pl.BlockSpec((rows // blocks, half), lambda i: (jnp.maximum(i - steps, 0), 0))
    return [(shape_of(rows, half), spec)], steps + blocks


def router_probs(normed, router_ref, experts):
    logits = dot(normed, router_ref[...])
    real = lax.broadcasted_iota(jnp.int32, logits.shape, 1) < experts
    logits = jnp.where(real, logits, MASKED)
    weights = jnp.exp(logits - jnp.max(logits, -1, keepdims=True))
    weights = jnp.where(real, weights, 0.0)
    return weights / jnp.sum(weights, -1, keepdims=True)


def middle_kernel(experts, steps, *refs):
    x_ref, *refs = refs
    piece_refs, refs = refs[:4], refs[4:]
    w_ref, gain_ref, router_ref, chosen_ref, slot_ref, middle_ref, normed_ref, gate_ref = refs[:8]
    buffer_refs, kept = refs[8:-1], refs[-1]
    step = pl.program_id(0)
    rows = x_ref.shape[0]

    @pl.when(step < steps)
    def _():
        member = which_member()
        parts = [dot(ref[...], w_ref[member ^ j], (1, 1)) for j, ref in enumerate(piece_refs)]
        values = x_ref[...].astype(F32) + ((parts[0] + parts[1]) + (parts[2] + parts[3]))
        middle_ref[...] = values
        normed = (values * row_scale(values) * gain_ref[...]).astype(BF16)
        normed_ref[...] = normed
        kept[pl.ds(pl.multiple_of(step * rows, rows), rows), :] = normed
        probs = router_probs(normed, router_ref, experts)
        gate_ref[...] = jnp.sum(probs * chosen_ref[...], -1, keepdims=True)

    dispatch_blocks(step, steps, slot_ref, kept, buffer_refs)


def middle_and_buffers(rows, pieces, weights, gain, router, chosen, slot, experts, slots):
    length, width = rows.shape
    steps = 4
    block = length // steps

    def by_rows(lanes):
        return pl.BlockSpec((block, lanes), lambda i: (jnp.minimum(i, steps - 1), 0))

    buffers, grid = buffer_outputs(experts, slots, width // 2, steps)
    lanes = pieces[0].shape[1]
    got = call(
        functools.partial(middle_kernel, experts, steps),
        [(rows, by_rows(width))]
        + [(piece, by_rows(lanes)) for piece in pieces]
        + [
            (weights, None),
            (gain, None),
            (router, None),
            (chosen, by_rows(chosen.shape[1])),
            (slot, None),
        ],
        [
            (shape_of(length, width, dtype=F32), by_rows(width)),
            (shape_of(length, width), by_rows(width)),
            (shape_of(length, 1, dtype=F32), by_rows(1)),
        ]
        + buffers,
        grid=(grid,),
        scratch=[pltpu.VMEM((length, width), BF16)],
    )
    return got[0], got[1], got[2], got[3:]


def order_of(index, count):
    return (index + count // 2) % count


def parts_of(refs, index, count):
    return refs[:2] if index >= count // 2 or count == 1 else refs[2:]


def part_outputs(rows, half, count):
    if count == 1:
        return [(shape_of(rows, half), None)] * 2
    split = count // 2
    shape = shape_of(rows * split, half)
    upper = pl.BlockSpec((rows, half), lambda i: (jnp.minimum(i, split - 1), 0))
    lower = pl.BlockSpec((rows, half), lambda i: (jnp.maximum(i - split, 0), 0))
    return [(shape, upper)] * 2 + [(shape, lower)] * 2


def ordered_blocks(rows, lanes, count):
    return pl.BlockSpec((rows, lanes), lambda i: ((i + count // 2) % count, 0))


GELU = 0.7978845608028654


def expert_kernel(count, *refs):
    own_refs, other_refs, refs = refs[:count], refs[count : 2 * count], refs[2 * count :]
    *pack_refs, active_ref, slope_ref = refs[:4]
    part_refs = refs[4:]
    half = own_refs[0].shape[1]
    upper, lower = pl.ds(0, half), pl.ds(half, half)
    core = which_core()
    step = pl.program_id(0)
    for index in range(count):
        keep_ref, give_ref = parts_of(part_refs, index, count)

        @pl.when(step == order_of(index, count))
        def _(index=index, keep_ref=keep_ref, give_ref=give_ref):
            mine, others = half_at(core, half), half_at(1 - core, half)
            own, other = own_refs[index][...], other_refs[index][...]
            keep = give = None
            for i, ref in enumerate(pack_refs):
                hidden = dot(own, ref[upper, mine]) + dot(other, ref[upper, others])
                square = hidden * hidden
                inner = jnp.tanh(GELU * hidden * (1.0 + 0.044715 * square))
                active = (0.5 * hidden * (1.0 + inner)).astype(BF16)
                slope = 0.5 * (1.0 + inner) + 0.5 * hidden * (1.0 - inner * inner) * (
                    GELU * (1.0 + 3 * 0.044715 * square)
                )
                active_ref[:, pl.ds(i * half, half)] = active
                slope_ref[:, pl.ds(i * half, half)] = slope.astype(BF16)
                first, second = dot(active, ref[lower, mine]), dot(active, ref[lower, others])
                keep = first if keep is None else keep + first
                give = second if give is None else give + second
            keep_ref[...] = keep.astype(BF16)
            give_ref[...] = give.astype(BF16)


def row_blocks(rows, lanes):
    return pl.BlockSpec((rows, lanes), lambda i: (i, 0))


def expert_rows(own, other, packs):
    count = len(own)
    rows, half = own[0].shape
    hidden = packs[0].shape[1]
    wide = (shape_of(rows * count, hidden), ordered_blocks(rows, hidden, count))
    got = call(
        functools.partial(expert_kernel, count),
        [(part, None) for part in own + other + packs],
        [wide, wide] + part_outputs(rows, half, count),
        grid=(count,),
    )
    return got[0], got[1], got[2:]


def expert_back_kernel(count, *refs):
    own_refs, other_refs, refs = refs[:count], refs[count : 2 * count], refs[2 * count :]
    slope_ref, *pack_refs, hidden_ref = refs[:4]
    part_refs = refs[4:]
    half = own_refs[0].shape[1]
    upper, lower = pl.ds(0, half), pl.ds(half, half)
    core = which_core()
    step = pl.program_id(0)
    for index in range(count):
        keep_ref, give_ref = parts_of(part_refs, index, count)

        @pl.when(step == order_of(index, count))
        def _(index=index, keep_ref=keep_ref, give_ref=give_ref):
            mine, others = half_at(core, half), half_at(1 - core, half)
            own, other = own_refs[index][...], other_refs[index][...]
            keep = give = None
            for i, ref in enumerate(pack_refs):
                lanes = pl.ds(i * half, half)
                grad = dot(own, ref[lower, mine], (1, 1)) + dot(other, ref[lower, others], (1, 1))
                grad = (grad * slope_ref[:, lanes].astype(F32)).astype(BF16)
                hidden_ref[:, lanes] = grad
                first = dot(grad, ref[upper, mine], (1, 1))
                second = dot(grad, ref[upper, others], (1, 1))
                keep = first if keep is None else keep + first
                give = second if give is None else give + second
            keep_ref[...] = keep.astype(BF16)
            give_ref[...] = give.astype(BF16)


def expert_rows_back(own, other, slope, packs):
    count = len(own)
    rows, half = own[0].shape
    hidden = packs[0].shape[1]
    blocks = ordered_blocks(rows, hidden, count)
    got = call(
        functools.partial(expert_back_kernel, count),
        [(part, None) for part in own + other]
        + [(slope, blocks)]
        + [(part, None) for part in packs],
        [(shape_of(rows * count, hidden), blocks)] + part_outputs(rows, half, count),
        grid=(count,),
    )
    return got[0], got[1:]


def expert_grads_kernel(count, *refs):
    own_refs, other_refs, refs = refs[:count], refs[count : 2 * count], refs[2 * count :]
    own_grads, other_grads, refs = refs[:count], refs[count : 2 * count], refs[2 * count :]
    active_ref, hidden_ref, first_ref, second_ref = refs
    rows, half = own_refs[0].shape
    core = which_core()
    for out, ref in enumerate((first_ref, second_ref)):
        own_half = pl.ds(out * half, half)
        for inputs, grads, side in (
            (own_refs, own_grads, core),
            (other_refs, other_grads, 1 - core),
        ):
            lanes = half_at(side, half)
            up = jnp.zeros((half, half), F32)
            down = jnp.zeros((half, half), F32)
            for index in range(count):
                part = pl.ds(index * rows, rows)
                up += dot(inputs[index][...], hidden_ref[part, own_half], (0, 0))
                down += dot(active_ref[part, own_half], grads[index][...], (0, 0))
            ref[pl.ds(0, half), lanes] = up.astype(BF16)
            ref[pl.ds(half, half), lanes] = down.astype(BF16)


def expert_weight_grads(own, other, own_grads, other_grads, active, hidden):
    count = len(own)
    rows, half = own[0].shape
    return call(
        functools.partial(expert_grads_kernel, count),
        [(part, None) for part in own + other + own_grads + other_grads]
        + [(active, None), (hidden, None)],
        [(shape_of(2 * half, 2 * half), None)] * 2,
        vmem=58,
    )


def combine_kernel(count, *refs):
    refs, slot_ref, out_ref = refs[:-2], refs[-2], refs[-1]
    block = out_ref.shape[0]
    total = jnp.zeros(out_ref.shape, F32)
    first = 0
    for index in range(count):
        if index == 0:
            value = (refs[0][...].astype(F32) + refs[1][...].astype(F32)).astype(BF16)
        else:
            value = refs[index + 1][...]
        ids = first + lax.broadcasted_iota(jnp.int32, (block, value.shape[0]), 1)
        chosen = jnp.where(ids == slot_ref[...], 1.0, 0.0).astype(BF16)
        total += dot(chosen, value)
        first += value.shape[0]
    out_ref[...] = total.astype(BF16)


def combine(first, rest, slot_column):
    length = slot_column.shape[0]
    half = first[0].shape[1]
    block = length // 4
    return call(
        functools.partial(combine_kernel, 1 + len(rest)),
        [(part, None) for part in first]
        + [(part, None) for part in rest]
        + [(slot_column, row_blocks(block, 1))],
        [(shape_of(length, half), row_blocks(block, half))],
        grid=(4,),
    )[0]


def grad_kernel(experts, steps, last, *refs):
    middle_ref, gate_ref, own_ref, other_ref, grad_ref, normed_ref, router_ref = refs[:7]
    chosen_ref, slot_ref, refs = refs[7], refs[8], refs[9:]
    if last:
        result_ref, *refs = refs
    logits_ref, refs = refs[0], refs[1:]
    buffer_refs, kept, joined = refs[:-2], refs[-2], refs[-1]
    step = pl.program_id(0)
    rows, width = middle_ref.shape

    @pl.when(step < steps)
    def _():
        half = width // 2
        core = which_core()
        joined[:, half_at(core, half)] = own_ref[...].astype(F32)
        joined[:, half_at(1 - core, half)] = other_ref[...].astype(F32)
        produced = joined[...]
        gate = gate_ref[...]
        if last:
            result_ref[...] = (middle_ref[...] + gate * produced).astype(BF16)
        grad = grad_ref[...].astype(F32)
        kept[pl.ds(pl.multiple_of(step * rows, rows), rows), :] = (gate * grad).astype(BF16)
        grad_gate = jnp.sum(grad * produced, -1, keepdims=True)
        probs = router_probs(normed_ref[...], router_ref, experts)
        grad_probs = chosen_ref[...] * grad_gate
        inner = jnp.sum(probs * grad_probs, -1, keepdims=True)
        logits_ref[...] = (probs * (grad_probs - inner)).astype(BF16)

    dispatch_blocks(step, steps, slot_ref, kept, buffer_refs)


def grads_and_buffers(
    middle, gate, own, other, grad, normed, router, chosen, slot, experts, slots, last
):
    length, width = middle.shape
    steps = 4
    block = length // steps

    def by_rows(value):
        lanes = value.shape[1]
        return (value, pl.BlockSpec((block, lanes), lambda i: (jnp.minimum(i, steps - 1), 0)))

    buffers, grid = buffer_outputs(experts, slots, width // 2, steps)
    outputs = [by_rows(shape_of(length, width))] if last else []
    outputs += [by_rows(shape_of(length, chosen.shape[1]))]
    got = call(
        functools.partial(grad_kernel, experts, steps, last),
        [by_rows(value) for value in (middle, gate, own, other, grad, normed)]
        + [(router, None), by_rows(chosen), (slot, None)],
        outputs + buffers,
        grid=(grid,),
        scratch=[pltpu.VMEM((length, width), BF16), pltpu.VMEM((block, width), F32)],
    )
    return got[: len(outputs)], got[len(outputs) :]


def attend_back_kernel(heads, *refs):
    own_ref, other_ref, logits_ref, router_ref, middle_ref, grad_ref, gain_ref = refs[:7]
    out_ref, qkv_ref, a_ref, w_ref, refs = refs[7], refs[8], refs[9], refs[10], refs[11:]
    mid_ref, low_ref, gain_grad_ref, dp_ref, diag_ref, keep_ref, give_ref = refs[:7]
    joined, grads_ref, dk, dv, strip, da_ref, ds_ref, query_ref, wide_ref = refs[7:]
    block = pl.program_id(0)
    length, width = middle_ref.shape
    rows = a_ref.shape[1]
    lanes_all = qkv_ref.shape[2]
    span = strip.shape[2]
    half = width // 2
    scaling = HEAD_DIM ** (-0.5)

    @pl.when(block == 0)
    def _():
        core = which_core()
        member = which_member()
        gain = gain_ref[...]
        gain_grad = jnp.zeros((1, width), F32)
        step = joined.shape[0]
        for at_row in range(0, length, step):
            part = pl.ds(at_row, step)
            joined[:, half_at(core, half)] = own_ref[part, :].astype(F32)
            joined[:, half_at(1 - core, half)] = other_ref[part, :].astype(F32)
            grad_normed = joined[...] + dot(logits_ref[part, :], router_ref[...], (1, 1))
            middle = middle_ref[part, :]
            scale = row_scale(middle)
            scaled = grad_normed * gain
            mean = jnp.mean(scaled * middle, -1, keepdims=True)
            grad = grad_ref[part, :].astype(F32) + (
                scale * scaled - middle * (scale * scale * scale) * mean
            )
            gain_grad += jnp.sum(grad_normed * middle * scale, 0, keepdims=True)
            mid_ref[part, :] = grad
            low = grad.astype(BF16)
            low_ref[part, :] = low
            grads_ref[part, :] = dot(low, out_ref[member]).astype(BF16)
        gain_grad_ref[...] = gain_grad
        dk[...] = jnp.zeros_like(dk)
        dv[...] = jnp.zeros_like(dv)
        strip[...] = jnp.zeros_like(strip)

    start = pl.multiple_of((length // rows - 1 - block) * rows, rows)
    here = pl.ds(pl.multiple_of(block * rows, rows), rows)
    queries, keys, values = qkv_ref[0, here, :], qkv_ref[1], qkv_ref[2]
    grads = grads_ref[here, :]
    for head in range(heads):
        lanes = head_lanes(lanes_all, head)
        part = pl.ds(head * rows, rows)
        own_grad = jnp.where(lanes, grads, jnp.zeros_like(grads))
        wide_ref[part, :] = own_grad
        query_ref[part, :] = jnp.where(lanes, queries, jnp.zeros_like(queries))
        da_ref[head] = dot(own_grad, values, (1, 1))
    step = 32
    dq = jnp.zeros((rows, lanes_all), F32)
    for head in range(heads):
        for at_row in range(0, rows, step):
            part = pl.ds(at_row, step)
            weights = a_ref[head, part, :].astype(F32)
            da = da_ref[head, part, :]
            ds = weights * (da - jnp.sum(weights * da, -1, keepdims=True))
            ds = ds.astype(BF16)
            ds_ref[pl.ds(head * rows + at_row, step), :] = ds
            strip[head, part, pl.ds(start, length)] += ds.astype(F32)
        own = dot(ds_ref[pl.ds(head * rows, rows), :], keys)
        dq = jnp.where(head_lanes(lanes_all, head), own, dq)
    dk[...] += dot(ds_ref[...], query_ref[...], (0, 0))
    dv[...] += dot(a_ref[...].reshape(heads * rows, length), wide_ref[...], (0, 0))
    dp_ref[0, here, :] = (dq * scaling).astype(BF16)

    @pl.when(block == length // rows - 1)
    def _():
        dp_ref[1] = (dk[...] * scaling).astype(BF16)
        dp_ref[2] = dv[...].astype(BF16)
        sub = lax.broadcasted_iota(jnp.int32, (8, span), 0)
        for head in range(heads):
            part = strip[head]
            size = rows // 2
            while size >= 8:
                part = part[:size] + pltpu.roll(part[size:], span - size, 1)
                size //= 2
            for bit in (4, 2, 1):
                part = jnp.where((sub & bit) != 0, pltpu.roll(part, span - bit, 1), part)
            diag_ref[head : head + 1, :] = jnp.sum(part, 0, keepdims=True)
        core = which_core()
        for side, ref in ((core, keep_ref), (1 - core, give_ref)):
            for at_row in range(0, length, 256):
                part = pl.ds(at_row, 256)
                total = jnp.zeros((256, half), F32)
                for v in range(3):
                    total += dot(dp_ref[v, part, :], w_ref[v, half_at(side, half), :], (1, 1))
                ref[part, :] = total.astype(BF16)


def attend_back(own, other, logits, router, middle, grad, gain, out, qkv, a, weights):
    length, width = middle.shape
    heads = a.shape[0]
    lanes = qkv.shape[2]
    half = width // 2
    span = 2 * length
    block = pl.BlockSpec((heads, BLOCK, length), lambda i: (0, i, 0))
    return call(
        functools.partial(attend_back_kernel, heads),
        [
            (value, None)
            for value in (own, other, logits, router, middle, grad, gain, out, qkv)
        ]
        + [(a, block), (weights, None)],
        [
            (shape_of(length, width, dtype=F32), None),
            (shape_of(length, width), None),
            (shape_of(1, width, dtype=F32), None),
            (shape_of(3, length, lanes), None),
            (shape_of(heads, span, dtype=F32), None),
            (shape_of(length, half), None),
            (shape_of(length, half), None),
        ],
        grid=(length // BLOCK,),
        scratch=[
            pltpu.VMEM((256, width), F32),
            pltpu.VMEM((length, lanes), BF16),
            pltpu.VMEM((length, lanes), F32),
            pltpu.VMEM((length, lanes), F32),
            pltpu.VMEM((heads, BLOCK, span), F32),
            pltpu.VMEM((heads, BLOCK, length), F32),
            pltpu.VMEM((heads * BLOCK, length), BF16),
            pltpu.VMEM((heads * BLOCK, lanes), BF16),
            pltpu.VMEM((heads * BLOCK, lanes), BF16),
        ],
        vmem=58,
        flops=LONG,
    )


def head_grads_kernel(normed_ref, dp_ref, low_ref, own_ref, out_ref):
    for v in range(3):
        out_ref[v] = dot(normed_ref[...], dp_ref[v], (0, 0)).astype(BF16)
    out_ref[3] = dot(low_ref[...], own_ref[...], (0, 0)).astype(BF16)


def head_weight_grads(normed, dp, low, own):
    length, width = normed.shape
    lanes = own.shape[1]
    return call(
        head_grads_kernel,
        [(value, None) for value in (normed, dp, low, own)],
        [(shape_of(4, width, lanes), None)],
        vmem=58,
    )[0]


def rows_back_kernel(own_ref, other_ref, x_ref, gain_ref, mid_ref, out_ref, gain_grad_ref, joined):
    rows, width = x_ref.shape
    half = width // 2
    core = which_core()

    @pl.when(pl.program_id(0) == 0)
    def _():
        gain_grad_ref[...] = jnp.zeros_like(gain_grad_ref)

    joined[:, half_at(core, half)] = own_ref[...].astype(F32)
    joined[:, half_at(1 - core, half)] = other_ref[...].astype(F32)
    grad = joined[...]
    values = x_ref[...].astype(F32)
    scale = row_scale(values)
    scaled = grad * gain_ref[...]
    mean = jnp.mean(scaled * values, -1, keepdims=True)
    change = scale * scaled - values * (scale * scale * scale) * mean
    out_ref[...] = (mid_ref[...] + change).astype(BF16)
    gain_grad_ref[...] += jnp.sum(grad * values * scale, 0, keepdims=True)


def rows_back(own, other, rows, gain, mid):
    length, width = rows.shape
    block = length // 4
    return call(
        rows_back_kernel,
        [
            (own, row_blocks(block, own.shape[1])),
            (other, row_blocks(block, own.shape[1])),
            (rows, row_blocks(block, width)),
            (gain, None),
            (mid, row_blocks(block, width)),
        ],
        [
            (shape_of(length, width), row_blocks(block, width)),
            (shape_of(1, width, dtype=F32), None),
        ],
        grid=(4,),
        scratch=[pltpu.VMEM((block, width), F32)],
    )


def query_weights(pieces, before_hosts=()):
    x, _, c, _ = place()

    def to(x, h, c, t):
        return (x, h, c, t ^ (x + 2 * c)) if x + 2 * c else None

    def across(x, h, c, t):
        return (x, h, 1 - c, t ^ (x + 2 * (1 - c)))

    own = jnp.where(x + 2 * c == 0, pieces, send(pieces, to))
    other = send(pieces, across)
    own, other = after((own, other), before_hosts)
    if lax.axis_size("dp") == 4:
        return [own, other, host_swap(own, 1), host_swap(other, 1)]
    both = ordered(c, own, other, 1)
    return [rows_over_hosts(both[:, None], 1).reshape(3, -1, pieces.shape[2])]


def out_weights(piece):
    _, _, c, _ = place()
    four = jnp.stack([piece] + [tensor_swap(piece, j) for j in (1, 2, 3)])
    four = rows_over_hosts(four[:, None], 1)
    four = ordered(c, four[:, :, None], core_swap(four)[:, :, None], 2)
    return four.reshape(4, -1, piece.shape[1])


def weights_out(i):
    def to(x, h, c, t):
        return (x, h, 1 - (t & 1), c + 2 * (i ^ (t >> 1) ^ c))

    return to


def weights_home(i):
    def to(x, h, c, t):
        return (x, h, t & 1, 2 * (i ^ (t >> 1) ^ (t & 1)) + 1 - c)

    return to


def pack(up, down):
    half = up.shape[0] // 2
    return jnp.concatenate([jnp.concatenate([up[:half], up[half:]], 1), down], 0)


def unpack_pair(packed):
    rows, half = packed.shape[0] // 2, packed.shape[1] // 2
    up = jnp.concatenate([packed[:rows, :half], packed[:rows, half:]], 0)
    return up, packed[rows:]


def expert_weights(packed):
    return [send(packed, weights_out(i)) for i in range(2)]


def for_own_layer(zero, one):
    x, _, _, _ = place()
    other = section_swap(jnp.where(x == 0, one, zero).astype(BF16))
    return jnp.where(x == 0, zero, one), other


def to_expert(buffers, experts):
    if len(buffers) == 1:
        pieces = buffers[0].reshape(experts, -1, buffers[0].shape[1])
        own = [expert_exchange(pieces).reshape(buffers[0].shape)]
    else:
        order = [len(buffers) - 1] + list(range(1, len(buffers) - 1))
        got = {j: expert_swap(buffers[j], j) for j in order}
        own = [buffers[0]] + [got[j] for j in range(1, len(buffers))]
    return own, [core_swap(part) for part in own]


def add(first, second):
    return first + second


def after(values, earlier):
    return lax.optimization_barrier((values, earlier))[0]


def from_expert(parts, slot_column, experts, at_sums=(), at_combine=()):
    if len(parts) == 2:
        keep, give = parts
        chip = add(keep, core_swap(give))
        pieces = add(chip, section_swap(chip)).reshape(experts, -1, chip.shape[1])
        whole = expert_exchange(pieces).reshape(chip.shape)
        rows = combine((whole, jnp.zeros_like(whole)), (), slot_column)
        return rows, core_swap(rows)
    split = experts // 2
    chips = [add(keep, core_swap(give)) for keep, give in (parts[:2], parts[2:])]
    back = {}
    for first, chip in ((split, chips[0]), (0, chips[1])):
        other = section_swap(chip)
        if not first:
            other = after(other, at_sums)
        count = chip.shape[0] // split
        for j in range(first + split - 1, first - 1, -1):
            piece = slice((j - first) * count, (j - first + 1) * count)
            if j == 0:
                local = (chip[piece], other[piece])
            else:
                back[j] = expert_swap(add(chip[piece], other[piece]), j)
    local = after(local, at_combine)
    rows = combine(local, [back[j] for j in range(1, experts)], slot_column)
    return rows, core_swap(rows)


def layer_forward(
    source, params, attention, packs, experts, slots, mix, at_own, at_middle, during
):
    gain_one, base, prefix, gain_two, router, chosen, slot, slot_column = params
    qkv_pieces, out_pieces = attention
    rows, normed, qkv, qkv_weights, own, weights = attend(
        source, mix, prefix, gain_one, qkv_pieces, base
    )
    own = after(own, at_own)
    other = section_swap(own)
    pieces = after((own, other, core_swap(own), core_swap(other)), at_middle)
    middle, normed_two, gate, buffers = middle_and_buffers(
        rows, pieces, out_pieces, gain_two, router, chosen, slot, experts, slots
    )
    arrived = to_expert(buffers, experts)
    at_sums, at_combine = during(arrived[0])
    active, slope, parts = expert_rows(*arrived, packs)
    produced = from_expert(parts, slot_column, experts, at_sums, at_combine)
    saved = (rows, normed, qkv, qkv_weights, own, weights, middle, normed_two, gate)
    return saved, (arrived, active, slope), produced


def layer_backward(
    layer, grad, forward, params, attention, packs, experts, slots, during, at_chip
):
    gain_one, base, prefix, gain_two, router, chosen, slot, slot_column = params
    out_pieces = attention[1]
    saved, (arrived, active, slope), produced = forward
    rows, normed, qkv, qkv_weights, own, weights, middle, normed_two, gate = saved
    last = layer == 1
    got, buffers = grads_and_buffers(
        middle, gate, *produced, grad, normed_two, router, chosen, slot, experts, slots, last
    )
    grad_logits = got[-1]
    grad_arrived = to_expert(buffers, experts)
    at_sums, at_combine = during(grad_arrived[0], got[0])
    hidden, parts = expert_rows_back(*grad_arrived, slope, packs)
    expert_grads = expert_weight_grads(*arrived, *grad_arrived, active, hidden)
    grad_normed_two = from_expert(
        parts, slot_column, experts, at_sums, (expert_grads, at_combine)
    )
    expert_grads = after(tuple(expert_grads), grad_normed_two[0])
    expert_grads = tuple(send(part, weights_home(i)) for i, part in enumerate(expert_grads))
    grad_router = dot(normed_two, grad_logits, (0, 0))[:, :experts]
    mid, low, grad_gain_two, dp, diagonal, keep, give = attend_back(
        *grad_normed_two,
        grad_logits,
        router,
        middle,
        grad,
        gain_two,
        out_pieces,
        qkv,
        weights,
        qkv_weights,
    )
    keep, give = after((keep, give), expert_grads[0])
    chip = add(keep, core_swap(give))
    head_grads = head_weight_grads(normed, dp, low, own)
    at_total = at_chip(grad_normed_two[0])
    total = add(chip, after(section_swap(chip), (head_grads, expert_grads[1], at_total)))
    grad_rows, grad_gain_one = rows_back(total, core_swap(total), rows, gain_one, mid)
    small = (grad_gain_one[0], grad_gain_two[0], grad_router, diagonal)
    return grad_rows, expert_grads, head_grads, small, total


def over_rows(grads, earlier=()):
    _, h, _, _ = place()
    hosts = lax.axis_size("dp") // 2
    parts = grads.reshape(4, hosts, 2, -1, grads.shape[2])
    parts = jnp.transpose(parts, (1, 2, 0, 3, 4))
    bit = hosts // 2
    while bit:
        pair = parts.reshape(2, bit, *parts.shape[1:])
        upper = (h & bit) != 0
        keep = jnp.where(upper, pair[1], pair[0])
        give = jnp.where(upper, pair[0], pair[1])
        parts = add(keep, after(host_swap(give, bit), earlier))
        bit //= 2
    return parts[0]


def to_quarter(part):
    x, _, c, _ = place()

    def to(x, h, c, t):
        return (x, h, c, t ^ (x + 2 * c)) if x + 2 * c else None

    return jnp.where(x + 2 * c == 0, part, send(part, to))


def over_cores(part):
    _, _, c, _ = place()
    keep = jnp.where(c == 0, part[0], part[1]).astype(F32)
    give = jnp.where(c == 0, part[1], part[0])
    return keep + core_swap(give).astype(F32)


def over_groups(values):
    one, two, three = (tensor_swap(values, j) for j in (1, 2, 3))
    values = (values + one) + (two + three)
    bit = 1
    while bit < lax.axis_size("dp") // 2:
        values = values + host_swap(values, bit)
        bit *= 2
    return values


def pick(flag, first, second):
    return jax.tree.map(lambda a, b: jnp.where(flag == 0, a, b), first, second)


def per_device(
    block_input,
    cotangent,
    query_key_value_weights,
    attention_output_weights,
    bias_table,
    norm_first,
    norm_second,
    router_projection_weights,
    expert_up,
    expert_down,
    routes,
    prefix_lengths,
    relative_buckets,
):
    x, h, c, t = place()
    _, piece, width = block_input.shape
    length = routes.shape[2]
    buckets, head_count = bias_table.shape[1:]
    experts = router_projection_weights.shape[2]
    heads = head_count // 4
    capacity = (5 * length + 4 * experts - 1) // (4 * experts)

    pieces = jnp.concatenate(
        [query_key_value_weights[0], attention_output_weights[0].T[None]], 0
    )
    other = section_swap(pieces)
    pieces = pick(x, (pieces, other), (other, pieces))
    scale = 32
    packed = jnp.concatenate(
        [
            routes[0, :, :, 0].reshape(-1),
            prefix_lengths // scale,
            prefix_lengths % scale,
        ]
    ).astype(BF16)
    both = ordered(c, packed[None], core_swap(packed)[None], 0)
    lower = at(both, t >> 1)
    route = lax.dynamic_slice_in_dim(lower, (t & 1) * length, length, 0)
    numbers = lower[2 * length :].astype(F32).astype(jnp.int32)
    prefix = lax.dynamic_slice_in_dim(numbers[:2] * scale + numbers[2:], t & 1, 1, 0)
    packed = jnp.concatenate(
        [
            route,
            norm_first[0],
            norm_second[0],
            router_projection_weights[0].reshape(-1),
            bias_table[0].reshape(-1),
        ]
    )
    other = section_swap(packed)
    packed = pick(x, (packed, other), (other, packed))

    half = expert_up.shape[3] // 2
    up, down = expert_up[0, 0], expert_down[0, 0]
    lower = pack(up[:, :half], down[:half])
    upper = pack(up[:, half:], down[half:])
    keep = jnp.where(x == 0, lower, upper)
    other = section_swap(after(jnp.where(x == 0, upper, lower), pieces))
    packs = pick(x, (keep, other), (other, keep))

    rows = to_groups(block_input)

    bucket_onehot = (
        relative_buckets[:, None] == jnp.arange(buckets, dtype=jnp.int32)[None, :]
    ).astype(BF16)
    earlier = (
        jnp.arange(length, dtype=jnp.int32)[None, :] < jnp.arange(length, dtype=jnp.int32)[:, None]
    ).astype(BF16)
    expert_ids = jnp.arange(experts, dtype=jnp.int32)

    def unpack(vector):
        route = vector[:length].astype(F32).astype(jnp.int32)
        at_one = length
        gain_one = vector[at_one : at_one + width].astype(F32)
        at_two = at_one + width
        gain_two = vector[at_two : at_two + width].astype(F32)
        at_router = at_two + width
        router = vector[at_router : at_router + width * experts].reshape(width, experts)
        table = vector[at_router + width * experts :].reshape(buckets, head_count)
        own = lax.dynamic_slice_in_dim(table, ((x + 2 * c) ^ t) * heads, heads, 1)
        rel = lax.dot_general(
            own, bucket_onehot, (((0,), (1,)), ((), ())), preferred_element_type=F32
        )
        base = jnp.roll(jnp.pad(rel, ((0, 0), (0, 1))), -(BLOCK - 1), axis=1)
        chosen = route[:, None] == expert_ids[None, :]
        rank = jnp.dot(earlier, chosen.astype(BF16), preferred_element_type=F32)
        rank = jnp.sum(jnp.where(chosen, rank, 0.0), 1).astype(jnp.int32)
        slot = (route ^ (2 * h + (t & 1))) * capacity + rank
        pad = ((0, 0), (0, 128 - experts))
        return (
            gain_one[None],
            base,
            prefix,
            gain_two[None],
            jnp.pad(router, pad),
            jnp.pad(chosen.astype(F32), pad),
            slot[None],
            slot[:, None],
        )

    params = [unpack(vector) for vector in packed]
    got = tuple(rows[:2])
    queries_zero = query_weights(pieces[0][:3], got)
    outs_zero = out_weights(after(pieces[0][3], pieces[0]))
    packs_zero = expert_weights(packs[0])
    slots = experts * capacity
    rows = after(tuple(rows), packs[0])
    later = {}

    def during_zero(arrived):
        arrived = tuple(arrived)
        later["queries"] = query_weights(after(pieces[1][:3], arrived))
        later["outs"] = out_weights(after(pieces[1][3], arrived))
        return tuple(later["queries"][:2]), ()

    zero = layer_forward(
        rows,
        params[0],
        (queries_zero, outs_zero),
        packs_zero,
        experts,
        slots,
        False,
        packs_zero[0],
        packs_zero[1],
        during_zero,
    )
    packs_one = expert_weights(after(packs[1], zero[2][0]))

    def during_one(arrived):
        later["top"] = to_groups(after(cotangent, tuple(arrived)))
        return tuple(later["top"]), ()

    one = layer_forward(
        (zero[0][6], zero[0][8], *zero[2]),
        params[1],
        (later["queries"], later["outs"]),
        packs_one,
        experts,
        slots,
        True,
        packs_one[0],
        packs_one[1],
        during_one,
    )
    top = whole_rows(later["top"])

    def during_back_one(arrived, result):
        outputs = after(jnp.where(x == 0, one[0][0], result), tuple(arrived))
        later["outputs"] = from_groups(outputs)
        return later["outputs"], ()

    grads_one = layer_backward(
        1,
        top,
        one,
        params[1],
        (None, later["outs"]),
        packs_one,
        experts,
        slots,
        during_back_one,
        lambda returned: (),
    )

    def during_back_zero(arrived, _):
        later["heads"] = over_rows(after(grads_one[2], tuple(arrived)))
        return later["heads"], ()

    def at_total_zero(returned):
        later["heads"] = to_quarter(after(later["heads"], returned))
        return later["heads"]

    grads_zero = layer_backward(
        0,
        grads_one[0],
        zero,
        params[0],
        (None, outs_zero),
        packs_zero,
        experts,
        slots,
        during_back_zero,
        at_total_zero,
    )
    outputs = later["outputs"]

    def summed(pair):
        return pair[0].astype(F32) + pair[1].astype(F32)

    expert_zero = summed(after(grads_zero[1], grads_zero[4]))
    own, other = for_own_layer(expert_zero, summed(grads_one[1]))
    expert_own, expert_other = unpack_pair(own), unpack_pair(other.astype(F32))
    heads_zero = over_cores(to_quarter(over_rows(grads_zero[2], grads_zero[4])))
    own, other = for_own_layer(heads_zero, over_cores(later["heads"]))
    heads_grad = own + other.astype(F32)
    grad_rows = from_groups(jnp.where(x == 0, grads_zero[0], grads_one[0]))

    def flat(small):
        gain_one, gain_two, router, diagonal = small
        total = jnp.roll(diagonal, BLOCK - 1, axis=1)[:, : 2 * length - 1]
        table = lax.dot_general(
            bucket_onehot.astype(F32),
            total,
            (((0,), (1,)), ((), ())),
            precision=lax.Precision.HIGHEST,
        )
        whole = lax.dynamic_update_slice_in_dim(
            jnp.zeros((buckets, head_count), F32), table, ((x + 2 * c) ^ t) * heads, 1
        )
        return jnp.concatenate([gain_one, gain_two, router.reshape(-1), whole.reshape(-1)])

    everything = over_groups(jnp.stack([flat(grads_zero[3]), flat(grads_one[3])]))
    core = core_swap(everything)
    size = everything.shape[1] - buckets * head_count
    tables = everything[:, size:] + core[:, size:]
    tables = tables + section_swap(tables)
    shared = at(jnp.where(c == 0, everything, core), x)

    grad_up = ordered(x, expert_own[0], expert_other[0], 1)
    grad_down = ordered(x, expert_own[1], expert_other[1], 0)
    grad_in = heads_grad[:3]
    grad_out = heads_grad[3].T

    return (
        outputs[None],
        grad_rows[None],
        grad_in[None],
        grad_out[None],
        at(tables, x).reshape(1, buckets, head_count),
        shared[:width][None],
        shared[width : 2 * width][None],
        shared[2 * width : size].reshape(1, width, experts),
        grad_up[None, None],
        grad_down[None, None],
    )


def solution(mesh):
    in_specs = (
        P("dp", "tensor", None),
        P("dp", "tensor", None),
        P("section", None, "dp", "tensor"),
        P("section", "tensor", "dp"),
        P("section", None, None),
        P("section", None),
        P("section", None),
        P("section", None, None),
        P("section", "dp", None, "tensor"),
        P("section", "dp", "tensor", None),
        P("section", "dp", None, None),
        P("dp"),
        P(),
    )
    out_specs = (
        P("section", "dp", "tensor", None),
        P("section", "dp", "tensor", None),
        P("section", None, "dp", "tensor"),
        P("section", "tensor", "dp"),
        P("section", None, None),
        P("section", None),
        P("section", None),
        P("section", None, None),
        P("section", "dp", None, "tensor"),
        P("section", "dp", "tensor", None),
    )
    return jax.shard_map(
        per_device, mesh=mesh, in_specs=in_specs, out_specs=out_specs, check_vma=False
    )
```

time: 960 us -> 791 us (0.82)
  Pallas kernels: 82.1 us -> 202 us
  waiting for transfers between devices: 335 us -> 234 us
  matrix products: 73.5 us -> 5.64 us
  other arithmetic: 123 us -> 58.3 us
  local copies, waits for them, and re-layouts: 99 us -> 58.2 us
    pallas_call x4 -> x22, Pallas kernels: 82.1 us -> 202 us  [call(): pl.pallas_call(kernel, grid=grid, in_specs=[spec(item) for item in inputs...]
    ppermute x148 -> x128, waiting for transfers between devices: 335 us -> 234 us  [send(): return lax.ppermute(value, AXES, pairs)]
    dot_general x36 -> x2, matrix products: 65.7 us -> 0.7 us  [dot(): return lax.dot_general(a, b, dims, preferred_element_type=F32)]
    convert_element_type x36 -> x2, other arithmetic: 31.2 us -> 2.88 us  [the longest x1 1.59 us: per_device(): other.astype(F32)]
    select_n x28 -> x6, other arithmetic: 29.1 us -> 4.26 us  [ordered(): first = jnp.where(flag == 0, own, other)]
    convert_element_type x9 -> x0, local copies, waits for them, and re-layouts: 10.6 us -> none  [the longest x2 5.01 us: head_grads_home(): pieces = grads.astype(BF16).reshape(groups, -1, grads.shape[1])]
    add x6 -> x24, other arithmetic: 2.77 us -> 13.1 us  [the longest x20 11.6 us: add(): return first + second]
    ppermute x148 -> x128, starting transfers between devices: 232 us -> 223 us  [send(): return lax.ppermute(value, AXES, pairs)]
  transfers between devices with their start and end apart: 148 -> 128, of which waited for: 71 -> 51; matrix products, arithmetic and copies ran while one was open for 22% -> 10% of each run, Pallas kernels for 6% -> 17%
where the time goes in v2:
time: 791 us; the launch traced here: 784 us
  waiting for transfers between devices  234 us (30%)
  starting transfers between devices  223 us (28%)
  Pallas kernels  202 us (26%)
  other arithmetic  58.3 us (7%)
  local copies, waits for them, and re-layouts  58.2 us (7%)
    ppermute x128, waiting for transfers between devices, send(): return lax.ppermute(value, AXES, pairs)  234 us
    ppermute x128, starting transfers between devices, send(): return lax.ppermute(value, AXES, pairs)  223 us
    pallas_call x22, Pallas kernels, call(): pl.pallas_call(kernel, grid=grid, in_specs=[spec(item) for item in inputs...  202 us
    unnamed x341, local copies, waits for them, and re-layouts  38.3 us
  transfers between devices with their start and end apart: 128, of which 51 were waited for; matrix products, arithmetic and copies ran while one was open for 10% of the time, Pallas kernels for 17%

profile of v2, /device:TPU:0, one launch (start us, length us, event | category | flops | bytes accessed | tf_op | source)
XLA Modules:
  0.0 784.3 jit_solution(6863474948242179441)
XLA Ops:
  29.3 9.3 %collective-permute-start.17 = (bf16[192,192]{1,0:T(8,128)(2,1)S(1)}, bf16[192,192]{1,0:T(8,128)(2,1)S(1)}, u32[]{:S(2)}, u32[]{:S(2)}) collective-permute-start(bf16[192,192]{1,0:T(8,128)(2,1)S(1)} %slice_bitcast_fusion.5), channel_id=1, source_target_pairs={{0,1},{1,0},{2,3},{3,2},{4,5},{5,4},{6,7},{7,6},{8,9},{9,8},{10,11... | collective-permute-start | bytes 221192 | tf_op jit(solution)/shard_map/ppermute | solution.py:34
  51.0 4.4 collective-permute-start.8
  63.4 5.1 collective-permute-done.9.refs_7_
  69.3 18.6 %shard_map.204 = (bf16[1024,768]{1,0:T(8,128)(2,1)}, bf16[1024,768]{1,0:T(8,128)(2,1)}, bf16[3,1024,192]{2,1,0:T(8,128)(2,1)}, bf16[3,768,192]{2,1,0:T(8,128)(2,...) custom-call(bf16[256,768]{1,0:T(8,128)(2,1)} %collective-permute-done.refs_0_, ...), custom_call_target="tpu_custom_call" | custom-call | flops 99999997952 | bytes 1000 | tf_op jit(solution)/shard_map/pallas_call | solution.py:173
  87.9 4.6 collective-permute-done.12.refs_8_.refs_9_
  94.9 9.7 %collective-permute-start.14 = (bf16[1024,192]{1,0:T(8,128)(2,1)S(1)}, bf16[1024,192]{1,0:T(8,128)(2,1)S(1)}, u32[]{:S(2)}, u32[]{:S(2)}) collective-permute-start(bf16[1024,192]{1,0:T(8,128)(2,1)S(1)} %copy-done.33), channel_id=1, source_target_pairs={{0,4},{1,5},{2,6},{3,7},{4,0},{5,1},{6,2},{7,3},{8,12},{9,13},{10,... | collective-permute-start | bytes 1179656 | tf_op jit(solution)/shard_map/ppermute | solution.py:34
  104.6 5.8 collective-permute-start.15
  114.2 7.8 shard_map.205
  125.6 15.1 %collective-permute-start.22 = (bf16[320,384]{1,0:T(8,128)(2,1)S(1)}, bf16[320,384]{1,0:T(8,128)(2,1)S(1)}, u32[]{:S(2)}, u32[]{:S(2)}) collective-permute-start(bf16[320,384]{1,0:T(8,128)(2,1)S(1)} %get-tuple-element.161), channel_id=1, source_target_pairs={{0,1},{1,0},{2,3},{3,2},{4,5},{5,4},{6,7},{7,6},{8,9},{9,8},{10,11... | collective-permute-start | bytes 737288 | tf_op jit(solution)/shard_map/ppermute | solution.py:34
  142.3 5.2 collective-permute-done.22.refs_1_
  147.5 6.1 collective-permute-done.23.refs_2_
  155.5 7.4 shard_map.206
  170.9 3.5 collective-permute-start.32
  176.4 4.3 collective-permute-done.32.refs_5_
  181.7 6.2 collective-permute-start.33
  188.0 3.4 collective-permute-done.35
  196.0 3.4 collective-permute-start.48
  200.6 4.8 collective-permute-done.36.refs_3_
  213.7 7.6 collective-permute-done.49
  227.7 5.8 collective-permute-done.40.refs_7_
  235.1 20.9 %shard_map.208 = (bf16[1024,768]{1,0:T(8,128)(2,1)}, bf16[1024,768]{1,0:T(8,128)(2,1)}, bf16[3,1024,192]{2,1,0:T(8,128)(2,1)}, bf16[3,768,192]{2,1,0:T(8,128)(2,...) custom-call(f32[1024,768]{1,0:T(8,128)} %copy-done.29, f32[1024,1]{1,0:T(8,128)} %copy-done.82, ...), custom_call_target="tpu_custom_call" | custom-call | flops 99999997952 | bytes 1000 | tf_op jit(solution)/shard_map/pallas_call | solution.py:173
  258.8 5.5 collective-permute-start.43
  266.0 5.0 collective-permute-start.44
  274.9 7.8 shard_map.209
  286.3 14.8 %collective-permute-start.51 = (bf16[320,384]{1,0:T(8,128)(2,1)S(1)}, bf16[320,384]{1,0:T(8,128)(2,1)S(1)}, u32[]{:S(2)}, u32[]{:S(2)}) collective-permute-start(bf16[320,384]{1,0:T(8,128)(2,1)S(1)} %get-tuple-element.186), channel_id=1, source_target_pairs={{0,1},{1,0},{2,3},{3,2},{4,5},{5,4},{6,7},{7,6},{8,9},{9,8},{10,11... | collective-permute-start | bytes 737288 | tf_op jit(solution)/shard_map/ppermute | solution.py:34
  302.6 5.3 collective-permute-done.51.refs_1_
  307.9 6.1 collective-permute-done.52.refs_2_
  315.9 7.2 shard_map.210
  324.2 4.1 collective-permute-start.60
  330.5 6.6 collective-permute-done.61
  337.1 9.4 %collective-permute-done.60 = bf16[256,768]{1,0:T(8,128)(2,1)S(1)} collective-permute-done((bf16[256,768]{1,0:T(8,128)(2,1)S(1)}, bf16[256,768]{1,0:T(8,128)(2,1)S(1)}, u32[]{:S(2)}, u32[]{:S(2)}) %collective-permute-start.60) | collective-permute-done | bytes 393248 | tf_op jit(solution)/shard_map/ppermute | solution.py:34
  349.3 11.1 %collective-permute-done.66 = bf16[640,384]{1,0:T(8,128)(2,1)S(1)} collective-permute-done((bf16[640,384]{1,0:T(8,128)(2,1)S(1)}, bf16[640,384]{1,0:T(8,128)(2,1)S(1)}, u32[]{:S(2)}, u32[]{:S(2)}) %collective-permute-start.66) | collective-permute-done | bytes 491552 | tf_op jit(solution)/shard_map/ppermute | solution.py:34
  363.4 6.9 collective-permute-done.68.refs_4_
  370.2 4.3 collective-permute-done.67.refs_3_
  377.5 4.9 shard_map.211.refs_2_
  386.6 6.5 shard_map.212
  398.4 5.3 collective-permute-done.70.refs_1_.refs_9_
  404.2 4.7 collective-permute-done.72.refs_3_.refs_11_
  410.4 6.8 shard_map.213
  421.7 11.8 %collective-permute-done.80 = bf16[640,384]{1,0:T(8,128)(2,1)S(1)} collective-permute-done((bf16[640,384]{1,0:T(8,128)(2,1)S(1)}, bf16[640,384]{1,0:T(8,128)(2,1)S(1)}, u32[]{:S(2)}, u32[]{:S(2)}) %collective-permute-start.80) | collective-permute-done | bytes 491552 | tf_op jit(solution)/shard_map/ppermute | solution.py:34
  435.4 7.8 collective-permute-done.83
  446.6 10.5 %shard_map.214 = (bf16[768,768]{1,0:T(8,128)(2,1)}, bf16[768,768]{1,0:T(8,128)(2,1)}) custom-call(bf16[320,384]{1,0:T(8,128)(2,1)} %copy-done.55, bf16[320,384]{1,0:T(8,128)(2,1)} %copy-done.56, bf16[320,384]{1,0:T(8,128)(2,1)} %copy-done.57, bf16[320,384]{1,0:T(8,128)(2,1)} %copy-done.58, bf16[320,384]{1,0:T(8,128)(2,1)} %copy-done.59, ...), custom_call_target="tpu_custom_call" | custom-call | flops 1000000000 | bytes 1000 | tf_op jit(solution)/shard_map/pallas_call | solution.py:173
  463.2 27.9 %shard_map.216 = (f32[1024,768]{1,0:T(8,128)}, bf16[1024,768]{1,0:T(8,128)(2,1)}, f32[1,768]{1,0:T(1,128)}, bf16[3,1024,192]{2,1,0:T(8,128)(2,1)}, f32[3,2048]{1...) custom-call(bf16[1024,384]{1,0:T(8,128)(2,1)} %copy-done.104, bf16[1024,384]{1,0:T(8,128)(2,1)} %copy-done.153, ...), custom_call_target="tpu_custom_call" | custom-call | flops 99999997952 | bytes 1000 | tf_op jit(solution)/shard_map/pallas_call | solution.py:173
  496.6 5.6 shard_map.217
  502.2 18.5 %collective-permute-done.90 = bf16[768,768]{1,0:T(8,128)(2,1)S(1)} collective-permute-done((bf16[768,768]{1,0:T(8,128)(2,1)}, bf16[768,768]{1,0:T(8,128)(2,1)S(1)}, u32[]{:S(2)}, u32[]{:S(2)}) %collective-permute-start.90) | collective-permute-done | bytes 1179680 | tf_op jit(solution)/shard_map/ppermute | solution.py:34
  527.8 5.3 shard_map.219
  537.4 5.3 collective-permute-done.92.refs_1_.refs_9_
  543.2 4.3 collective-permute-done.94.refs_3_.refs_11_
  551.7 8.4 %shard_map.220 = (bf16[1280,768]{1,0:T(8,128)(2,1)S(1)}, bf16[640,384]{1,0:T(8,128)(2,1)S(1)}, bf16[640,384]{1,0:T(8,128)(2,1)S(1)}, bf16[640,384]{1,0:T(8,128)(2,1)S(1)}, bf16[640,384]{1,0:T(8,128)(2,1)}) custom-call(bf16[320,384]{1,0:T(8,128)(2,1)} %get-tuple-element.233.refs_0_.refs_8_, bf16[320,384]{1,0:T(8,128)(2,1)S(1)} %collective-permute-done.92.refs_1_.refs_9_, ...), custom_call_target="tpu_custom_call" | custom-call | flops 1000000000 | bytes 1000 | tf_op jit(solution)/shard_map/pallas_call | solution.py:173
  565.3 16.3 %collective-permute-done.101 = bf16[1,2,4,192,192]{4,3,2,1,0:T(8,128)(2,1)} collective-permute-done((bf16[1,2,4,192,192]{4,3,2,1,0:T(8,128)(2,1)}, bf16[1,2,4,192,192]{4,3,2,1,0:T(8,128)(2,1)}, u32[]{:S(2)}, u32[]{:S(2)}) %collective-permute-start.101) | collective-permute-done | bytes 589856 | tf_op jit(solution)/shard_map/ppermute | solution.py:34
  591.6 4.5 collective-permute-done.100
  599.2 10.5 %shard_map.221 = (bf16[768,768]{1,0:T(8,128)(2,1)}, bf16[768,768]{1,0:T(8,128)(2,1)}) custom-call(bf16[320,384]{1,0:T(8,128)(2,1)} %copy-done.47, bf16[320,384]{1,0:T(8,128)(2,1)} %copy-done.48, bf16[320,384]{1,0:T(8,128)(2,1)} %copy-done.49, bf16[320,384]{1,0:T(8,128)(2,1)} %copy-done.50, bf16[320,384]{1,0:T(8,128)(2,1)} %copy-done.51, ...), custom_call_target="tpu_custom_call" | custom-call | flops 1000000000 | bytes 1000 | tf_op jit(solution)/shard_map/pallas_call | solution.py:173
  616.4 5.8 collective-permute-done.73
  622.3 5.4 collective-permute-done.74
  628.7 5.8 collective-permute-start.108
  634.5 27.8 %shard_map.223 = (f32[1024,768]{1,0:T(8,128)}, bf16[1024,768]{1,0:T(8,128)(2,1)}, f32[1,768]{1,0:T(1,128)}, bf16[3,1024,192]{2,1,0:T(8,128)(2,1)}, f32[3,2048]{1...) custom-call(bf16[1024,384]{1,0:T(8,128)(2,1)} %copy-done.103, ...), custom_call_target="tpu_custom_call" | custom-call | flops 99999997952 | bytes 1000 | tf_op jit(solution)/shard_map/pallas_call | solution.py:173
  667.0 3.7 collective-permute-start.111
  671.7 5.5 shard_map.224
  685.7 11.7 %collective-permute-start.119 = (bf16[4,192,192]{2,1,0:T(8,128)(2,1)S(1)}, bf16[4,192,192]{2,1,0:T(8,128)(2,1)}, u32[]{:S(2)}, u32[]{:S(2)}) collective-permute-start(bf16[4,192,192]{2,1,0:T(8,128)(2,1)S(1)} %select_bitcast_fusion.4), channel_id=1, source_target_pairs={{0,4},{1,5},{2,6},{3,7},{4,0},{5,1},{6,2},{7,3},{8,12},{9,13},{10,... | collective-permute-start | bytes 884744 | tf_op jit(solution)/shard_map/ppermute | solution.py:34
  700.5 12.5 %collective-permute-done.111 = bf16[768,768]{1,0:T(8,128)(2,1)} collective-permute-done((bf16[768,768]{1,0:T(8,128)(2,1)}, bf16[768,768]{1,0:T(8,128)(2,1)}, u32[]{:S(2)}, u32[]{:S(2)}) %collective-permute-start.111) | collective-permute-done | bytes 1179680 | tf_op jit(solution)/shard_map/ppermute | solution.py:34
  732.1 4.4 collective-permute-start.123
  738.1 10.7 %collective-permute-start.118 = (bf16[4,192,192]{2,1,0:T(8,128)(2,1)S(1)}, bf16[4,192,192]{2,1,0:T(8,128)(2,1)S(1)}, u32[]{:S(2)}, u32[]{:S(2)}) collective-permute-start(bf16[4,192,192]{2,1,0:T(8,128)(2,1)S(1)} %copy-done.135), channel_id=1, source_target_pairs={{0,4},{1,5},{2,6},{3,7},{4,0},{5,1},{6,2},{7,3},{8,12},{9,13},{10,... | collective-permute-start | bytes 884744 | tf_op jit(solution)/shard_map/ppermute | solution.py:34
  755.4 5.4 collective-permute-start.120
  762.7 8.0 %collective-permute-done.126 = f32[2,384]{1,0:T(2,128)} collective-permute-done((f32[2,384]{1,0:T(2,128)S(1)}, f32[2,384]{1,0:T(2,128)}, u32[]{:S(2)}, u32[]{:S(2)}) %collective-permute-start.126) | collective-permute-done | bytes 3104 | tf_op jit(solution)/shard_map/ppermute | solution.py:34
  (718 shorter events, 256.1 us)
Async XLA Ops:
  2.3 12.6 %collective-permute-start.10 = (bf16[2052]{0:T(1024)(128)(2,1)S(1)}, bf16[2052]{0:T(1024)(128)(2,1)S(1)}, u32[]{:S(2)}, u32[]{:S(2)}) collective-permute-start(bf16[2052]{0:T(1024)(128)(2,1)S(1)} %concatenate.77), channel_id=1, source_target_pairs={{0,4},{1,5},{2,6},{3,7},{4,0},{5,1},{6,2},{7,3},{8,12},{9,13},{10,... | collective-permute-start | bytes 12320 | tf_op jit(solution)/shard_map/ppermute | solution.py:34
  5.6 15.2 %collective-permute-start.4 = (bf16[4,192,192]{2,1,0:T(8,128)(2,1)}, bf16[4,192,192]{2,1,0:T(8,128)(2,1)}, u32[]{:S(2)}, u32[]{:S(2)}) collective-permute-start(bf16[4,192,192]{2,1,0:T(8,128)(2,1)} %pad_maximum_fusion.10), channel_id=1, source_target_pairs={{0,16},{1,17},{2,18},{3,19},{4,20},{5,21},{6,22},{7,23},{8,24},{9,... | collective-permute-start | bytes 884744 | tf_op jit(solution)/shard_map/ppermute | solution.py:34
  9.0 35.8 %collective-permute-start.1 = (bf16[256,768]{1,0:T(8,128)(2,1)}, bf16[256,768]{1,0:T(8,128)(2,1)}, u32[]{:S(2)}, u32[]{:S(2)}) collective-permute-start(bf16[256,768]{1,0:T(8,128)(2,1)} %get-tuple-element.346), channel_id=1, source_target_pairs={{0,5},{1,4},{2,1},{3,0},{4,7},{5,6},{6,3},{7,2},{8,13},{9,12},{10,... | collective-permute-start | bytes 1179656 | tf_op jit(solution)/shard_map/ppermute | solution.py:34
  10.4 36.0 %collective-permute-start = (bf16[256,768]{1,0:T(8,128)(2,1)}, bf16[256,768]{1,0:T(8,128)(2,1)}, u32[]{:S(2)}, u32[]{:S(2)}) collective-permute-start(bf16[256,768]{1,0:T(8,128)(2,1)} %get-tuple-element.347), channel_id=1, source_target_pairs={{0,4},{1,5},{2,0},{3,1},{4,6},{5,7},{6,2},{7,3},{8,12},{9,13},{10,... | collective-permute-start | bytes 1179656 | tf_op jit(solution)/shard_map/ppermute | solution.py:34
  25.1 31.8 %collective-permute-start.5 = (bf16[768,768]{1,0:T(8,128)(2,1)}, bf16[768,768]{1,0:T(8,128)(2,1)}, u32[]{:S(2)}, u32[]{:S(2)}) collective-permute-start(bf16[768,768]{1,0:T(8,128)(2,1)} %broadcast_select_fusion.4), channel_id=1, source_target_pairs={{0,16},{1,17},{2,18},{3,19},{4,20},{5,21},{6,22},{7,23},{8,24},{9,... | collective-permute-start | bytes 3538952 | tf_op jit(solution)/shard_map/ppermute | solution.py:34
  42.0 13.5 %collective-permute-start.20 = (bf16[4,1,192,192]{3,2,0,1:T(8,128)(2,1)}, bf16[4,1,192,192]{3,2,0,1:T(8,128)(2,1)}, u32[]{:S(2)}, u32[]{:S(2)}) collective-permute-start(bf16[4,1,192,192]{3,2,0,1:T(8,128)(2,1)} %maximum_bitcast_fusion.3), channel_id=1, source_target_pairs={{0,8},{1,9},{2,10},{3,11},{4,12},{5,13},{6,14},{7,15},{8,0},{9,1},... | collective-permute-start | bytes 884744 | tf_op jit(solution)/shard_map/ppermute | solution.py:34
  46.4 15.3 %collective-permute-start.3 = (bf16[256,768]{1,0:T(8,128)(2,1)}, bf16[256,768]{1,0:T(8,128)(2,1)S(1)}, u32[]{:S(2)}, u32[]{:S(2)}) collective-permute-start(bf16[256,768]{1,0:T(8,128)(2,1)} %collective-permute-done.1.refs_1_), channel_id=1, source_target_pairs={{0,4},{1,5},{2,6},{3,7},{4,0},{5,1},{6,2},{7,3},{8,12},{9,13},{10,... | collective-permute-start | bytes 1179656 | tf_op jit(solution)/shard_map/ppermute | solution.py:34
  46.4 16.0 %collective-permute-start.2 = (bf16[256,768]{1,0:T(8,128)(2,1)}, bf16[256,768]{1,0:T(8,128)(2,1)}, u32[]{:S(2)}, u32[]{:S(2)}) collective-permute-start(bf16[256,768]{1,0:T(8,128)(2,1)} %collective-permute-done.refs_0_), channel_id=1, source_target_pairs={{0,4},{1,5},{2,6},{3,7},{4,0},{5,1},{6,2},{7,3},{8,12},{9,13},{10,... | collective-permute-start | bytes 1179656 | tf_op jit(solution)/shard_map/ppermute | solution.py:34
  55.5 13.1 %collective-permute-start.9 = (bf16[3,192,192]{2,1,0:T(8,128)(2,1)S(1)}, bf16[3,192,192]{2,1,0:T(8,128)(2,1)S(1)}, u32[]{:S(2)}, u32[]{:S(2)}) collective-permute-start(bf16[3,192,192]{2,1,0:T(8,128)(2,1)S(1)} %collective-permute-done.7.refs_5_), channel_id=1, source_target_pairs={{0,8},{1,9},{2,10},{3,11},{4,12},{5,13},{6,14},{7,15},{8,0},{9,1},... | collective-permute-start | bytes 663560 | tf_op jit(solution)/shard_map/ppermute | solution.py:34
  56.9 53.5 %collective-permute-start.21 = (bf16[4,2,192,192]{3,2,0,1:T(8,128)(2,1)S(1)}, bf16[4,2,192,192]{3,2,0,1:T(8,128)(2,1)}, u32[]{:S(2)}, u32[]{:S(2)}) collective-permute-start(bf16[4,2,192,192]{3,2,0,1:T(8,128)(2,1)S(1)} %pad_maximum_fusion.7), channel_id=1, source_target_pairs={{0,4},{1,5},{2,6},{3,7},{4,0},{5,1},{6,2},{7,3},{8,12},{9,13},{10,... | collective-permute-start | bytes 1769480 | tf_op jit(solution)/shard_map/ppermute | solution.py:34
  61.7 50.4 %collective-permute-start.16 = (bf16[768,768]{1,0:T(8,128)(2,1)}, bf16[768,768]{1,0:T(8,128)(2,1)S(1)}, u32[]{:S(2)}, u32[]{:S(2)}) collective-permute-start(bf16[768,768]{1,0:T(8,128)(2,1)} %get-tuple-element.301), channel_id=1, source_target_pairs={{0,6},{1,2},{2,4},{3,0},{4,5},{5,1},{6,7},{7,3},{8,14},{9,10},{10,... | collective-permute-start | bytes 3538952 | tf_op jit(solution)/shard_map/ppermute | solution.py:34
  62.4 30.1 %collective-permute-start.12 = (bf16[768,768]{1,0:T(8,128)(2,1)}, bf16[768,768]{1,0:T(8,128)(2,1)S(1)}, u32[]{:S(2)}, u32[]{:S(2)}) collective-permute-start(bf16[768,768]{1,0:T(8,128)(2,1)} %get-tuple-element.301), channel_id=1, source_target_pairs={{0,4},{1,0},{2,6},{3,2},{4,7},{5,3},{6,5},{7,1},{8,12},{9,8},{10,1... | collective-permute-start | bytes 3538952 | tf_op jit(solution)/shard_map/ppermute | solution.py:34
  94.9 17.3 %collective-permute-start.14 = (bf16[1024,192]{1,0:T(8,128)(2,1)S(1)}, bf16[1024,192]{1,0:T(8,128)(2,1)S(1)}, u32[]{:S(2)}, u32[]{:S(2)}) collective-permute-start(bf16[1024,192]{1,0:T(8,128)(2,1)S(1)} %copy-done.33), channel_id=1, source_target_pairs={{0,4},{1,5},{2,6},{3,7},{4,0},{5,1},{6,2},{7,3},{8,12},{9,13},{10,... | collective-permute-start | bytes 1179656 | tf_op jit(solution)/shard_map/ppermute | solution.py:34
  125.6 21.9 %collective-permute-start.22 = (bf16[320,384]{1,0:T(8,128)(2,1)S(1)}, bf16[320,384]{1,0:T(8,128)(2,1)S(1)}, u32[]{:S(2)}, u32[]{:S(2)}) collective-permute-start(bf16[320,384]{1,0:T(8,128)(2,1)S(1)} %get-tuple-element.161), channel_id=1, source_target_pairs={{0,1},{1,0},{2,3},{3,2},{4,5},{5,4},{6,7},{7,6},{8,9},{9,8},{10,11... | collective-permute-start | bytes 737288 | tf_op jit(solution)/shard_map/ppermute | solution.py:34
  140.8 12.9 %collective-permute-start.23 = (bf16[320,384]{1,0:T(8,128)(2,1)S(1)}, bf16[320,384]{1,0:T(8,128)(2,1)S(1)}, u32[]{:S(2)}, u32[]{:S(2)}) collective-permute-start(bf16[320,384]{1,0:T(8,128)(2,1)S(1)} %get-tuple-element.162), channel_id=1, source_target_pairs={{0,8},{1,9},{2,10},{3,11},{4,12},{5,13},{6,14},{7,15},{8,0},{9,1},... | collective-permute-start | bytes 737288 | tf_op jit(solution)/shard_map/ppermute | solution.py:34
  167.5 14.1 %collective-permute-start.30 = (bf16[640,384]{1,0:T(8,128)(2,1)S(1)}, bf16[640,384]{1,0:T(8,128)(2,1)S(1)}, u32[]{:S(2)}, u32[]{:S(2)}) collective-permute-start(bf16[640,384]{1,0:T(8,128)(2,1)S(1)} %add.239), channel_id=1, source_target_pairs={{0,16},{1,17},{2,18},{3,19},{4,20},{5,21},{6,22},{7,23},{8,24},{9,... | collective-permute-start | bytes 1474568 | tf_op jit(solution)/shard_map/ppermute | solution.py:34
  174.6 16.8 %collective-permute-start.35 = (bf16[640,384]{1,0:T(8,128)(2,1)S(1)}, bf16[640,384]{1,0:T(8,128)(2,1)S(1)}, u32[]{:S(2)}, u32[]{:S(2)}) collective-permute-start(bf16[640,384]{1,0:T(8,128)(2,1)S(1)} %add.241), channel_id=1, source_target_pairs={{0,16},{1,17},{2,18},{3,19},{4,20},{5,21},{6,22},{7,23},{8,24},{9,... | collective-permute-start | bytes 1474568 | tf_op jit(solution)/shard_map/ppermute | solution.py:34
  181.7 17.8 %collective-permute-start.33 = (bf16[320,384]{1,0:T(8,128)(2,1)S(1)}, bf16[320,384]{1,0:T(8,128)(2,1)S(1)}, u32[]{:S(2)}, u32[]{:S(2)}) collective-permute-start(bf16[320,384]{1,0:T(8,128)(2,1)S(1)} %get-tuple-element.357), channel_id=1, source_target_pairs={{0,1},{1,0},{2,3},{3,2},{4,5},{5,4},{6,7},{7,6},{8,9},{9,8},{10,11... | collective-permute-start | bytes 737288 | tf_op jit(solution)/shard_map/ppermute | solution.py:34
  196.0 13.1 %collective-permute-start.48 = (bf16[192,192]{1,0:T(8,128)(2,1)S(1)}, bf16[192,192]{1,0:T(8,128)(2,1)S(1)}, u32[]{:S(2)}, u32[]{:S(2)}) collective-permute-start(bf16[192,192]{1,0:T(8,128)(2,1)S(1)} %slice_bitcast_fusion.4), channel_id=1, source_target_pairs={{0,3},{1,2},{2,1},{3,0},{4,7},{5,6},{6,5},{7,4},{8,11},{9,10},{10,... | collective-permute-start | bytes 221192 | tf_op jit(solution)/shard_map/ppermute | solution.py:34
  209.2 24.4 %collective-permute-start.38 = (bf16[1024,384]{1,0:T(8,128)(2,1)S(1)}, bf16[1024,384]{1,0:T(8,128)(2,1)S(1)}, u32[]{:S(2)}, u32[]{:S(2)}) collective-permute-start(bf16[1024,384]{1,0:T(8,128)(2,1)S(1)} %shard_map.207.refs_2_), channel_id=1, source_target_pairs={{0,4},{1,5},{2,6},{3,7},{4,0},{5,1},{6,2},{7,3},{8,12},{9,13},{10,... | collective-permute-start | bytes 2359304 | tf_op jit(solution)/shard_map/ppermute | solution.py:34
  211.7 16.0 %collective-permute-start.39 = (bf16[3,192,192]{2,1,0:T(8,128)(2,1)S(1)}, bf16[3,192,192]{2,1,0:T(8,128)(2,1)}, u32[]{:S(2)}, u32[]{:S(2)}) collective-permute-start(bf16[3,192,192]{2,1,0:T(8,128)(2,1)S(1)} %copy-done.140), channel_id=1, source_target_pairs={{0,8},{1,9},{2,10},{3,11},{4,12},{5,13},{6,14},{7,15},{8,0},{9,1},... | collective-permute-start | bytes 663560 | tf_op jit(solution)/shard_map/ppermute | solution.py:34
  212.3 21.3 %collective-permute-start.40 = (bf16[3,192,192]{2,1,0:T(8,128)(2,1)S(1)}, bf16[3,192,192]{2,1,0:T(8,128)(2,1)S(1)}, u32[]{:S(2)}, u32[]{:S(2)}) collective-permute-start(bf16[3,192,192]{2,1,0:T(8,128)(2,1)S(1)} %copy-done.156), channel_id=1, source_target_pairs={{0,8},{1,9},{2,10},{3,11},{4,12},{5,13},{6,14},{7,15},{8,0},{9,1},... | collective-permute-start | bytes 663560 | tf_op jit(solution)/shard_map/ppermute | solution.py:34
  221.6 49.4 %collective-permute-start.50 = (bf16[4,2,192,192]{3,2,0,1:T(8,128)(2,1)S(1)}, bf16[4,2,192,192]{3,2,0,1:T(8,128)(2,1)}, u32[]{:S(2)}, u32[]{:S(2)}) collective-permute-start(bf16[4,2,192,192]{3,2,0,1:T(8,128)(2,1)S(1)} %pad_maximum_fusion.8), channel_id=1, source_target_pairs={{0,4},{1,5},{2,6},{3,7},{4,0},{5,1},{6,2},{7,3},{8,12},{9,13},{10,... | collective-permute-start | bytes 1769480 | tf_op jit(solution)/shard_map/ppermute | solution.py:34
  221.7 51.1 %collective-permute-start.45 = (bf16[768,768]{1,0:T(8,128)(2,1)}, bf16[768,768]{1,0:T(8,128)(2,1)S(1)}, u32[]{:S(2)}, u32[]{:S(2)}) collective-permute-start(bf16[768,768]{1,0:T(8,128)(2,1)} %get-tuple-element.176), channel_id=1, source_target_pairs={{0,6},{1,2},{2,4},{3,0},{4,5},{5,1},{6,7},{7,3},{8,14},{9,10},{10,... | collective-permute-start | bytes 3538952 | tf_op jit(solution)/shard_map/ppermute | solution.py:34
  227.7 28.3 %collective-permute-start.41 = (bf16[768,768]{1,0:T(8,128)(2,1)}, bf16[768,768]{1,0:T(8,128)(2,1)S(1)}, u32[]{:S(2)}, u32[]{:S(2)}) collective-permute-start(bf16[768,768]{1,0:T(8,128)(2,1)} %get-tuple-element.176), channel_id=1, source_target_pairs={{0,4},{1,0},{2,6},{3,2},{4,7},{5,3},{6,5},{7,1},{8,12},{9,8},{10,1... | collective-permute-start | bytes 3538952 | tf_op jit(solution)/shard_map/ppermute | solution.py:34
  258.8 14.0 %collective-permute-start.43 = (bf16[1024,192]{1,0:T(8,128)(2,1)S(1)}, bf16[1024,192]{1,0:T(8,128)(2,1)S(1)}, u32[]{:S(2)}, u32[]{:S(2)}) collective-permute-start(bf16[1024,192]{1,0:T(8,128)(2,1)S(1)} %copy-done.34), channel_id=1, source_target_pairs={{0,4},{1,5},{2,6},{3,7},{4,0},{5,1},{6,2},{7,3},{8,12},{9,13},{10,... | collective-permute-start | bytes 1179656 | tf_op jit(solution)/shard_map/ppermute | solution.py:34
  286.3 21.6 %collective-permute-start.51 = (bf16[320,384]{1,0:T(8,128)(2,1)S(1)}, bf16[320,384]{1,0:T(8,128)(2,1)S(1)}, u32[]{:S(2)}, u32[]{:S(2)}) collective-permute-start(bf16[320,384]{1,0:T(8,128)(2,1)S(1)} %get-tuple-element.186), channel_id=1, source_target_pairs={{0,1},{1,0},{2,3},{3,2},{4,5},{5,4},{6,7},{7,6},{8,9},{9,8},{10,11... | collective-permute-start | bytes 737288 | tf_op jit(solution)/shard_map/ppermute | solution.py:34
  301.1 12.9 %collective-permute-start.52 = (bf16[320,384]{1,0:T(8,128)(2,1)S(1)}, bf16[320,384]{1,0:T(8,128)(2,1)S(1)}, u32[]{:S(2)}, u32[]{:S(2)}) collective-permute-start(bf16[320,384]{1,0:T(8,128)(2,1)S(1)} %get-tuple-element.187), channel_id=1, source_target_pairs={{0,8},{1,9},{2,10},{3,11},{4,12},{5,13},{6,14},{7,15},{8,0},{9,1},... | collective-permute-start | bytes 737288 | tf_op jit(solution)/shard_map/ppermute | solution.py:34
  323.5 13.6 %collective-permute-start.61 = (bf16[256,768]{1,0:T(8,128)(2,1)S(1)}, bf16[256,768]{1,0:T(8,128)(2,1)S(1)}, u32[]{:S(2)}, u32[]{:S(2)}) collective-permute-start(bf16[256,768]{1,0:T(8,128)(2,1)S(1)} %get-tuple-element.338), channel_id=1, source_target_pairs={{0,5},{1,4},{2,1},{3,0},{4,7},{5,6},{6,3},{7,2},{8,13},{9,12},{10,... | collective-permute-start | bytes 1179656 | tf_op jit(solution)/shard_map/ppermute | solution.py:34
  324.2 22.4 %collective-permute-start.60 = (bf16[256,768]{1,0:T(8,128)(2,1)S(1)}, bf16[256,768]{1,0:T(8,128)(2,1)S(1)}, u32[]{:S(2)}, u32[]{:S(2)}) collective-permute-start(bf16[256,768]{1,0:T(8,128)(2,1)S(1)} %get-tuple-element.339), channel_id=1, source_target_pairs={{0,4},{1,5},{2,0},{3,1},{4,6},{5,7},{6,2},{7,3},{8,12},{9,13},{10,... | collective-permute-start | bytes 1179656 | tf_op jit(solution)/shard_map/ppermute | solution.py:34
  328.3 18.3 %collective-permute-start.65 = (bf16[640,384]{1,0:T(8,128)(2,1)S(1)}, bf16[640,384]{1,0:T(8,128)(2,1)S(1)}, u32[]{:S(2)}, u32[]{:S(2)}) collective-permute-start(bf16[640,384]{1,0:T(8,128)(2,1)S(1)} %get-tuple-element.196), channel_id=1, source_target_pairs={{0,4},{1,5},{2,6},{3,7},{4,0},{5,1},{6,2},{7,3},{8,12},{9,13},{10,... | collective-permute-start | bytes 1474568 | tf_op jit(solution)/shard_map/ppermute | solution.py:34
  328.7 19.6 %collective-permute-start.59 = (bf16[640,384]{1,0:T(8,128)(2,1)S(1)}, bf16[640,384]{1,0:T(8,128)(2,1)S(1)}, u32[]{:S(2)}, u32[]{:S(2)}) collective-permute-start(bf16[640,384]{1,0:T(8,128)(2,1)S(1)} %add.245), channel_id=1, source_target_pairs={{0,16},{1,17},{2,18},{3,19},{4,20},{5,21},{6,22},{7,23},{8,24},{9,... | collective-permute-start | bytes 1474568 | tf_op jit(solution)/shard_map/ppermute | solution.py:34
  346.7 13.7 %collective-permute-start.66 = (bf16[640,384]{1,0:T(8,128)(2,1)S(1)}, bf16[640,384]{1,0:T(8,128)(2,1)S(1)}, u32[]{:S(2)}, u32[]{:S(2)}) collective-permute-start(bf16[640,384]{1,0:T(8,128)(2,1)S(1)} %add.247), channel_id=1, source_target_pairs={{0,16},{1,17},{2,18},{3,19},{4,20},{5,21},{6,22},{7,23},{8,24},{9,... | collective-permute-start | bytes 1474568 | tf_op jit(solution)/shard_map/ppermute | solution.py:34
  349.2 14.1 %collective-permute-start.64 = (bf16[320,384]{1,0:T(8,128)(2,1)}, bf16[320,384]{1,0:T(8,128)(2,1)}, u32[]{:S(2)}, u32[]{:S(2)}) collective-permute-start(bf16[320,384]{1,0:T(8,128)(2,1)} %get-tuple-element.354), channel_id=1, source_target_pairs={{0,1},{1,0},{2,3},{3,2},{4,5},{5,4},{6,7},{7,6},{8,9},{9,8},{10,11... | collective-permute-start | bytes 737288 | tf_op jit(solution)/shard_map/ppermute | solution.py:34
  361.4 13.2 %collective-permute-start.67 = (bf16[320,384]{1,0:T(8,128)(2,1)}, bf16[320,384]{1,0:T(8,128)(2,1)}, u32[]{:S(2)}, u32[]{:S(2)}) collective-permute-start(bf16[320,384]{1,0:T(8,128)(2,1)} %get-tuple-element.331), channel_id=1, source_target_pairs={{0,8},{1,9},{2,10},{3,11},{4,12},{5,13},{6,14},{7,15},{8,0},{9,1},... | collective-permute-start | bytes 737288 | tf_op jit(solution)/shard_map/ppermute | solution.py:34
  419.4 14.1 %collective-permute-start.80 = (bf16[640,384]{1,0:T(8,128)(2,1)S(1)}, bf16[640,384]{1,0:T(8,128)(2,1)S(1)}, u32[]{:S(2)}, u32[]{:S(2)}) collective-permute-start(bf16[640,384]{1,0:T(8,128)(2,1)S(1)} %add.257), channel_id=1, source_target_pairs={{0,16},{1,17},{2,18},{3,19},{4,20},{5,21},{6,22},{7,23},{8,24},{9,... | collective-permute-start | bytes 1474568 | tf_op jit(solution)/shard_map/ppermute | solution.py:34
  420.9 22.3 %collective-permute-start.83 = (bf16[640,384]{1,0:T(8,128)(2,1)S(1)}, bf16[640,384]{1,0:T(8,128)(2,1)S(1)}, u32[]{:S(2)}, u32[]{:S(2)}) collective-permute-start(bf16[640,384]{1,0:T(8,128)(2,1)S(1)} %add.259), channel_id=1, source_target_pairs={{0,16},{1,17},{2,18},{3,19},{4,20},{5,21},{6,22},{7,23},{8,24},{9,... | collective-permute-start | bytes 1474568 | tf_op jit(solution)/shard_map/ppermute | solution.py:34
  433.6 23.5 %collective-permute-start.81 = (bf16[320,384]{1,0:T(8,128)(2,1)S(1)}, bf16[320,384]{1,0:T(8,128)(2,1)S(1)}, u32[]{:S(2)}, u32[]{:S(2)}) collective-permute-start(bf16[320,384]{1,0:T(8,128)(2,1)S(1)} %get-tuple-element.351), channel_id=1, source_target_pairs={{0,1},{1,0},{2,3},{3,2},{4,5},{5,4},{6,7},{7,6},{8,9},{9,8},{10,11... | collective-permute-start | bytes 737288 | tf_op jit(solution)/shard_map/ppermute | solution.py:34
  443.3 13.8 %collective-permute-start.85 = (bf16[320,384]{1,0:T(8,128)(2,1)S(1)}, bf16[320,384]{1,0:T(8,128)(2,1)S(1)}, u32[]{:S(2)}, u32[]{:S(2)}) collective-permute-start(bf16[320,384]{1,0:T(8,128)(2,1)S(1)} %get-tuple-element.328), channel_id=1, source_target_pairs={{0,9},{1,8},{2,11},{3,10},{4,13},{5,12},{6,15},{7,14},{8,1},{9,0},... | collective-permute-start | bytes 737288 | tf_op jit(solution)/shard_map/ppermute | solution.py:34
  460.1 31.0 %collective-permute-start.87 = (bf16[768,768]{1,0:T(8,128)(2,1)S(1)}, bf16[768,768]{1,0:T(8,128)(2,1)S(1)}, u32[]{:S(2)}, u32[]{:S(2)}) collective-permute-start(bf16[768,768]{1,0:T(8,128)(2,1)S(1)} %copy-done.152), channel_id=1, source_target_pairs={{0,1},{1,7},{2,3},{3,5},{4,0},{5,6},{6,2},{7,4},{8,9},{9,15},{10,1... | collective-permute-start | bytes 3538952 | tf_op jit(solution)/shard_map/ppermute | solution.py:34
  491.3 29.3 %collective-permute-start.90 = (bf16[768,768]{1,0:T(8,128)(2,1)}, bf16[768,768]{1,0:T(8,128)(2,1)S(1)}, u32[]{:S(2)}, u32[]{:S(2)}) collective-permute-start(bf16[768,768]{1,0:T(8,128)(2,1)} %get-tuple-element.228), channel_id=1, source_target_pairs={{0,3},{1,5},{2,1},{3,7},{4,2},{5,4},{6,0},{7,6},{8,11},{9,13},{10,... | collective-permute-start | bytes 3538952 | tf_op jit(solution)/shard_map/ppermute | solution.py:34
  495.0 25.6 %collective-permute-start.89 = (bf16[1024,384]{1,0:T(8,128)(2,1)S(1)}, bf16[1024,384]{1,0:T(8,128)(2,1)S(1)}, u32[]{:S(2)}, u32[]{:S(2)}) collective-permute-start(bf16[1024,384]{1,0:T(8,128)(2,1)S(1)} %add.262), channel_id=1, source_target_pairs={{0,16},{1,17},{2,18},{3,19},{4,20},{5,21},{6,22},{7,23},{8,24},{9,... | collective-permute-start | bytes 2359304 | tf_op jit(solution)/shard_map/ppermute | solution.py:34
  561.8 19.8 %collective-permute-start.101 = (bf16[1,2,4,192,192]{4,3,2,1,0:T(8,128)(2,1)}, bf16[1,2,4,192,192]{4,3,2,1,0:T(8,128)(2,1)}, u32[]{:S(2)}, u32[]{:S(2)}) collective-permute-start(bf16[1,2,4,192,192]{4,3,2,1,0:T(8,128)(2,1)} %broadcast_select_fusion.9), channel_id=1, source_target_pairs={{0,8},{1,9},{2,10},{3,11},{4,12},{5,13},{6,14},{7,15},{8,0},{9,1},... | collective-permute-start | bytes 1769480 | tf_op jit(solution)/shard_map/ppermute | solution.py:34
  562.9 18.7 %collective-permute-start.99 = (bf16[640,384]{1,0:T(8,128)(2,1)}, bf16[640,384]{1,0:T(8,128)(2,1)}, u32[]{:S(2)}, u32[]{:S(2)}) collective-permute-start(bf16[640,384]{1,0:T(8,128)(2,1)} %get-tuple-element.239), channel_id=1, source_target_pairs={{0,4},{1,5},{2,6},{3,7},{4,0},{5,1},{6,2},{7,3},{8,12},{9,13},{10,... | collective-permute-start | bytes 1474568 | tf_op jit(solution)/shard_map/ppermute | solution.py:34
  563.8 23.4 %collective-permute-start.104 = (bf16[640,384]{1,0:T(8,128)(2,1)}, bf16[640,384]{1,0:T(8,128)(2,1)}, u32[]{:S(2)}, u32[]{:S(2)}) collective-permute-start(bf16[640,384]{1,0:T(8,128)(2,1)} %add.267), channel_id=1, source_target_pairs={{0,16},{1,17},{2,18},{3,19},{4,20},{5,21},{6,22},{7,23},{8,24},{9,... | collective-permute-start | bytes 1474568 | tf_op jit(solution)/shard_map/ppermute | solution.py:34
  582.9 13.1 %collective-permute-start.100 = (bf16[640,384]{1,0:T(8,128)(2,1)S(1)}, bf16[640,384]{1,0:T(8,128)(2,1)S(1)}, u32[]{:S(2)}, u32[]{:S(2)}) collective-permute-start(bf16[640,384]{1,0:T(8,128)(2,1)S(1)} %add.264), channel_id=1, source_target_pairs={{0,16},{1,17},{2,18},{3,19},{4,20},{5,21},{6,22},{7,23},{8,24},{9,... | collective-permute-start | bytes 1474568 | tf_op jit(solution)/shard_map/ppermute | solution.py:34
  588.7 21.0 %collective-permute-start.106 = (bf16[320,384]{1,0:T(8,128)(2,1)S(1)}, bf16[320,384]{1,0:T(8,128)(2,1)S(1)}, u32[]{:S(2)}, u32[]{:S(2)}) collective-permute-start(bf16[320,384]{1,0:T(8,128)(2,1)S(1)} %get-tuple-element.326), channel_id=1, source_target_pairs={{0,9},{1,8},{2,11},{3,10},{4,13},{5,12},{6,15},{7,14},{8,1},{9,0},... | collective-permute-start | bytes 737288 | tf_op jit(solution)/shard_map/ppermute | solution.py:34
  590.4 19.3 %collective-permute-start.105 = (bf16[320,384]{1,0:T(8,128)(2,1)S(1)}, bf16[320,384]{1,0:T(8,128)(2,1)S(1)}, u32[]{:S(2)}, u32[]{:S(2)}) collective-permute-start(bf16[320,384]{1,0:T(8,128)(2,1)S(1)} %get-tuple-element.327), channel_id=1, source_target_pairs={{0,8},{1,9},{2,10},{3,11},{4,12},{5,13},{6,14},{7,15},{8,0},{9,1},... | collective-permute-start | bytes 737288 | tf_op jit(solution)/shard_map/ppermute | solution.py:34
  596.1 13.6 %collective-permute-start.102 = (bf16[320,384]{1,0:T(8,128)(2,1)S(1)}, bf16[320,384]{1,0:T(8,128)(2,1)S(1)}, u32[]{:S(2)}, u32[]{:S(2)}) collective-permute-start(bf16[320,384]{1,0:T(8,128)(2,1)S(1)} %get-tuple-element.348), channel_id=1, source_target_pairs={{0,1},{1,0},{2,3},{3,2},{4,5},{5,4},{6,7},{7,6},{8,9},{9,8},{10,11... | collective-permute-start | bytes 737288 | tf_op jit(solution)/shard_map/ppermute | solution.py:34
  612.6 21.9 %collective-permute-start.107 = (bf16[1024,384]{1,0:T(8,128)(2,1)S(1)}, bf16[1024,384]{1,0:T(8,128)(2,1)}, u32[]{:S(2)}, u32[]{:S(2)}) collective-permute-start(bf16[1024,384]{1,0:T(8,128)(2,1)S(1)} %shard_map.222.refs_0_), channel_id=1, source_target_pairs={{0,4},{1,5},{2,6},{3,7},{4,0},{5,1},{6,2},{7,3},{8,12},{9,13},{10,... | collective-permute-start | bytes 2359304 | tf_op jit(solution)/shard_map/ppermute | solution.py:34
  613.7 13.9 %collective-permute-start.74 = (bf16[256,768]{1,0:T(8,128)(2,1)S(1)}, bf16[256,768]{1,0:T(8,128)(2,1)}, u32[]{:S(2)}, u32[]{:S(2)}) collective-permute-start(bf16[256,768]{1,0:T(8,128)(2,1)S(1)} %get-tuple-element.309), channel_id=1, source_target_pairs={{0,3},{1,2},{2,7},{3,6},{4,1},{5,0},{6,5},{7,4},{8,11},{9,10},{10,... | collective-permute-start | bytes 1179656 | tf_op jit(solution)/shard_map/ppermute | solution.py:34
  628.7 33.6 %collective-permute-start.108 = (bf16[768,768]{1,0:T(8,128)(2,1)}, bf16[768,768]{1,0:T(8,128)(2,1)S(1)}, u32[]{:S(2)}, u32[]{:S(2)}) collective-permute-start(bf16[768,768]{1,0:T(8,128)(2,1)} %get-tuple-element.256), channel_id=1, source_target_pairs={{0,1},{1,7},{2,3},{3,5},{4,0},{5,6},{6,2},{7,4},{8,9},{9,15},{10,1... | collective-permute-start | bytes 3538952 | tf_op jit(solution)/shard_map/ppermute | solution.py:34
  662.3 16.5 %collective-permute-start.109 = (bf16[1024,384]{1,0:T(8,128)(2,1)}, bf16[1024,384]{1,0:T(8,128)(2,1)}, u32[]{:S(2)}, u32[]{:S(2)}) collective-permute-start(bf16[1024,384]{1,0:T(8,128)(2,1)} %get-tuple-element.258), channel_id=1, source_target_pairs={{0,4},{1,5},{2,6},{3,7},{4,0},{5,1},{6,2},{7,3},{8,12},{9,13},{10,... | collective-permute-start | bytes 2359304 | tf_op jit(solution)/shard_map/ppermute | solution.py:34
  665.0 19.6 %collective-permute-start.112 = (bf16[2,4,192,192]{3,2,1,0:T(8,128)(2,1)S(1)}, bf16[2,4,192,192]{3,2,1,0:T(8,128)(2,1)}, u32[]{:S(2)}, u32[]{:S(2)}) collective-permute-start(bf16[2,4,192,192]{3,2,1,0:T(8,128)(2,1)S(1)} %copy-done.114), channel_id=1, source_target_pairs={{4,6},{5,7},{6,4},{7,5},{12,14},{13,15},{14,12},{15,13},{16,17},{1... | collective-permute-start | bytes 1769480 | tf_op jit(solution)/shard_map/ppermute | solution.py:34
  667.0 46.0 %collective-permute-start.111 = (bf16[768,768]{1,0:T(8,128)(2,1)}, bf16[768,768]{1,0:T(8,128)(2,1)}, u32[]{:S(2)}, u32[]{:S(2)}) collective-permute-start(bf16[768,768]{1,0:T(8,128)(2,1)} %get-tuple-element.262), channel_id=1, source_target_pairs={{0,3},{1,5},{2,1},{3,7},{4,2},{5,4},{6,0},{7,6},{8,11},{9,13},{10,... | collective-permute-start | bytes 3538952 | tf_op jit(solution)/shard_map/ppermute | solution.py:34
  680.2 32.9 %collective-permute-start.110 = (bf16[1024,384]{1,0:T(8,128)(2,1)S(1)}, bf16[1024,384]{1,0:T(8,128)(2,1)}, u32[]{:S(2)}, u32[]{:S(2)}) collective-permute-start(bf16[1024,384]{1,0:T(8,128)(2,1)S(1)} %add.270), channel_id=1, source_target_pairs={{0,16},{1,17},{2,18},{3,19},{4,20},{5,21},{6,22},{7,23},{8,24},{9,... | collective-permute-start | bytes 2359304 | tf_op jit(solution)/shard_map/ppermute | solution.py:34
  683.4 31.1 %collective-permute-start.116 = (bf16[1,2,4,192,192]{4,3,2,1,0:T(8,128)(2,1)}, bf16[1,2,4,192,192]{4,3,2,1,0:T(8,128)(2,1)}, u32[]{:S(2)}, u32[]{:S(2)}) collective-permute-start(bf16[1,2,4,192,192]{4,3,2,1,0:T(8,128)(2,1)} %broadcast_select_fusion.8), channel_id=1, source_target_pairs={{0,8},{1,9},{2,10},{3,11},{4,12},{5,13},{6,14},{7,15},{8,0},{9,1},... | collective-permute-start | bytes 1769480 | tf_op jit(solution)/shard_map/ppermute | solution.py:34
  685.7 68.3 %collective-permute-start.119 = (bf16[4,192,192]{2,1,0:T(8,128)(2,1)S(1)}, bf16[4,192,192]{2,1,0:T(8,128)(2,1)}, u32[]{:S(2)}, u32[]{:S(2)}) collective-permute-start(bf16[4,192,192]{2,1,0:T(8,128)(2,1)S(1)} %select_bitcast_fusion.4), channel_id=1, source_target_pairs={{0,4},{1,5},{2,6},{3,7},{4,0},{5,1},{6,2},{7,3},{8,12},{9,13},{10,... | collective-permute-start | bytes 884744 | tf_op jit(solution)/shard_map/ppermute | solution.py:34
  719.7 55.5 %collective-permute-start.127 = (bf16[768,768]{1,0:T(8,128)(2,1)}, bf16[768,768]{1,0:T(8,128)(2,1)}, u32[]{:S(2)}, u32[]{:S(2)}) collective-permute-start(bf16[768,768]{1,0:T(8,128)(2,1)} %get-tuple-element.299), channel_id=1, source_target_pairs={{0,16},{1,17},{2,18},{3,19},{4,20},{5,21},{6,22},{7,23},{8,24},{9,... | collective-permute-start | bytes 3538952 | tf_op jit(solution)/shard_map/ppermute | solution.py:34
  732.1 16.6 %collective-permute-start.123 = (f32[2,4992]{1,0:T(2,128)S(1)}, f32[2,4992]{1,0:T(2,128)S(1)}, u32[]{:S(2)}, u32[]{:S(2)}) collective-permute-start(f32[2,4992]{1,0:T(2,128)S(1)} %pad_maximum_fusion.11), channel_id=1, source_target_pairs={{0,3},{1,2},{2,1},{3,0},{4,7},{5,6},{6,5},{7,4},{8,11},{9,10},{10,... | collective-permute-start | bytes 119816 | tf_op jit(solution)/shard_map/ppermute | solution.py:34
  738.1 16.0 %collective-permute-start.118 = (bf16[4,192,192]{2,1,0:T(8,128)(2,1)S(1)}, bf16[4,192,192]{2,1,0:T(8,128)(2,1)S(1)}, u32[]{:S(2)}, u32[]{:S(2)}) collective-permute-start(bf16[4,192,192]{2,1,0:T(8,128)(2,1)S(1)} %copy-done.135), channel_id=1, source_target_pairs={{0,4},{1,5},{2,6},{3,7},{4,0},{5,1},{6,2},{7,3},{8,12},{9,13},{10,... | collective-permute-start | bytes 884744 | tf_op jit(solution)/shard_map/ppermute | solution.py:34
  749.9 27.5 %collective-permute-start.114 = (bf16[256,768]{1,0:T(8,128)(2,1)}, bf16[256,768]{1,0:T(8,128)(2,1)S(1)}, u32[]{:S(2)}, u32[]{:S(2)}) collective-permute-start(bf16[256,768]{1,0:T(8,128)(2,1)} %get-tuple-element.306), channel_id=1, source_target_pairs={{0,2},{1,3},{2,6},{3,7},{4,0},{5,1},{6,4},{7,5},{8,10},{9,11},{10,... | collective-permute-start | bytes 1179656 | tf_op jit(solution)/shard_map/ppermute | solution.py:34
  753.3 24.1 %collective-permute-start.115 = (bf16[256,768]{1,0:T(8,128)(2,1)}, bf16[256,768]{1,0:T(8,128)(2,1)}, u32[]{:S(2)}, u32[]{:S(2)}) collective-permute-start(bf16[256,768]{1,0:T(8,128)(2,1)} %get-tuple-element.307), channel_id=1, source_target_pairs={{0,3},{1,2},{2,7},{3,6},{4,1},{5,0},{6,5},{7,4},{8,11},{9,10},{10,... | collective-permute-start | bytes 1179656 | tf_op jit(solution)/shard_map/ppermute | solution.py:34
  755.4 16.8 %collective-permute-start.120 = (bf16[4,192,192]{2,1,0:T(8,128)(2,1)S(1)}, bf16[4,192,192]{2,1,0:T(8,128)(2,1)S(1)}, u32[]{:S(2)}, u32[]{:S(2)}) collective-permute-start(bf16[4,192,192]{2,1,0:T(8,128)(2,1)S(1)} %select_convert_fusion.1), channel_id=1, source_target_pairs={{0,16},{1,17},{2,18},{3,19},{4,20},{5,21},{6,22},{7,23},{8,24},{9,... | collective-permute-start | bytes 884744 | tf_op jit(solution)/shard_map/ppermute | solution.py:34
  (230 other events, 2425.4 us)

commit v3 on v2

--- a/solution.py
+++ b/solution.py
@@ -133,8 +133,13 @@
             return (x, h, t >> 1, 2 * (1 - c) + (i ^ (t & 1)))
 
         got.append(send(at(pieces, 2 * (1 - c) + (i ^ (t & 1))), to))
-    low = t & 1
-    return jnp.stack([jnp.where(low == 0, got[0], got[1]), jnp.where(low == 0, got[1], got[0])])
+
+    def finish():
+        low = t & 1
+        first, second = jnp.where(low == 0, got[0], got[1]), jnp.where(low == 0, got[1], got[0])
+        return jnp.stack([first, second])
+
+    return tuple(got), finish
 
 
 def head_lanes(width, head):
@@ -189,29 +194,30 @@
 SMEM = pl.BlockSpec(memory_space=pltpu.SMEM)
 
 
-def attend_kernel(heads, mix, parts, *refs):
+def attend_kernel(heads, mix, orders, *refs):
     if mix:
         middle_ref, gate_ref, own_ref, other_ref, *refs = refs
     else:
         row_refs, refs = refs[:4], refs[4:]
-    part_refs, refs = refs[:parts], refs[parts:]
+    part_refs, refs = refs[: len(orders)], refs[len(orders) :]
     prefix_ref, gain_ref, base_ref, x_ref, normed_ref, qkv_ref, w_ref, *refs = refs
     o_ref, a_ref, strip, causal, scores_ref = refs
     block = pl.program_id(0)
     length, width = x_ref.shape
-    rows = o_ref.shape[0]
+    rows = a_ref.shape[1]
     span = base_ref.shape[1]
-    lanes_all = o_ref.shape[1]
+    lanes_all = o_ref.shape[1] // 2
 
     @pl.when(block == 0)
     def _():
         step = 256
-        for j, ref in enumerate(part_refs):
-            count = ref.shape[1]
-            first = (lax.axis_index("dp") ^ j) * count if parts > 1 else 0
-            first = pl.multiple_of(first, 8) if parts > 1 else 0
+        for ref, order in zip(part_refs, orders):
+            count = ref.shape[0]
+            first = 0
+            if order is not None:
+                first = pl.multiple_of((lax.axis_index("dp") ^ order) * count, 8)
             for v in range(3):
-                w_ref[v, pl.ds(first, count), :] = ref[v]
+                w_ref[v, pl.ds(first, count), :] = ref[:, v * lanes_all : (v + 1) * lanes_all]
         if not mix:
             for ref, piece in zip(row_refs, piece_order()):
                 count = ref.shape[0]
@@ -266,26 +272,36 @@
             weights = weights * (1.0 / jnp.sum(weights, -1, keepdims=True))
             a_ref[head, part, :] = weights.astype(BF16)
         out = jnp.where(head_lanes(lanes_all, head), dot(a_ref[head], values), out)
-    o_ref[...] = out.astype(BF16)
+    blocks = length // rows
+    place = pl.ds(pl.multiple_of(lax.rem(block, blocks // 2) * rows, rows), rows)
+
+    @pl.when(block < blocks // 2)
+    def _():
+        o_ref[place, :lanes_all] = out.astype(BF16)
+
+    @pl.when(block >= blocks // 2)
+    def _():
+        o_ref[place, lanes_all:] = out.astype(BF16)
 
 
 def attend(source, mix, prefix, gain, weights, base):
+    weights, orders = weights
     width = gain.shape[1]
     length = source[0].shape[0] * (1 if mix else 4)
-    lanes = weights[0].shape[2]
+    lanes = weights[0].shape[1] // 3
     heads = lanes // HEAD_DIM
     span = base.shape[1]
     inputs = [(part, None) for part in (*source, *weights)]
     inputs += [(prefix, SMEM), (gain, None), (base, None)]
     return call(
-        functools.partial(attend_kernel, heads, mix, len(weights)),
+        functools.partial(attend_kernel, heads, mix, orders),
         inputs,
         [
             (shape_of(length, width), None),
             (shape_of(length, width), None),
             (shape_of(3, length, lanes), None),
             (shape_of(3, width, lanes), None),
-            (shape_of(length, lanes), pl.BlockSpec((BLOCK, lanes), lambda i: (i, 0))),
+            (shape_of(length // 2, 2 * lanes), None),
             (
                 shape_of(heads, length, length),
                 pl.BlockSpec((heads, BLOCK, length), lambda i: (0, i, 0)),
@@ -361,10 +377,15 @@
     step = pl.program_id(0)
     rows = x_ref.shape[0]
 
-    @pl.when(step < steps)
-    def _():
+    def mix(side):
         member = which_member()
-        parts = [dot(ref[...], w_ref[member ^ j], (1, 1)) for j, ref in enumerate(piece_refs)]
+        half = piece_refs[0].shape[1] // 2
+        first = pl.multiple_of(lax.rem(step, steps // 2) * rows, rows)
+        lanes = slice(side * half, (side + 1) * half)
+        parts = [
+            dot(ref[pl.ds(first, rows), lanes], w_ref[member ^ j], (1, 1))
+            for j, ref in enumerate(piece_refs)
+        ]
         values = x_ref[...].astype(F32) + ((parts[0] + parts[1]) + (parts[2] + parts[3]))
         middle_ref[...] = values
         normed = (values * row_scale(values) * gain_ref[...]).astype(BF16)
@@ -373,6 +394,14 @@
         probs = router_probs(normed, router_ref, experts)
         gate_ref[...] = jnp.sum(probs * chosen_ref[...], -1, keepdims=True)
 
+    @pl.when(step < steps // 2)
+    def _():
+        mix(0)
+
+    @pl.when((step >= steps // 2) & (step < steps))
+    def _():
+        mix(1)
+
     dispatch_blocks(step, steps, slot_ref, kept, buffer_refs)
 
 
@@ -385,11 +414,10 @@
         return pl.BlockSpec((block, lanes), lambda i: (jnp.minimum(i, steps - 1), 0))
 
     buffers, grid = buffer_outputs(experts, slots, width // 2, steps)
-    lanes = pieces[0].shape[1]
     got = call(
         functools.partial(middle_kernel, experts, steps),
         [(rows, by_rows(width))]
-        + [(piece, by_rows(lanes)) for piece in pieces]
+        + [(piece, None) for piece in pieces]
         + [
             (weights, None),
             (gain, None),
@@ -533,23 +561,23 @@
 def expert_grads_kernel(count, *refs):
     own_refs, other_refs, refs = refs[:count], refs[count : 2 * count], refs[2 * count :]
     own_grads, other_grads, refs = refs[:count], refs[count : 2 * count], refs[2 * count :]
-    active_ref, hidden_ref, first_ref, second_ref = refs
+    active_ref, hidden_ref, first_ref, second_ref, inputs, grads = refs
     rows, half = own_refs[0].shape
     core = which_core()
-    for out, ref in enumerate((first_ref, second_ref)):
-        own_half = pl.ds(out * half, half)
-        for inputs, grads, side in (
-            (own_refs, own_grads, core),
-            (other_refs, other_grads, 1 - core),
-        ):
-            lanes = half_at(side, half)
-            up = jnp.zeros((half, half), F32)
-            down = jnp.zeros((half, half), F32)
-            for index in range(count):
-                part = pl.ds(index * rows, rows)
-                up += dot(inputs[index][...], hidden_ref[part, own_half], (0, 0))
-                down += dot(active_ref[part, own_half], grads[index][...], (0, 0))
+    for sources, gradients, side in (
+        (own_refs, own_grads, core),
+        (other_refs, other_grads, 1 - core),
+    ):
+        lanes = half_at(side, half)
+        for index in range(count):
+            part = pl.ds(index * rows, rows)
+            inputs[part, :] = sources[index][...]
+            grads[part, :] = gradients[index][...]
+        for out, ref in enumerate((first_ref, second_ref)):
+            own_half = pl.ds(out * half, half)
+            up = dot(inputs[...], hidden_ref[:, own_half], (0, 0))
             ref[pl.ds(0, half), lanes] = up.astype(BF16)
+            down = dot(active_ref[:, own_half], grads[...], (0, 0))
             ref[pl.ds(half, half), lanes] = down.astype(BF16)
 
 
@@ -561,6 +589,7 @@
         [(part, None) for part in own + other + own_grads + other_grads]
         + [(active, None), (hidden, None)],
         [(shape_of(2 * half, 2 * half), None)] * 2,
+        scratch=[pltpu.VMEM((rows * count, half), BF16)] * 2,
         vmem=58,
     )
 
@@ -787,18 +816,22 @@
 
 
 def head_grads_kernel(normed_ref, dp_ref, low_ref, own_ref, out_ref):
+    lanes = dp_ref.shape[2]
     for v in range(3):
-        out_ref[v] = dot(normed_ref[...], dp_ref[v], (0, 0)).astype(BF16)
-    out_ref[3] = dot(low_ref[...], own_ref[...], (0, 0)).astype(BF16)
+        part = dot(normed_ref[...], dp_ref[v], (0, 0))
+        out_ref[:, v * lanes : (v + 1) * lanes] = part.astype(BF16)
+    half = own_ref.shape[0]
+    part = dot(low_ref[:half, :], own_ref[:, :lanes], (0, 0))
+    part += dot(low_ref[half:, :], own_ref[:, lanes:], (0, 0))
+    out_ref[:, 3 * lanes :] = part.astype(BF16)
 
 
 def head_weight_grads(normed, dp, low, own):
-    length, width = normed.shape
-    lanes = own.shape[1]
+    width = normed.shape[1]
     return call(
         head_grads_kernel,
         [(value, None) for value in (normed, dp, low, own)],
-        [(shape_of(4, width, lanes), None)],
+        [(shape_of(width, 4 * dp.shape[2]), None)],
         vmem=58,
     )[0]
 
@@ -845,7 +878,7 @@
     )
 
 
-def query_weights(pieces, before_hosts=()):
+def to_own_quarter(pieces):
     x, _, c, _ = place()
 
     def to(x, h, c, t):
@@ -854,21 +887,30 @@
     def across(x, h, c, t):
         return (x, h, 1 - c, t ^ (x + 2 * (1 - c)))
 
-    own = jnp.where(x + 2 * c == 0, pieces, send(pieces, to))
-    other = send(pieces, across)
-    own, other = after((own, other), before_hosts)
+    return jnp.where(x + 2 * c == 0, pieces, send(pieces, to)), send(pieces, across)
+
+
+def query_weights(own, other):
     if lax.axis_size("dp") == 4:
-        return [own, other, host_swap(own, 1), host_swap(other, 1)]
-    both = ordered(c, own, other, 1)
-    return [rows_over_hosts(both[:, None], 1).reshape(3, -1, pieces.shape[2])]
-
-
-def out_weights(piece):
+        return [own, other, host_swap(own, 1), host_swap(other, 1)], (0, 1, 2, 3)
     _, _, c, _ = place()
-    four = jnp.stack([piece] + [tensor_swap(piece, j) for j in (1, 2, 3)])
-    four = rows_over_hosts(four[:, None], 1)
-    four = ordered(c, four[:, :, None], core_swap(four)[:, :, None], 2)
-    return four.reshape(4, -1, piece.shape[1])
+    both = ordered(c, own[None], other[None], 0)
+    return [rows_over_hosts(both[None], 0).reshape(-1, own.shape[1])], (None,)
+
+
+def over_quarters(piece):
+    half = piece.shape[0] // 2
+    piece = jnp.concatenate([piece[:half], piece[half:]], 1)
+    return jnp.stack([piece] + [tensor_swap(piece, j) for j in (1, 2, 3)])
+
+
+def out_weights(four):
+    _, _, c, _ = place()
+    hosts = rows_over_hosts(four[:, None], 1)
+    whole = ordered(c, hosts[:, :, None], core_swap(hosts)[:, :, None], 2)
+    lanes = whole.shape[4] // 2
+    halves = jnp.stack([whole[..., :lanes], whole[..., lanes:]], 3)
+    return halves.reshape(4, -1, lanes)
 
 
 def weights_out(i):
@@ -922,10 +964,12 @@
 
 
 def after(values, earlier):
+    if not jax.tree.leaves(earlier):
+        return values
     return lax.optimization_barrier((values, earlier))[0]
 
 
-def from_expert(parts, slot_column, experts, at_sums=(), at_combine=()):
+def from_expert(parts, slot_column, experts, at_upper=(), at_lower=(), at_combine=()):
     if len(parts) == 2:
         keep, give = parts
         chip = add(keep, core_swap(give))
@@ -938,8 +982,7 @@
     back = {}
     for first, chip in ((split, chips[0]), (0, chips[1])):
         other = section_swap(chip)
-        if not first:
-            other = after(other, at_sums)
+        other = after(other, at_upper if first else at_lower)
         count = chip.shape[0] // split
         for j in range(first + split - 1, first - 1, -1):
             piece = slice((j - first) * count, (j - first + 1) * count)
@@ -967,15 +1010,15 @@
         rows, pieces, out_pieces, gain_two, router, chosen, slot, experts, slots
     )
     arrived = to_expert(buffers, experts)
-    at_sums, at_combine = during(arrived[0])
+    gates = during(tuple(arrived[0]))
     active, slope, parts = expert_rows(*arrived, packs)
-    produced = from_expert(parts, slot_column, experts, at_sums, at_combine)
+    produced = from_expert(parts, slot_column, experts, *gates)
     saved = (rows, normed, qkv, qkv_weights, own, weights, middle, normed_two, gate)
     return saved, (arrived, active, slope), produced
 
 
 def layer_backward(
-    layer, grad, forward, params, attention, packs, experts, slots, during, at_chip
+    layer, grad, forward, params, attention, packs, experts, slots, during, before_total
 ):
     gain_one, base, prefix, gain_two, router, chosen, slot, slot_column = params
     out_pieces = attention[1]
@@ -987,51 +1030,52 @@
     )
     grad_logits = got[-1]
     grad_arrived = to_expert(buffers, experts)
-    at_sums, at_combine = during(grad_arrived[0], got[0])
+    at_lower = during(tuple(grad_arrived[0]))
     hidden, parts = expert_rows_back(*grad_arrived, slope, packs)
     expert_grads = expert_weight_grads(*arrived, *grad_arrived, active, hidden)
+    first = send(expert_grads[0], weights_home(0))
     grad_normed_two = from_expert(
-        parts, slot_column, experts, at_sums, (expert_grads, at_combine)
-    )
-    expert_grads = after(tuple(expert_grads), grad_normed_two[0])
-    expert_grads = tuple(send(part, weights_home(i)) for i, part in enumerate(expert_grads))
+        parts, slot_column, experts, tuple(expert_grads), at_lower, first
+    )
+    second = send(after(expert_grads[1], grad_normed_two[0]), weights_home(1))
     grad_router = dot(normed_two, grad_logits, (0, 0))[:, :experts]
-    mid, low, grad_gain_two, dp, diagonal, keep, give = attend_back(
-        *grad_normed_two,
-        grad_logits,
-        router,
-        middle,
-        grad,
-        gain_two,
-        out_pieces,
-        qkv,
-        weights,
-        qkv_weights,
-    )
-    keep, give = after((keep, give), expert_grads[0])
+    mid, low, grad_gain_two, dp, diagonal, keep, give = after(
+        attend_back(
+            *grad_normed_two,
+            grad_logits,
+            router,
+            middle,
+            grad,
+            gain_two,
+            out_pieces,
+            qkv,
+            weights,
+            qkv_weights,
+        ),
+        second,
+    )
     chip = add(keep, core_swap(give))
     head_grads = head_weight_grads(normed, dp, low, own)
-    at_total = at_chip(grad_normed_two[0])
-    total = add(chip, after(section_swap(chip), (head_grads, expert_grads[1], at_total)))
+    heads, at_total = before_total(head_grads, got[0])
+    total = add(chip, after(section_swap(chip), (head_grads, at_total)))
     grad_rows, grad_gain_one = rows_back(total, core_swap(total), rows, gain_one, mid)
     small = (grad_gain_one[0], grad_gain_two[0], grad_router, diagonal)
-    return grad_rows, expert_grads, head_grads, small, total
-
-
-def over_rows(grads, earlier=()):
+    return grad_rows, (first, second), heads, small, total
+
+
+def over_rows(grads):
     _, h, _, _ = place()
     hosts = lax.axis_size("dp") // 2
-    parts = grads.reshape(4, hosts, 2, -1, grads.shape[2])
-    parts = jnp.transpose(parts, (1, 2, 0, 3, 4))
+    parts = grads.reshape(hosts, 2, -1, grads.shape[1])
     bit = hosts // 2
     while bit:
         pair = parts.reshape(2, bit, *parts.shape[1:])
         upper = (h & bit) != 0
         keep = jnp.where(upper, pair[1], pair[0])
-        give = jnp.where(upper, pair[0], pair[1])
-        parts = add(keep, after(host_swap(give, bit), earlier))
+        arrived = host_swap(jnp.where(upper, pair[0], pair[1]), bit)
+        parts = add(keep, arrived)
         bit //= 2
-    return parts[0]
+    return arrived, lambda earlier: add(keep, after(arrived, earlier))[0]
 
 
 def to_quarter(part):
@@ -1087,10 +1131,12 @@
     heads = head_count // 4
     capacity = (5 * length + 4 * experts - 1) // (4 * experts)
 
+    rows = to_groups(block_input)
     pieces = jnp.concatenate(
-        [query_key_value_weights[0], attention_output_weights[0].T[None]], 0
-    )
-    other = section_swap(pieces)
+        [query_key_value_weights[0, v] for v in range(3)] + [attention_output_weights[0].T], 1
+    )
+    early = section_swap(pieces)
+    other = after(early, tuple(rows[:2]))
     pieces = pick(x, (pieces, other), (other, pieces))
     scale = 32
     packed = jnp.concatenate(
@@ -1122,10 +1168,8 @@
     lower = pack(up[:, :half], down[:half])
     upper = pack(up[:, half:], down[half:])
     keep = jnp.where(x == 0, lower, upper)
-    other = section_swap(after(jnp.where(x == 0, upper, lower), pieces))
+    other = section_swap(after(jnp.where(x == 0, upper, lower), early))
     packs = pick(x, (keep, other), (other, keep))
-
-    rows = to_groups(block_input)
 
     bucket_onehot = (
         relative_buckets[:, None] == jnp.arange(buckets, dtype=jnp.int32)[None, :]
@@ -1166,19 +1210,23 @@
         )
 
     params = [unpack(vector) for vector in packed]
-    got = tuple(rows[:2])
-    queries_zero = query_weights(pieces[0][:3], got)
-    outs_zero = out_weights(after(pieces[0][3], pieces[0]))
+    lanes = 3 * heads * HEAD_DIM
+    queries_zero = query_weights(*to_own_quarter(pieces[0][:, :lanes]))
+    outs_zero = out_weights(over_quarters(pieces[0][:, lanes:]))
     packs_zero = expert_weights(packs[0])
     slots = experts * capacity
     rows = after(tuple(rows), packs[0])
     later = {}
 
     def during_zero(arrived):
-        arrived = tuple(arrived)
-        later["queries"] = query_weights(after(pieces[1][:3], arrived))
-        later["outs"] = out_weights(after(pieces[1][3], arrived))
-        return tuple(later["queries"][:2]), ()
+        piece = after(pieces[1], arrived)
+        own, other = to_own_quarter(piece[:, :lanes])
+        four = over_quarters(piece[:, lanes:])
+        hosts = query_weights(own, other)
+        later["queries"] = hosts
+        later["outs"] = out_weights(four)
+        later["first"] = send(after(packs[1], (arrived, own, other)), weights_out(0))
+        return (own, other, four), (tuple(hosts[0]), later["first"]), ()
 
     zero = layer_forward(
         rows,
@@ -1189,53 +1237,51 @@
         slots,
         False,
         packs_zero[0],
-        packs_zero[1],
+        (),
         during_zero,
     )
-    packs_one = expert_weights(after(packs[1], zero[2][0]))
-
+    second = send(after(packs[1], zero[2][0]), weights_out(1))
+    packs_one = [later["first"], second]
+    outs_one = later["outs"]
     def during_one(arrived):
-        later["top"] = to_groups(after(cotangent, tuple(arrived)))
-        return tuple(later["top"]), ()
+        later["top"] = to_groups(after(cotangent, arrived))
+        return (), (), tuple(later["top"][:2])
 
     one = layer_forward(
         (zero[0][6], zero[0][8], *zero[2]),
         params[1],
-        (later["queries"], later["outs"]),
+        (later["queries"], outs_one),
         packs_one,
         experts,
         slots,
         True,
-        packs_one[0],
-        packs_one[1],
+        second,
+        (),
         during_one,
     )
     top = whole_rows(later["top"])
 
-    def during_back_one(arrived, result):
-        outputs = after(jnp.where(x == 0, one[0][0], result), tuple(arrived))
-        later["outputs"] = from_groups(outputs)
-        return later["outputs"], ()
+    def before_total_one(heads, result):
+        arrived, heads = over_rows(heads)
+        outputs, finish = from_groups(jnp.where(x == 0, one[0][0], result))
+        later["outputs"] = finish
+        return heads(()), (arrived, outputs)
 
     grads_one = layer_backward(
         1,
         top,
         one,
         params[1],
-        (None, later["outs"]),
+        (None, outs_one),
         packs_one,
         experts,
         slots,
-        during_back_one,
-        lambda returned: (),
-    )
-
-    def during_back_zero(arrived, _):
-        later["heads"] = over_rows(after(grads_one[2], tuple(arrived)))
-        return later["heads"], ()
-
-    def at_total_zero(returned):
-        later["heads"] = to_quarter(after(later["heads"], returned))
+        lambda arrived: (),
+        before_total_one,
+    )
+
+    def during_back_zero(arrived):
+        later["heads"] = to_quarter(after(grads_one[2], arrived))
         return later["heads"]
 
     grads_zero = layer_backward(
@@ -1248,9 +1294,9 @@
         experts,
         slots,
         during_back_zero,
-        at_total_zero,
-    )
-    outputs = later["outputs"]
+        lambda heads, _: (over_rows(heads)[1], ()),
+    )
+    outputs = later["outputs"]()
 
     def summed(pair):
         return pair[0].astype(F32) + pair[1].astype(F32)
@@ -1258,10 +1304,10 @@
     expert_zero = summed(after(grads_zero[1], grads_zero[4]))
     own, other = for_own_layer(expert_zero, summed(grads_one[1]))
     expert_own, expert_other = unpack_pair(own), unpack_pair(other.astype(F32))
-    heads_zero = over_cores(to_quarter(over_rows(grads_zero[2], grads_zero[4])))
+    heads_zero = over_cores(to_quarter(grads_zero[2](grads_zero[4])))
     own, other = for_own_layer(heads_zero, over_cores(later["heads"]))
     heads_grad = own + other.astype(F32)
-    grad_rows = from_groups(jnp.where(x == 0, grads_zero[0], grads_one[0]))
+    grad_rows = from_groups(jnp.where(x == 0, grads_zero[0], grads_one[0]))[1]()
 
     def flat(small):
         gain_one, gain_two, router, diagonal = small
@@ -1286,8 +1332,9 @@
 
     grad_up = ordered(x, expert_own[0], expert_other[0], 1)
     grad_down = ordered(x, expert_own[1], expert_other[1], 0)
-    grad_in = heads_grad[:3]
-    grad_out = heads_grad[3].T
+    wide = heads * HEAD_DIM
+    grad_in = jnp.stack([heads_grad[:, v * wide : (v + 1) * wide] for v in range(3)])
+    grad_out = heads_grad[:, 3 * wide :].T
 
     return (
         outputs[None],

time: 791 us -> 698 us (0.88)
  starting transfers between devices: 223 us -> 165 us
  waiting for transfers between devices: 234 us -> 216 us
  other arithmetic: 58.3 us -> 48.8 us
  local copies, waits for them, and re-layouts: 58.2 us -> 49.2 us
    ppermute x128, starting transfers between devices: 223 us -> 165 us  [send(): return lax.ppermute(value, AXES, pairs)]
    ppermute x128, waiting for transfers between devices: 234 us -> 216 us  [send(): return lax.ppermute(value, AXES, pairs)]
    unnamed x341 -> x337, local copies, waits for them, and re-layouts: 38.3 us -> 32.6 us
  transfers between devices with their start and end apart: 128 -> 128, of which waited for: 51 -> 55; matrix products, arithmetic and copies ran while one was open for 10% -> 10% of each run, Pallas kernels for 17% -> 22%
where the time goes in v3:
time: 698 us; the launch traced here: 689 us
  waiting for transfers between devices  216 us (31%)
  Pallas kernels  200 us (29%)
  starting transfers between devices  165 us (24%)
  local copies, waits for them, and re-layouts  49.2 us (7%)
  other arithmetic  48.8 us (7%)
    ppermute x128, waiting for transfers between devices, send(): return lax.ppermute(value, AXES, pairs)  216 us
    pallas_call x22, Pallas kernels, call(): pl.pallas_call(kernel, grid=grid, in_specs=[spec(item) for item in inputs...  200 us
    ppermute x128, starting transfers between devices, send(): return lax.ppermute(value, AXES, pairs)  165 us
    unnamed x337, local copies, waits for them, and re-layouts  32.6 us
  transfers between devices with their start and end apart: 128, of which 55 were waited for; matrix products, arithmetic and copies ran while one was open for 10% of the time, Pallas kernels for 22%

profile of v3, /device:TPU:0, one launch (start us, length us, event | category | flops | bytes accessed | tf_op | source)
XLA Modules:
  0.0 688.7 jit_solution(3811253894926767488)
XLA Ops:
  23.5 8.0 %collective-permute-done.refs_0_ = bf16[256,768]{1,0:T(8,128)(2,1)} collective-permute-done((bf16[256,768]{1,0:T(8,128)(2,1)}, bf16[256,768]{1,0:T(8,128)(2,1)}, u32[]{:S(2)}, u32[]{:S(2)}) %collective-permute-start) | collective-permute-done | bytes 393248 | tf_op jit(solution)/shard_map/ppermute | solution.py:34
  33.8 4.3 collective-permute-start.18
  39.2 3.2 collective-permute-done.18
  60.1 20.1 %shard_map.204 = (bf16[1024,768]{1,0:T(8,128)(2,1)}, bf16[1024,768]{1,0:T(8,128)(2,1)}, bf16[3,1024,192]{2,1,0:T(8,128)(2,1)}, bf16[3,768,192]{2,1,0:T(8,128)(2,...) custom-call(bf16[256,768]{1,0:T(8,128)(2,1)} %collective-permute-done.refs_0_, ...), custom_call_target="tpu_custom_call" | custom-call | flops 99999997952 | bytes 1000 | tf_op jit(solution)/shard_map/pallas_call | solution.py:178
  80.2 6.9 %collective-permute-start.13 = (bf16[512,384]{1,0:T(8,128)(2,1)}, bf16[512,384]{1,0:T(8,128)(2,1)S(1)}, u32[]{:S(2)}, u32[]{:S(2)}) collective-permute-start(bf16[512,384]{1,0:T(8,128)(2,1)} %get-tuple-element.144.refs_1_.own_ref), channel_id=1, source_target_pairs={{0,16},{1,17},{2,18},{3,19},{4,20},{5,21},{6,22},{7,23},{8,24},{9,... | collective-permute-start | bytes 1179656 | tf_op jit(solution)/shard_map/ppermute | solution.py:34
  91.7 3.3 collective-permute-done.13.refs_2_
  99.0 7.8 %shard_map.205 = (f32[1024,768]{1,0:T(8,128)S(1)}, bf16[1024,768]{1,0:T(8,128)(2,1)S(1)}, f32[1024,1]{1,0:T(8,128)S(1)}, bf16[320,384]{1,0:T(8,128)(2,1)S(1)}, b...) custom-call(bf16[1024,768]{1,0:T(8,128)(2,1)S(1)} %copy-done.3, ...), custom_call_target="tpu_custom_call" | custom-call | flops 1000000000 | bytes 1000 | tf_op jit(solution)/shard_map/pallas_call | solution.py:178
  113.9 7.5 %collective-permute-done.21.refs_1_ = bf16[320,384]{1,0:T(8,128)(2,1)S(1)} collective-permute-done((bf16[320,384]{1,0:T(8,128)(2,1)S(1)}, bf16[320,384]{1,0:T(8,128)(2,1)S(1)}, u32[]{:S(2)}, u32[]{:S(2)}) %collective-permute-start.21) | collective-permute-done | bytes 245792 | tf_op jit(solution)/shard_map/ppermute | solution.py:34
  121.9 5.7 collective-permute-done.23.refs_3_
  128.4 4.0 collective-permute-start.32
  132.5 8.0 %shard_map.206 = (bf16[1280,768]{1,0:T(8,128)(2,1)S(1)}, bf16[1280,768]{1,0:T(8,128)(2,1)S(1)}, bf16[640,384]{1,0:T(8,128)(2,1)S(1)}, bf16[640,384]{1,0:T(8,128)...) custom-call(bf16[320,384]{1,0:T(8,128)(2,1)S(1)} %get-tuple-element.147.refs_0_, ...), custom_call_target="tpu_custom_call" | custom-call | flops 1000000000 | bytes 1000 | tf_op jit(solution)/shard_map/pallas_call | solution.py:178
  153.3 7.8 %collective-permute-done.38 = bf16[640,384]{1,0:T(8,128)(2,1)} collective-permute-done((bf16[640,384]{1,0:T(8,128)(2,1)}, bf16[640,384]{1,0:T(8,128)(2,1)}, u32[]{:S(2)}, u32[]{:S(2)}) %collective-permute-start.38) | collective-permute-done | bytes 491552 | tf_op jit(solution)/shard_map/ppermute | solution.py:34
  165.8 5.5 collective-permute-done.30
  174.4 3.0 collective-permute-start.40
  178.1 3.7 collective-permute-start.41
  181.8 2.9 shard_map.207.refs_2_
  184.8 3.9 collective-permute-done.41
  190.2 6.8 collective-permute-done.49
  197.3 3.0 collective-permute-start.45
  201.2 22.0 %shard_map.208 = (bf16[1024,768]{1,0:T(8,128)(2,1)}, bf16[1024,768]{1,0:T(8,128)(2,1)}, bf16[3,1024,192]{2,1,0:T(8,128)(2,1)}, bf16[3,768,192]{2,1,0:T(8,128)(2,...) custom-call(f32[1024,768]{1,0:T(8,128)} %copy-done.30, f32[1024,1]{1,0:T(8,128)} %copy-done.84, ...), custom_call_target="tpu_custom_call" | custom-call | flops 99999997952 | bytes 1000 | tf_op jit(solution)/shard_map/pallas_call | solution.py:178
  226.4 3.1 collective-permute-start.47
  229.5 4.3 collective-permute-done.46.refs_2_
  238.9 7.8 %shard_map.209 = (f32[1024,768]{1,0:T(8,128)S(1)}, bf16[1024,768]{1,0:T(8,128)(2,1)S(1)}, f32[1024,1]{1,0:T(8,128)S(1)}, bf16[320,384]{1,0:T(8,128)(2,1)S(1)}, b...) custom-call(bf16[1024,768]{1,0:T(8,128)(2,1)S(1)} %copy-done, ...), custom_call_target="tpu_custom_call" | custom-call | flops 1000000000 | bytes 1000 | tf_op jit(solution)/shard_map/pallas_call | solution.py:178
  250.9 3.0 collective-permute-start.53
  253.9 5.3 collective-permute-done.51.refs_1_
  259.7 3.8 collective-permute-done.53.refs_3_
  265.0 7.3 %shard_map.210 = (bf16[1280,768]{1,0:T(8,128)(2,1)S(1)}, bf16[1280,768]{1,0:T(8,128)(2,1)S(1)}, bf16[640,384]{1,0:T(8,128)(2,1)S(1)}, bf16[640,384]{1,0:T(8,128)...) custom-call(bf16[320,384]{1,0:T(8,128)(2,1)S(1)} %get-tuple-element.165.refs_0_, ...), custom_call_target="tpu_custom_call" | custom-call | flops 1000000000 | bytes 1000 | tf_op jit(solution)/shard_map/pallas_call | solution.py:178
  281.6 6.9 %collective-permute-done.59 = bf16[640,384]{1,0:T(8,128)(2,1)S(1)} collective-permute-done((bf16[640,384]{1,0:T(8,128)(2,1)S(1)}, bf16[640,384]{1,0:T(8,128)(2,1)S(1)}, u32[]{:S(2)}, u32[]{:S(2)}) %collective-permute-start.59) | collective-permute-done | bytes 491552 | tf_op jit(solution)/shard_map/ppermute | solution.py:34
  291.6 7.0 %collective-permute-done.64 = bf16[640,384]{1,0:T(8,128)(2,1)S(1)} collective-permute-done((bf16[640,384]{1,0:T(8,128)(2,1)S(1)}, bf16[640,384]{1,0:T(8,128)(2,1)S(1)}, u32[]{:S(2)}, u32[]{:S(2)}) %collective-permute-start.64) | collective-permute-done | bytes 491552 | tf_op jit(solution)/shard_map/ppermute | solution.py:34
  304.3 3.9 collective-permute-done.66.refs_4_
  308.2 5.2 collective-permute-done.65.refs_3_
  316.3 5.2 shard_map.211.refs_2_
  325.7 6.5 shard_map.212
  337.5 5.3 collective-permute-done.72.refs_1_.refs_9_
  342.7 5.9 collective-permute-done.73.refs_2_.refs_10_
  350.5 7.4 %shard_map.213 = (bf16[1280,768]{1,0:T(8,128)(2,1)S(1)}, bf16[640,384]{1,0:T(8,128)(2,1)S(1)}, bf16[640,384]{1,0:T(8,128)(2,1)}, bf16[640,384]{1,0:T(8,128)(2,1)S(1)}, bf16[640,384]{1,0:T(8,128)(2,1)S(1)}) custom-call(bf16[320,384]{1,0:T(8,128)(2,1)S(1)} %get-tuple-element.178.refs_0_.refs_8_, bf16[320,384]{1,0:T(8,128)(2,1)S(1)} %collective-permute-done.72.refs_1_.refs_9_, ...), custom_call_target="tpu_custom_call" | custom-call | flops 1000000000 | bytes 1000 | tf_op jit(solution)/shard_map/pallas_call | solution.py:178
  362.8 8.8 %shard_map.214 = (bf16[768,768]{1,0:T(8,128)(2,1)}, bf16[768,768]{1,0:T(8,128)(2,1)}) custom-call(bf16[320,384]{1,0:T(8,128)(2,1)} %copy-done.56, bf16[320,384]{1,0:T(8,128)(2,1)} %copy-done.57, bf16[320,384]{1,0:T(8,128)(2,1)} %copy-done.58, bf16[320,384]{1,0:T(8,128)(2,1)} %copy-done.59, bf16[320,384]{1,0:T(8,128)(2,1)} %copy-done.60, ...), custom_call_target="tpu_custom_call" | custom-call | flops 1000000000 | bytes 1000 | tf_op jit(solution)/shard_map/pallas_call | solution.py:178
  375.2 10.3 %collective-permute-done.84 = bf16[640,384]{1,0:T(8,128)(2,1)S(1)} collective-permute-done((bf16[640,384]{1,0:T(8,128)(2,1)S(1)}, bf16[640,384]{1,0:T(8,128)(2,1)S(1)}, u32[]{:S(2)}, u32[]{:S(2)}) %collective-permute-start.84) | collective-permute-done | bytes 491552 | tf_op jit(solution)/shard_map/ppermute | solution.py:34
  385.5 3.1 collective-permute-start.86
  389.5 4.4 collective-permute-done.82.refs_2_
  393.9 5.8 collective-permute-done.86.refs_4_
  400.4 2.9 shard_map.215.refs_0_
  404.0 13.3 %collective-permute-start.88 = (bf16[768,768]{1,0:T(8,128)(2,1)S(1)}, bf16[768,768]{1,0:T(8,128)(2,1)}, u32[]{:S(2)}, u32[]{:S(2)}) collective-permute-start(bf16[768,768]{1,0:T(8,128)(2,1)S(1)} %copy-done.151), channel_id=1, source_target_pairs={{0,3},{1,5},{2,1},{3,7},{4,2},{5,4},{6,0},{7,6},{8,11},{9,13},{10,... | collective-permute-start | bytes 3538952 | tf_op jit(solution)/shard_map/ppermute | solution.py:34
  418.2 27.4 %shard_map.216 = (f32[1024,768]{1,0:T(8,128)}, bf16[1024,768]{1,0:T(8,128)(2,1)}, f32[1,768]{1,0:T(1,128)}, bf16[3,1024,192]{2,1,0:T(8,128)(2,1)}, f32[3,2048]{1...) custom-call(bf16[1024,384]{1,0:T(8,128)(2,1)} %copy-done.105, bf16[1024,384]{1,0:T(8,128)(2,1)} %copy-done.152, ...), custom_call_target="tpu_custom_call" | custom-call | flops 99999997952 | bytes 1000 | tf_op jit(solution)/shard_map/pallas_call | solution.py:178
  445.7 5.6 shard_map.217
  457.2 6.0 collective-permute-done.70
  463.3 7.8 %collective-permute-done.71 = bf16[256,768]{1,0:T(8,128)(2,1)S(1)} collective-permute-done((bf16[256,768]{1,0:T(8,128)(2,1)S(1)}, bf16[256,768]{1,0:T(8,128)(2,1)S(1)}, u32[]{:S(2)}, u32[]{:S(2)}) %collective-permute-start.71) | collective-permute-done | bytes 393248 | tf_op jit(solution)/shard_map/ppermute | solution.py:34
  479.1 4.7 shard_map.219
  488.0 5.3 collective-permute-done.93.refs_1_.refs_9_
  493.3 6.4 collective-permute-done.94.refs_2_.refs_10_
  501.5 6.5 shard_map.220
  509.1 3.6 collective-permute-start.100
  515.6 8.8 %shard_map.221 = (bf16[768,768]{1,0:T(8,128)(2,1)}, bf16[768,768]{1,0:T(8,128)(2,1)}) custom-call(bf16[320,384]{1,0:T(8,128)(2,1)} %copy-done.48, bf16[320,384]{1,0:T(8,128)(2,1)} %copy-done.49, bf16[320,384]{1,0:T(8,128)(2,1)} %copy-done.50, bf16[320,384]{1,0:T(8,128)(2,1)} %copy-done.51, bf16[320,384]{1,0:T(8,128)(2,1)} %copy-done.52, ...), custom_call_target="tpu_custom_call" | custom-call | flops 1000000000 | bytes 1000 | tf_op jit(solution)/shard_map/pallas_call | solution.py:178
  529.0 10.3 %collective-permute-done.101 = bf16[640,384]{1,0:T(8,128)(2,1)S(1)} collective-permute-done((bf16[640,384]{1,0:T(8,128)(2,1)S(1)}, bf16[640,384]{1,0:T(8,128)(2,1)S(1)}, u32[]{:S(2)}, u32[]{:S(2)}) %collective-permute-start.101) | collective-permute-done | bytes 491552 | tf_op jit(solution)/shard_map/ppermute | solution.py:34
  542.3 4.0 collective-permute-done.108.refs_4_
  546.3 6.0 collective-permute-done.104.refs_2_
  558.7 11.0 %collective-permute-start.110 = (bf16[768,768]{1,0:T(8,128)(2,1)}, bf16[768,768]{1,0:T(8,128)(2,1)S(1)}, u32[]{:S(2)}, u32[]{:S(2)}) collective-permute-start(bf16[768,768]{1,0:T(8,128)(2,1)} %get-tuple-element.244), channel_id=1, source_target_pairs={{0,3},{1,5},{2,1},{3,7},{4,2},{5,4},{6,0},{7,6},{8,11},{9,13},{10,... | collective-permute-start | bytes 3538952 | tf_op jit(solution)/shard_map/ppermute | solution.py:34
  569.7 27.6 %shard_map.223 = (f32[1024,768]{1,0:T(8,128)}, bf16[1024,768]{1,0:T(8,128)(2,1)}, f32[1,768]{1,0:T(1,128)}, bf16[3,1024,192]{2,1,0:T(8,128)(2,1)}, f32[3,2048]{1...) custom-call(bf16[1024,384]{1,0:T(8,128)(2,1)} %copy-done.104, ...), custom_call_target="tpu_custom_call" | custom-call | flops 99999997952 | bytes 1000 | tf_op jit(solution)/shard_map/pallas_call | solution.py:178
  600.0 5.7 shard_map.224
  614.1 14.7 %collective-permute-done.112 = bf16[1024,384]{1,0:T(8,128)(2,1)} collective-permute-done((bf16[1024,384]{1,0:T(8,128)(2,1)S(1)}, bf16[1024,384]{1,0:T(8,128)(2,1)}, u32[]{:S(2)}, u32[]{:S(2)}) %collective-permute-start.112) | collective-permute-done | bytes 786464 | tf_op jit(solution)/shard_map/ppermute | solution.py:34
  632.1 2.9 fusion.2
  648.8 7.7 %collective-permute-start.118 = (bf16[192,768]{1,0:T(8,128)(2,1)S(1)}, bf16[192,768]{1,0:T(8,128)(2,1)S(1)}, u32[]{:S(2)}, u32[]{:S(2)}) collective-permute-start(bf16[192,768]{1,0:T(8,128)(2,1)S(1)} %copy-done.140), channel_id=1, source_target_pairs={{0,4},{1,5},{2,6},{3,7},{4,0},{5,1},{6,2},{7,3},{8,12},{9,13},{10,... | collective-permute-start | bytes 884744 | tf_op jit(solution)/shard_map/ppermute | solution.py:34
  660.6 3.2 collective-permute-start.115
  669.7 6.0 collective-permute-done.126
  (719 shorter events, 230.8 us)
Async XLA Ops:
  2.3 13.3 %collective-permute-start.10 = (bf16[2052]{0:T(1024)(128)(2,1)S(1)}, bf16[2052]{0:T(1024)(128)(2,1)S(1)}, u32[]{:S(2)}, u32[]{:S(2)}) collective-permute-start(bf16[2052]{0:T(1024)(128)(2,1)S(1)} %concatenate.83), channel_id=1, source_target_pairs={{0,4},{1,5},{2,6},{3,7},{4,0},{5,1},{6,2},{7,3},{8,12},{9,13},{10,... | collective-permute-start | bytes 12320 | tf_op jit(solution)/shard_map/ppermute | solution.py:34
  6.3 16.5 %collective-permute-start.4 = (bf16[192,768]{1,0:T(8,128)(2,1)}, bf16[192,768]{1,0:T(8,128)(2,1)}, u32[]{:S(2)}, u32[]{:S(2)}) collective-permute-start(bf16[192,768]{1,0:T(8,128)(2,1)} %pad_maximum_fusion.11), channel_id=1, source_target_pairs={{0,16},{1,17},{2,18},{3,19},{4,20},{5,21},{6,22},{7,23},{8,24},{9,... | collective-permute-start | bytes 884744 | tf_op jit(solution)/shard_map/ppermute | solution.py:34
  9.7 13.8 %collective-permute-start.1 = (bf16[256,768]{1,0:T(8,128)(2,1)}, bf16[256,768]{1,0:T(8,128)(2,1)}, u32[]{:S(2)}, u32[]{:S(2)}) collective-permute-start(bf16[256,768]{1,0:T(8,128)(2,1)} %get-tuple-element.334), channel_id=1, source_target_pairs={{0,5},{1,4},{2,1},{3,0},{4,7},{5,6},{6,3},{7,2},{8,13},{9,12},{10,... | collective-permute-start | bytes 1179656 | tf_op jit(solution)/shard_map/ppermute | solution.py:34
  11.1 20.3 %collective-permute-start = (bf16[256,768]{1,0:T(8,128)(2,1)}, bf16[256,768]{1,0:T(8,128)(2,1)}, u32[]{:S(2)}, u32[]{:S(2)}) collective-permute-start(bf16[256,768]{1,0:T(8,128)(2,1)} %get-tuple-element.335), channel_id=1, source_target_pairs={{0,4},{1,5},{2,0},{3,1},{4,6},{5,7},{6,2},{7,3},{8,12},{9,13},{10,... | collective-permute-start | bytes 1179656 | tf_op jit(solution)/shard_map/ppermute | solution.py:34
  22.8 30.1 %collective-permute-start.5 = (bf16[768,768]{1,0:T(8,128)(2,1)}, bf16[768,768]{1,0:T(8,128)(2,1)S(1)}, u32[]{:S(2)}, u32[]{:S(2)}) collective-permute-start(bf16[768,768]{1,0:T(8,128)(2,1)} %broadcast_select_fusion.4), channel_id=1, source_target_pairs={{0,16},{1,17},{2,18},{3,19},{4,20},{5,21},{6,22},{7,23},{8,24},{9,... | collective-permute-start | bytes 3538952 | tf_op jit(solution)/shard_map/ppermute | solution.py:34
  44.6 12.3 %collective-permute-start.3 = (bf16[256,768]{1,0:T(8,128)(2,1)}, bf16[256,768]{1,0:T(8,128)(2,1)S(1)}, u32[]{:S(2)}, u32[]{:S(2)}) collective-permute-start(bf16[256,768]{1,0:T(8,128)(2,1)} %collective-permute-done.1.refs_1_), channel_id=1, source_target_pairs={{0,4},{1,5},{2,6},{3,7},{4,0},{5,1},{6,2},{7,3},{8,12},{9,13},{10,... | collective-permute-start | bytes 1179656 | tf_op jit(solution)/shard_map/ppermute | solution.py:34
  52.9 42.1 %collective-permute-start.20 = (bf16[4,2,96,384]{3,2,0,1:T(8,128)(2,1)}, bf16[4,2,96,384]{3,2,0,1:T(8,128)(2,1)}, u32[]{:S(2)}, u32[]{:S(2)}) collective-permute-start(bf16[4,2,96,384]{3,2,0,1:T(8,128)(2,1)} %pad_maximum_fusion.9), channel_id=1, source_target_pairs={{0,4},{1,5},{2,6},{3,7},{4,0},{5,1},{6,2},{7,3},{8,12},{9,13},{10,... | collective-permute-start | bytes 1769480 | tf_op jit(solution)/shard_map/ppermute | solution.py:34
  56.9 23.3 %collective-permute-start.12 = (bf16[768,768]{1,0:T(8,128)(2,1)}, bf16[768,768]{1,0:T(8,128)(2,1)S(1)}, u32[]{:S(2)}, u32[]{:S(2)}) collective-permute-start(bf16[768,768]{1,0:T(8,128)(2,1)} %get-tuple-element.287), channel_id=1, source_target_pairs={{0,4},{1,0},{2,6},{3,2},{4,7},{5,3},{6,5},{7,1},{8,12},{9,8},{10,1... | collective-permute-start | bytes 3538952 | tf_op jit(solution)/shard_map/ppermute | solution.py:34
  80.2 14.8 %collective-permute-start.13 = (bf16[512,384]{1,0:T(8,128)(2,1)}, bf16[512,384]{1,0:T(8,128)(2,1)S(1)}, u32[]{:S(2)}, u32[]{:S(2)}) collective-permute-start(bf16[512,384]{1,0:T(8,128)(2,1)} %get-tuple-element.144.refs_1_.own_ref), channel_id=1, source_target_pairs={{0,16},{1,17},{2,18},{3,19},{4,20},{5,21},{6,22},{7,23},{8,24},{9,... | collective-permute-start | bytes 1179656 | tf_op jit(solution)/shard_map/ppermute | solution.py:34
  88.0 39.7 %collective-permute-start.28 = (bf16[768,768]{1,0:T(8,128)(2,1)}, bf16[768,768]{1,0:T(8,128)(2,1)S(1)}, u32[]{:S(2)}, u32[]{:S(2)}) collective-permute-start(bf16[768,768]{1,0:T(8,128)(2,1)} %get-tuple-element.287), channel_id=1, source_target_pairs={{0,6},{1,2},{2,4},{3,0},{4,5},{5,1},{6,7},{7,3},{8,14},{9,10},{10,... | collective-permute-start | bytes 3538952 | tf_op jit(solution)/shard_map/ppermute | solution.py:34
  113.7 13.9 %collective-permute-start.23 = (bf16[320,384]{1,0:T(8,128)(2,1)S(1)}, bf16[320,384]{1,0:T(8,128)(2,1)S(1)}, u32[]{:S(2)}, u32[]{:S(2)}) collective-permute-start(bf16[320,384]{1,0:T(8,128)(2,1)S(1)} %get-tuple-element.150), channel_id=1, source_target_pairs={{0,9},{1,8},{2,11},{3,10},{4,13},{5,12},{6,15},{7,14},{8,1},{9,0},... | collective-permute-start | bytes 737288 | tf_op jit(solution)/shard_map/ppermute | solution.py:34
  113.9 14.5 %collective-permute-start.24 = (bf16[320,384]{1,0:T(8,128)(2,1)S(1)}, bf16[320,384]{1,0:T(8,128)(2,1)S(1)}, u32[]{:S(2)}, u32[]{:S(2)}) collective-permute-start(bf16[320,384]{1,0:T(8,128)(2,1)S(1)} %get-tuple-element.147.refs_0_), channel_id=1, source_target_pairs={{0,4},{1,5},{2,6},{3,7},{4,0},{5,1},{6,2},{7,3},{8,12},{9,13},{10,... | collective-permute-start | bytes 737288 | tf_op jit(solution)/shard_map/ppermute | solution.py:34
  127.7 15.9 %collective-permute-start.31 = (bf16[192,576]{1,0:T(8,128)(2,1)S(1)}, bf16[192,576]{1,0:T(8,128)(2,1)S(1)}, u32[]{:S(2)}, u32[]{:S(2)}) collective-permute-start(bf16[192,576]{1,0:T(8,128)(2,1)S(1)} %slice.387), channel_id=1, source_target_pairs={{4,6},{5,7},{6,4},{7,5},{12,14},{13,15},{14,12},{15,13},{16,17},{1... | collective-permute-start | bytes 663560 | tf_op jit(solution)/shard_map/ppermute | solution.py:34
  128.4 15.9 %collective-permute-start.32 = (bf16[192,576]{1,0:T(8,128)(2,1)S(1)}, bf16[192,576]{1,0:T(8,128)(2,1)S(1)}, u32[]{:S(2)}, u32[]{:S(2)}) collective-permute-start(bf16[192,576]{1,0:T(8,128)(2,1)S(1)} %slice.387), channel_id=1, source_target_pairs={{0,6},{1,7},{2,4},{3,5},{4,0},{5,1},{6,2},{7,3},{8,14},{9,15},{10,... | collective-permute-start | bytes 663560 | tf_op jit(solution)/shard_map/ppermute | solution.py:34
  144.3 26.9 %collective-permute-start.35 = (bf16[768,768]{1,0:T(8,128)(2,1)}, bf16[768,768]{1,0:T(8,128)(2,1)S(1)}, u32[]{:S(2)}, u32[]{:S(2)}) collective-permute-start(bf16[768,768]{1,0:T(8,128)(2,1)} %get-tuple-element.161), channel_id=1, source_target_pairs={{0,4},{1,0},{2,6},{3,2},{4,7},{5,3},{6,5},{7,1},{8,12},{9,8},{10,1... | collective-permute-start | bytes 3538952 | tf_op jit(solution)/shard_map/ppermute | solution.py:34
  146.8 14.3 %collective-permute-start.38 = (bf16[640,384]{1,0:T(8,128)(2,1)}, bf16[640,384]{1,0:T(8,128)(2,1)}, u32[]{:S(2)}, u32[]{:S(2)}) collective-permute-start(bf16[640,384]{1,0:T(8,128)(2,1)} %add.241), channel_id=1, source_target_pairs={{0,16},{1,17},{2,18},{3,19},{4,20},{5,21},{6,22},{7,23},{8,24},{9,... | collective-permute-start | bytes 1474568 | tf_op jit(solution)/shard_map/ppermute | solution.py:34
  148.6 22.6 %collective-permute-start.30 = (bf16[640,384]{1,0:T(8,128)(2,1)S(1)}, bf16[640,384]{1,0:T(8,128)(2,1)S(1)}, u32[]{:S(2)}, u32[]{:S(2)}) collective-permute-start(bf16[640,384]{1,0:T(8,128)(2,1)S(1)} %add.239), channel_id=1, source_target_pairs={{0,16},{1,17},{2,18},{3,19},{4,20},{5,21},{6,22},{7,23},{8,24},{9,... | collective-permute-start | bytes 1474568 | tf_op jit(solution)/shard_map/ppermute | solution.py:34
  151.2 14.6 %collective-permute-start.33 = (bf16[192,576]{1,0:T(8,128)(2,1)}, bf16[192,576]{1,0:T(8,128)(2,1)S(1)}, u32[]{:S(2)}, u32[]{:S(2)}) collective-permute-start(bf16[192,576]{1,0:T(8,128)(2,1)} %broadcast_select_fusion.20.refs_4_), channel_id=1, source_target_pairs={{0,8},{1,9},{2,10},{3,11},{4,12},{5,13},{6,14},{7,15},{8,0},{9,1},... | collective-permute-start | bytes 663560 | tf_op jit(solution)/shard_map/ppermute | solution.py:34
  151.8 12.9 %collective-permute-start.34 = (bf16[192,576]{1,0:T(8,128)(2,1)}, bf16[192,576]{1,0:T(8,128)(2,1)S(1)}, u32[]{:S(2)}, u32[]{:S(2)}) collective-permute-start(bf16[192,576]{1,0:T(8,128)(2,1)} %copy-done.155), channel_id=1, source_target_pairs={{0,8},{1,9},{2,10},{3,11},{4,12},{5,13},{6,14},{7,15},{8,0},{9,1},... | collective-permute-start | bytes 663560 | tf_op jit(solution)/shard_map/ppermute | solution.py:34
  162.5 15.7 %collective-permute-start.43 = (bf16[320,384]{1,0:T(8,128)(2,1)S(1)}, bf16[320,384]{1,0:T(8,128)(2,1)S(1)}, u32[]{:S(2)}, u32[]{:S(2)}) collective-permute-start(bf16[320,384]{1,0:T(8,128)(2,1)S(1)} %get-tuple-element.326), channel_id=1, source_target_pairs={{0,9},{1,8},{2,11},{3,10},{4,13},{5,12},{6,15},{7,14},{8,1},{9,0},... | collective-permute-start | bytes 737288 | tf_op jit(solution)/shard_map/ppermute | solution.py:34
  164.7 17.1 %collective-permute-start.42 = (bf16[320,384]{1,0:T(8,128)(2,1)S(1)}, bf16[320,384]{1,0:T(8,128)(2,1)S(1)}, u32[]{:S(2)}, u32[]{:S(2)}) collective-permute-start(bf16[320,384]{1,0:T(8,128)(2,1)S(1)} %get-tuple-element.327), channel_id=1, source_target_pairs={{0,8},{1,9},{2,10},{3,11},{4,12},{5,13},{6,14},{7,15},{8,0},{9,1},... | collective-permute-start | bytes 737288 | tf_op jit(solution)/shard_map/ppermute | solution.py:34
  184.7 15.6 %collective-permute-start.44 = (bf16[1024,384]{1,0:T(8,128)(2,1)S(1)}, bf16[1024,384]{1,0:T(8,128)(2,1)S(1)}, u32[]{:S(2)}, u32[]{:S(2)}) collective-permute-start(bf16[1024,384]{1,0:T(8,128)(2,1)S(1)} %shard_map.207.refs_2_), channel_id=1, source_target_pairs={{0,4},{1,5},{2,6},{3,7},{4,0},{5,1},{6,2},{7,3},{8,12},{9,13},{10,... | collective-permute-start | bytes 2359304 | tf_op jit(solution)/shard_map/ppermute | solution.py:34
  197.2 38.8 %collective-permute-start.50 = (bf16[4,2,96,384]{3,2,0,1:T(8,128)(2,1)S(1)}, bf16[4,2,96,384]{3,2,0,1:T(8,128)(2,1)S(1)}, u32[]{:S(2)}, u32[]{:S(2)}) collective-permute-start(bf16[4,2,96,384]{3,2,0,1:T(8,128)(2,1)S(1)} %pad_maximum_fusion.10), channel_id=1, source_target_pairs={{0,4},{1,5},{2,6},{3,7},{4,0},{5,1},{6,2},{7,3},{8,12},{9,13},{10,... | collective-permute-start | bytes 1769480 | tf_op jit(solution)/shard_map/ppermute | solution.py:34
  197.3 26.7 %collective-permute-start.45 = (bf16[768,768]{1,0:T(8,128)(2,1)}, bf16[768,768]{1,0:T(8,128)(2,1)S(1)}, u32[]{:S(2)}, u32[]{:S(2)}) collective-permute-start(bf16[768,768]{1,0:T(8,128)(2,1)} %get-tuple-element.161), channel_id=1, source_target_pairs={{0,6},{1,2},{2,4},{3,0},{4,5},{5,1},{6,7},{7,3},{8,14},{9,10},{10,... | collective-permute-start | bytes 3538952 | tf_op jit(solution)/shard_map/ppermute | solution.py:34
  250.9 12.6 %collective-permute-start.53 = (bf16[320,384]{1,0:T(8,128)(2,1)S(1)}, bf16[320,384]{1,0:T(8,128)(2,1)S(1)}, u32[]{:S(2)}, u32[]{:S(2)}) collective-permute-start(bf16[320,384]{1,0:T(8,128)(2,1)S(1)} %get-tuple-element.168), channel_id=1, source_target_pairs={{0,9},{1,8},{2,11},{3,10},{4,13},{5,12},{6,15},{7,14},{8,1},{9,0},... | collective-permute-start | bytes 737288 | tf_op jit(solution)/shard_map/ppermute | solution.py:34
  274.4 14.1 %collective-permute-start.59 = (bf16[640,384]{1,0:T(8,128)(2,1)S(1)}, bf16[640,384]{1,0:T(8,128)(2,1)S(1)}, u32[]{:S(2)}, u32[]{:S(2)}) collective-permute-start(bf16[640,384]{1,0:T(8,128)(2,1)S(1)} %add.245), channel_id=1, source_target_pairs={{0,16},{1,17},{2,18},{3,19},{4,20},{5,21},{6,22},{7,23},{8,24},{9,... | collective-permute-start | bytes 1474568 | tf_op jit(solution)/shard_map/ppermute | solution.py:34
  276.6 21.9 %collective-permute-start.64 = (bf16[640,384]{1,0:T(8,128)(2,1)S(1)}, bf16[640,384]{1,0:T(8,128)(2,1)S(1)}, u32[]{:S(2)}, u32[]{:S(2)}) collective-permute-start(bf16[640,384]{1,0:T(8,128)(2,1)S(1)} %add.247), channel_id=1, source_target_pairs={{0,16},{1,17},{2,18},{3,19},{4,20},{5,21},{6,22},{7,23},{8,24},{9,... | collective-permute-start | bytes 1474568 | tf_op jit(solution)/shard_map/ppermute | solution.py:34
  278.1 25.7 %collective-permute-start.61 = (bf16[256,768]{1,0:T(8,128)(2,1)}, bf16[256,768]{1,0:T(8,128)(2,1)}, u32[]{:S(2)}, u32[]{:S(2)}) collective-permute-start(bf16[256,768]{1,0:T(8,128)(2,1)} %get-tuple-element.332), channel_id=1, source_target_pairs={{0,5},{1,4},{2,1},{3,0},{4,7},{5,6},{6,3},{7,2},{8,13},{9,12},{10,... | collective-permute-start | bytes 1179656 | tf_op jit(solution)/shard_map/ppermute | solution.py:34
  279.2 24.6 %collective-permute-start.60 = (bf16[256,768]{1,0:T(8,128)(2,1)}, bf16[256,768]{1,0:T(8,128)(2,1)}, u32[]{:S(2)}, u32[]{:S(2)}) collective-permute-start(bf16[256,768]{1,0:T(8,128)(2,1)} %get-tuple-element.333), channel_id=1, source_target_pairs={{0,4},{1,5},{2,0},{3,1},{4,6},{5,7},{6,2},{7,3},{8,12},{9,13},{10,... | collective-permute-start | bytes 1179656 | tf_op jit(solution)/shard_map/ppermute | solution.py:34
  289.4 14.9 %collective-permute-start.62 = (bf16[320,384]{1,0:T(8,128)(2,1)}, bf16[320,384]{1,0:T(8,128)(2,1)}, u32[]{:S(2)}, u32[]{:S(2)}) collective-permute-start(bf16[320,384]{1,0:T(8,128)(2,1)} %get-tuple-element.352), channel_id=1, source_target_pairs={{0,1},{1,0},{2,3},{3,2},{4,5},{5,4},{6,7},{7,6},{8,9},{9,8},{10,11... | collective-permute-start | bytes 737288 | tf_op jit(solution)/shard_map/ppermute | solution.py:34
  303.8 17.7 %collective-permute-start.69 = (bf16[256,768]{1,0:T(8,128)(2,1)}, bf16[256,768]{1,0:T(8,128)(2,1)}, u32[]{:S(2)}, u32[]{:S(2)}) collective-permute-start(bf16[256,768]{1,0:T(8,128)(2,1)} %collective-permute-done.61), channel_id=1, source_target_pairs={{0,4},{1,5},{2,6},{3,7},{4,0},{5,1},{6,2},{7,3},{8,12},{9,13},{10,... | collective-permute-start | bytes 1179656 | tf_op jit(solution)/shard_map/ppermute | solution.py:34
  303.8 17.7 %collective-permute-start.68 = (bf16[256,768]{1,0:T(8,128)(2,1)}, bf16[256,768]{1,0:T(8,128)(2,1)}, u32[]{:S(2)}, u32[]{:S(2)}) collective-permute-start(bf16[256,768]{1,0:T(8,128)(2,1)} %collective-permute-done.60), channel_id=1, source_target_pairs={{0,4},{1,5},{2,6},{3,7},{4,0},{5,1},{6,2},{7,3},{8,12},{9,13},{10,... | collective-permute-start | bytes 1179656 | tf_op jit(solution)/shard_map/ppermute | solution.py:34
  335.2 13.4 %collective-permute-start.73 = (bf16[320,384]{1,0:T(8,128)(2,1)S(1)}, bf16[320,384]{1,0:T(8,128)(2,1)S(1)}, u32[]{:S(2)}, u32[]{:S(2)}) collective-permute-start(bf16[320,384]{1,0:T(8,128)(2,1)S(1)} %get-tuple-element.180), channel_id=1, source_target_pairs={{0,8},{1,9},{2,10},{3,11},{4,12},{5,13},{6,14},{7,15},{8,0},{9,1},... | collective-permute-start | bytes 737288 | tf_op jit(solution)/shard_map/ppermute | solution.py:34
  336.3 12.3 %collective-permute-start.74 = (bf16[320,384]{1,0:T(8,128)(2,1)S(1)}, bf16[320,384]{1,0:T(8,128)(2,1)S(1)}, u32[]{:S(2)}, u32[]{:S(2)}) collective-permute-start(bf16[320,384]{1,0:T(8,128)(2,1)S(1)} %get-tuple-element.181), channel_id=1, source_target_pairs={{0,9},{1,8},{2,11},{3,10},{4,13},{5,12},{6,15},{7,14},{8,1},{9,0},... | collective-permute-start | bytes 737288 | tf_op jit(solution)/shard_map/ppermute | solution.py:34
  359.4 12.6 %collective-permute-start.83 = (bf16[640,384]{1,0:T(8,128)(2,1)}, bf16[640,384]{1,0:T(8,128)(2,1)S(1)}, u32[]{:S(2)}, u32[]{:S(2)}) collective-permute-start(bf16[640,384]{1,0:T(8,128)(2,1)} %get-tuple-element.191), channel_id=1, source_target_pairs={{0,4},{1,5},{2,6},{3,7},{4,0},{5,1},{6,2},{7,3},{8,12},{9,13},{10,... | collective-permute-start | bytes 1474568 | tf_op jit(solution)/shard_map/ppermute | solution.py:34
  361.3 13.3 %collective-permute-start.80 = (bf16[640,384]{1,0:T(8,128)(2,1)S(1)}, bf16[640,384]{1,0:T(8,128)(2,1)S(1)}, u32[]{:S(2)}, u32[]{:S(2)}) collective-permute-start(bf16[640,384]{1,0:T(8,128)(2,1)S(1)} %add.257), channel_id=1, source_target_pairs={{0,16},{1,17},{2,18},{3,19},{4,20},{5,21},{6,22},{7,23},{8,24},{9,... | collective-permute-start | bytes 1474568 | tf_op jit(solution)/shard_map/ppermute | solution.py:34
  371.6 17.9 %collective-permute-start.81 = (bf16[768,768]{1,0:T(8,128)(2,1)}, bf16[768,768]{1,0:T(8,128)(2,1)S(1)}, u32[]{:S(2)}, u32[]{:S(2)}) collective-permute-start(bf16[768,768]{1,0:T(8,128)(2,1)} %get-tuple-element.187), channel_id=1, source_target_pairs={{0,1},{1,7},{2,3},{3,5},{4,0},{5,6},{6,2},{7,4},{8,9},{9,15},{10,1... | collective-permute-start | bytes 3538952 | tf_op jit(solution)/shard_map/ppermute | solution.py:34
  372.2 13.2 %collective-permute-start.84 = (bf16[640,384]{1,0:T(8,128)(2,1)S(1)}, bf16[640,384]{1,0:T(8,128)(2,1)S(1)}, u32[]{:S(2)}, u32[]{:S(2)}) collective-permute-start(bf16[640,384]{1,0:T(8,128)(2,1)S(1)} %add.259), channel_id=1, source_target_pairs={{0,16},{1,17},{2,18},{3,19},{4,20},{5,21},{6,22},{7,23},{8,24},{9,... | collective-permute-start | bytes 1474568 | tf_op jit(solution)/shard_map/ppermute | solution.py:34
  374.7 19.2 %collective-permute-start.82 = (bf16[320,384]{1,0:T(8,128)(2,1)S(1)}, bf16[320,384]{1,0:T(8,128)(2,1)S(1)}, u32[]{:S(2)}, u32[]{:S(2)}) collective-permute-start(bf16[320,384]{1,0:T(8,128)(2,1)S(1)} %get-tuple-element.349), channel_id=1, source_target_pairs={{0,1},{1,0},{2,3},{3,2},{4,5},{5,4},{6,7},{7,6},{8,9},{9,8},{10,11... | collective-permute-start | bytes 737288 | tf_op jit(solution)/shard_map/ppermute | solution.py:34
  385.5 14.2 %collective-permute-start.86 = (bf16[320,384]{1,0:T(8,128)(2,1)S(1)}, bf16[320,384]{1,0:T(8,128)(2,1)S(1)}, u32[]{:S(2)}, u32[]{:S(2)}) collective-permute-start(bf16[320,384]{1,0:T(8,128)(2,1)S(1)} %get-tuple-element.322), channel_id=1, source_target_pairs={{0,9},{1,8},{2,11},{3,10},{4,13},{5,12},{6,15},{7,14},{8,1},{9,0},... | collective-permute-start | bytes 737288 | tf_op jit(solution)/shard_map/ppermute | solution.py:34
  403.3 14.1 %collective-permute-start.87 = (bf16[1024,384]{1,0:T(8,128)(2,1)S(1)}, bf16[1024,384]{1,0:T(8,128)(2,1)S(1)}, u32[]{:S(2)}, u32[]{:S(2)}) collective-permute-start(bf16[1024,384]{1,0:T(8,128)(2,1)S(1)} %shard_map.215.refs_0_), channel_id=1, source_target_pairs={{0,4},{1,5},{2,6},{3,7},{4,0},{5,1},{6,2},{7,3},{8,12},{9,13},{10,... | collective-permute-start | bytes 2359304 | tf_op jit(solution)/shard_map/ppermute | solution.py:34
  404.0 41.6 %collective-permute-start.88 = (bf16[768,768]{1,0:T(8,128)(2,1)S(1)}, bf16[768,768]{1,0:T(8,128)(2,1)}, u32[]{:S(2)}, u32[]{:S(2)}) collective-permute-start(bf16[768,768]{1,0:T(8,128)(2,1)S(1)} %copy-done.151), channel_id=1, source_target_pairs={{0,3},{1,5},{2,1},{3,7},{4,2},{5,4},{6,0},{7,6},{8,11},{9,13},{10,... | collective-permute-start | bytes 3538952 | tf_op jit(solution)/shard_map/ppermute | solution.py:34
  452.8 18.4 %collective-permute-start.91 = (bf16[1,2,192,768]{3,2,1,0:T(8,128)(2,1)S(1)}, bf16[1,2,192,768]{3,2,1,0:T(8,128)(2,1)S(1)}, u32[]{:S(2)}, u32[]{:S(2)}) collective-permute-start(bf16[1,2,192,768]{3,2,1,0:T(8,128)(2,1)S(1)} %bitcast.148), channel_id=1, source_target_pairs={{0,8},{1,9},{2,10},{3,11},{4,12},{5,13},{6,14},{7,15},{8,0},{9,1},... | collective-permute-start | bytes 1769480 | tf_op jit(solution)/shard_map/ppermute | solution.py:34
  454.2 19.7 %collective-permute-start.90 = (bf16[1024,384]{1,0:T(8,128)(2,1)S(1)}, bf16[1024,384]{1,0:T(8,128)(2,1)S(1)}, u32[]{:S(2)}, u32[]{:S(2)}) collective-permute-start(bf16[1024,384]{1,0:T(8,128)(2,1)S(1)} %add.262), channel_id=1, source_target_pairs={{0,16},{1,17},{2,18},{3,19},{4,20},{5,21},{6,22},{7,23},{8,24},{9,... | collective-permute-start | bytes 2359304 | tf_op jit(solution)/shard_map/ppermute | solution.py:34
  455.5 15.6 %collective-permute-start.71 = (bf16[256,768]{1,0:T(8,128)(2,1)S(1)}, bf16[256,768]{1,0:T(8,128)(2,1)S(1)}, u32[]{:S(2)}, u32[]{:S(2)}) collective-permute-start(bf16[256,768]{1,0:T(8,128)(2,1)S(1)} %get-tuple-element.295), channel_id=1, source_target_pairs={{0,3},{1,2},{2,7},{3,6},{4,1},{5,0},{6,5},{7,4},{8,11},{9,10},{10,... | collective-permute-start | bytes 1179656 | tf_op jit(solution)/shard_map/ppermute | solution.py:34
  486.4 13.3 %collective-permute-start.94 = (bf16[320,384]{1,0:T(8,128)(2,1)S(1)}, bf16[320,384]{1,0:T(8,128)(2,1)S(1)}, u32[]{:S(2)}, u32[]{:S(2)}) collective-permute-start(bf16[320,384]{1,0:T(8,128)(2,1)S(1)} %get-tuple-element.217), channel_id=1, source_target_pairs={{0,8},{1,9},{2,10},{3,11},{4,12},{5,13},{6,14},{7,15},{8,0},{9,1},... | collective-permute-start | bytes 737288 | tf_op jit(solution)/shard_map/ppermute | solution.py:34
  488.0 12.2 %collective-permute-start.96 = (bf16[320,384]{1,0:T(8,128)(2,1)S(1)}, bf16[320,384]{1,0:T(8,128)(2,1)S(1)}, u32[]{:S(2)}, u32[]{:S(2)}) collective-permute-start(bf16[320,384]{1,0:T(8,128)(2,1)S(1)} %get-tuple-element.215.refs_0_.refs_8_), channel_id=1, source_target_pairs={{0,4},{1,5},{2,6},{3,7},{4,0},{5,1},{6,2},{7,3},{8,12},{9,13},{10,... | collective-permute-start | bytes 737288 | tf_op jit(solution)/shard_map/ppermute | solution.py:34
  508.4 18.0 %collective-permute-start.102 = (bf16[2,192,768]{2,1,0:T(8,128)(2,1)S(1)}, bf16[2,192,768]{2,1,0:T(8,128)(2,1)S(1)}, u32[]{:S(2)}, u32[]{:S(2)}) collective-permute-start(bf16[2,192,768]{2,1,0:T(8,128)(2,1)S(1)} %add_bitcast_fusion.1), channel_id=1, source_target_pairs={{4,6},{5,7},{6,4},{7,5},{12,14},{13,15},{14,12},{15,13},{16,17},{1... | collective-permute-start | bytes 1769480 | tf_op jit(solution)/shard_map/ppermute | solution.py:34
  509.1 15.3 %collective-permute-start.100 = (bf16[640,384]{1,0:T(8,128)(2,1)S(1)}, bf16[640,384]{1,0:T(8,128)(2,1)}, u32[]{:S(2)}, u32[]{:S(2)}) collective-permute-start(bf16[640,384]{1,0:T(8,128)(2,1)S(1)} %get-tuple-element.221), channel_id=1, source_target_pairs={{0,4},{1,5},{2,6},{3,7},{4,0},{5,1},{6,2},{7,3},{8,12},{9,13},{10,... | collective-permute-start | bytes 1474568 | tf_op jit(solution)/shard_map/ppermute | solution.py:34
  512.9 14.4 %collective-permute-start.106 = (bf16[640,384]{1,0:T(8,128)(2,1)S(1)}, bf16[640,384]{1,0:T(8,128)(2,1)S(1)}, u32[]{:S(2)}, u32[]{:S(2)}) collective-permute-start(bf16[640,384]{1,0:T(8,128)(2,1)S(1)} %add.267), channel_id=1, source_target_pairs={{0,16},{1,17},{2,18},{3,19},{4,20},{5,21},{6,22},{7,23},{8,24},{9,... | collective-permute-start | bytes 1474568 | tf_op jit(solution)/shard_map/ppermute | solution.py:34
  524.4 17.8 %collective-permute-start.103 = (bf16[768,768]{1,0:T(8,128)(2,1)}, bf16[768,768]{1,0:T(8,128)(2,1)S(1)}, u32[]{:S(2)}, u32[]{:S(2)}) collective-permute-start(bf16[768,768]{1,0:T(8,128)(2,1)} %get-tuple-element.226), channel_id=1, source_target_pairs={{0,1},{1,7},{2,3},{3,5},{4,0},{5,6},{6,2},{7,4},{8,9},{9,15},{10,1... | collective-permute-start | bytes 3538952 | tf_op jit(solution)/shard_map/ppermute | solution.py:34
  525.6 13.7 %collective-permute-start.101 = (bf16[640,384]{1,0:T(8,128)(2,1)S(1)}, bf16[640,384]{1,0:T(8,128)(2,1)S(1)}, u32[]{:S(2)}, u32[]{:S(2)}) collective-permute-start(bf16[640,384]{1,0:T(8,128)(2,1)S(1)} %add.264), channel_id=1, source_target_pairs={{0,16},{1,17},{2,18},{3,19},{4,20},{5,21},{6,22},{7,23},{8,24},{9,... | collective-permute-start | bytes 1474568 | tf_op jit(solution)/shard_map/ppermute | solution.py:34
  527.3 18.9 %collective-permute-start.108 = (bf16[320,384]{1,0:T(8,128)(2,1)S(1)}, bf16[320,384]{1,0:T(8,128)(2,1)S(1)}, u32[]{:S(2)}, u32[]{:S(2)}) collective-permute-start(bf16[320,384]{1,0:T(8,128)(2,1)S(1)} %get-tuple-element.320), channel_id=1, source_target_pairs={{0,9},{1,8},{2,11},{3,10},{4,13},{5,12},{6,15},{7,14},{8,1},{9,0},... | collective-permute-start | bytes 737288 | tf_op jit(solution)/shard_map/ppermute | solution.py:34
  528.3 17.9 %collective-permute-start.107 = (bf16[320,384]{1,0:T(8,128)(2,1)S(1)}, bf16[320,384]{1,0:T(8,128)(2,1)S(1)}, u32[]{:S(2)}, u32[]{:S(2)}) collective-permute-start(bf16[320,384]{1,0:T(8,128)(2,1)S(1)} %get-tuple-element.321), channel_id=1, source_target_pairs={{0,8},{1,9},{2,10},{3,11},{4,12},{5,13},{6,14},{7,15},{8,0},{9,1},... | collective-permute-start | bytes 737288 | tf_op jit(solution)/shard_map/ppermute | solution.py:34
  539.4 12.9 %collective-permute-start.104 = (bf16[320,384]{1,0:T(8,128)(2,1)S(1)}, bf16[320,384]{1,0:T(8,128)(2,1)S(1)}, u32[]{:S(2)}, u32[]{:S(2)}) collective-permute-start(bf16[320,384]{1,0:T(8,128)(2,1)S(1)} %get-tuple-element.346), channel_id=1, source_target_pairs={{0,1},{1,0},{2,3},{3,2},{4,5},{5,4},{6,7},{7,6},{8,9},{9,8},{10,11... | collective-permute-start | bytes 737288 | tf_op jit(solution)/shard_map/ppermute | solution.py:34
  555.2 14.5 %collective-permute-start.109 = (bf16[1024,384]{1,0:T(8,128)(2,1)S(1)}, bf16[1024,384]{1,0:T(8,128)(2,1)}, u32[]{:S(2)}, u32[]{:S(2)}) collective-permute-start(bf16[1024,384]{1,0:T(8,128)(2,1)S(1)} %shard_map.222.refs_0_), channel_id=1, source_target_pairs={{0,4},{1,5},{2,6},{3,7},{4,0},{5,1},{6,2},{7,3},{8,12},{9,13},{10,... | collective-permute-start | bytes 2359304 | tf_op jit(solution)/shard_map/ppermute | solution.py:34
  558.7 38.6 %collective-permute-start.110 = (bf16[768,768]{1,0:T(8,128)(2,1)}, bf16[768,768]{1,0:T(8,128)(2,1)S(1)}, u32[]{:S(2)}, u32[]{:S(2)}) collective-permute-start(bf16[768,768]{1,0:T(8,128)(2,1)} %get-tuple-element.244), channel_id=1, source_target_pairs={{0,3},{1,5},{2,1},{3,7},{4,2},{5,4},{6,0},{7,6},{8,11},{9,13},{10,... | collective-permute-start | bytes 3538952 | tf_op jit(solution)/shard_map/ppermute | solution.py:34
  607.9 22.3 %collective-permute-start.116 = (bf16[1,2,192,768]{3,2,1,0:T(8,128)(2,1)}, bf16[1,2,192,768]{3,2,1,0:T(8,128)(2,1)}, u32[]{:S(2)}, u32[]{:S(2)}) collective-permute-start(bf16[1,2,192,768]{3,2,1,0:T(8,128)(2,1)} %bitcast.53), channel_id=1, source_target_pairs={{0,8},{1,9},{2,10},{3,11},{4,12},{5,13},{6,14},{7,15},{8,0},{9,1},... | collective-permute-start | bytes 1769480 | tf_op jit(solution)/shard_map/ppermute | solution.py:34
  608.9 19.8 %collective-permute-start.112 = (bf16[1024,384]{1,0:T(8,128)(2,1)S(1)}, bf16[1024,384]{1,0:T(8,128)(2,1)}, u32[]{:S(2)}, u32[]{:S(2)}) collective-permute-start(bf16[1024,384]{1,0:T(8,128)(2,1)S(1)} %add.270), channel_id=1, source_target_pairs={{0,16},{1,17},{2,18},{3,19},{4,20},{5,21},{6,22},{7,23},{8,24},{9,... | collective-permute-start | bytes 2359304 | tf_op jit(solution)/shard_map/ppermute | solution.py:34
  612.3 51.4 %collective-permute-start.119 = (bf16[192,768]{1,0:T(8,128)(2,1)}, bf16[192,768]{1,0:T(8,128)(2,1)S(1)}, u32[]{:S(2)}, u32[]{:S(2)}) collective-permute-start(bf16[192,768]{1,0:T(8,128)(2,1)} %select_bitcast_fusion.8), channel_id=1, source_target_pairs={{0,4},{1,5},{2,6},{3,7},{4,0},{5,1},{6,2},{7,3},{8,12},{9,13},{10,... | collective-permute-start | bytes 884744 | tf_op jit(solution)/shard_map/ppermute | solution.py:34
  635.0 44.6 %collective-permute-start.127 = (bf16[768,768]{1,0:T(8,128)(2,1)}, bf16[768,768]{1,0:T(8,128)(2,1)}, u32[]{:S(2)}, u32[]{:S(2)}) collective-permute-start(bf16[768,768]{1,0:T(8,128)(2,1)} %get-tuple-element.285), channel_id=1, source_target_pairs={{0,16},{1,17},{2,18},{3,19},{4,20},{5,21},{6,22},{7,23},{8,24},{9,... | collective-permute-start | bytes 3538952 | tf_op jit(solution)/shard_map/ppermute | solution.py:34
  648.8 15.1 %collective-permute-start.118 = (bf16[192,768]{1,0:T(8,128)(2,1)S(1)}, bf16[192,768]{1,0:T(8,128)(2,1)S(1)}, u32[]{:S(2)}, u32[]{:S(2)}) collective-permute-start(bf16[192,768]{1,0:T(8,128)(2,1)S(1)} %copy-done.140), channel_id=1, source_target_pairs={{0,4},{1,5},{2,6},{3,7},{4,0},{5,1},{6,2},{7,3},{8,12},{9,13},{10,... | collective-permute-start | bytes 884744 | tf_op jit(solution)/shard_map/ppermute | solution.py:34
  657.8 23.9 %collective-permute-start.114 = (bf16[256,768]{1,0:T(8,128)(2,1)S(1)}, bf16[256,768]{1,0:T(8,128)(2,1)S(1)}, u32[]{:S(2)}, u32[]{:S(2)}) collective-permute-start(bf16[256,768]{1,0:T(8,128)(2,1)S(1)} %get-tuple-element.292), channel_id=1, source_target_pairs={{0,2},{1,3},{2,6},{3,7},{4,0},{5,1},{6,4},{7,5},{8,10},{9,11},{10,... | collective-permute-start | bytes 1179656 | tf_op jit(solution)/shard_map/ppermute | solution.py:34
  660.6 21.2 %collective-permute-start.115 = (bf16[256,768]{1,0:T(8,128)(2,1)S(1)}, bf16[256,768]{1,0:T(8,128)(2,1)}, u32[]{:S(2)}, u32[]{:S(2)}) collective-permute-start(bf16[256,768]{1,0:T(8,128)(2,1)S(1)} %get-tuple-element.293), channel_id=1, source_target_pairs={{0,3},{1,2},{2,7},{3,6},{4,1},{5,0},{6,5},{7,4},{8,11},{9,10},{10,... | collective-permute-start | bytes 1179656 | tf_op jit(solution)/shard_map/ppermute | solution.py:34
  (228 other events, 2248.9 us)

commit v4 on v3

--- a/solution.py
+++ b/solution.py
@@ -747,14 +747,14 @@
             strip[head, part, pl.ds(start, length)] += ds.astype(F32)
         own = dot(ds_ref[pl.ds(head * rows, rows), :], keys)
         dq = jnp.where(head_lanes(lanes_all, head), own, dq)
-    dk[...] += dot(ds_ref[...], query_ref[...], (0, 0))
-    dv[...] += dot(a_ref[...].reshape(heads * rows, length), wide_ref[...], (0, 0))
+    dk[...] += dot(query_ref[...], ds_ref[...], (0, 0))
+    dv[...] += dot(wide_ref[...], a_ref[...].reshape(heads * rows, length), (0, 0))
     dp_ref[0, here, :] = (dq * scaling).astype(BF16)
 
     @pl.when(block == length // rows - 1)
     def _():
-        dp_ref[1] = (dk[...] * scaling).astype(BF16)
-        dp_ref[2] = dv[...].astype(BF16)
+        dp_ref[1] = (dk[...].T * scaling).astype(BF16)
+        dp_ref[2] = dv[...].T.astype(BF16)
         sub = lax.broadcasted_iota(jnp.int32, (8, span), 0)
         for head in range(heads):
             part = strip[head]
@@ -802,8 +802,8 @@
         scratch=[
             pltpu.VMEM((256, width), F32),
             pltpu.VMEM((length, lanes), BF16),
-            pltpu.VMEM((length, lanes), F32),
-            pltpu.VMEM((length, lanes), F32),
+            pltpu.VMEM((lanes, length), F32),
+            pltpu.VMEM((lanes, length), F32),
             pltpu.VMEM((heads, BLOCK, span), F32),
             pltpu.VMEM((heads, BLOCK, length), F32),
             pltpu.VMEM((heads * BLOCK, length), BF16),
@@ -1035,7 +1035,7 @@
     expert_grads = expert_weight_grads(*arrived, *grad_arrived, active, hidden)
     first = send(expert_grads[0], weights_home(0))
     grad_normed_two = from_expert(
-        parts, slot_column, experts, tuple(expert_grads), at_lower, first
+        parts, slot_column, experts, tuple(expert_grads), at_lower
     )
     second = send(after(expert_grads[1], grad_normed_two[0]), weights_home(1))
     grad_router = dot(normed_two, grad_logits, (0, 0))[:, :experts]

time: 698 us -> 684 us (0.980)
  waiting for transfers between devices: 216 us -> 208 us
    ppermute x128, waiting for transfers between devices: 216 us -> 208 us  [send(): return lax.ppermute(value, AXES, pairs)]
    unnamed x337 -> x329, local copies, waits for them, and re-layouts: 32.6 us -> 33.3 us
  transfers between devices with their start and end apart: 128 -> 128, of which waited for: 55 -> 56; matrix products, arithmetic and copies ran while one was open for 10% -> 10% of each run, Pallas kernels for 22% -> 22%
where the time goes in v4:
time: 684 us; the launch traced here: 674 us
  waiting for transfers between devices  208 us (30%)
  Pallas kernels  197 us (29%)
  starting transfers between devices  160 us (23%)
  local copies, waits for them, and re-layouts  49.8 us (7%)
  other arithmetic  49.4 us (7%)
    ppermute x128, waiting for transfers between devices, send(): return lax.ppermute(value, AXES, pairs)  208 us
    pallas_call x22, Pallas kernels, call(): pl.pallas_call(kernel, grid=grid, in_specs=[spec(item) for item in inputs...  197 us
    ppermute x128, starting transfers between devices, send(): return lax.ppermute(value, AXES, pairs)  160 us
    unnamed x329, local copies, waits for them, and re-layouts  33.3 us
  transfers between devices with their start and end apart: 128, of which 56 were waited for; matrix products, arithmetic and copies ran while one was open for 10% of the time, Pallas kernels for 22%

profile of v4, /device:TPU:0, one launch (start us, length us, event | category | flops | bytes accessed | tf_op | source)
XLA Modules:
  0.0 673.8 jit_solution(4707480390059085091)
XLA Ops:
  23.5 8.0 %collective-permute-done.refs_0_ = bf16[256,768]{1,0:T(8,128)(2,1)} collective-permute-done((bf16[256,768]{1,0:T(8,128)(2,1)}, bf16[256,768]{1,0:T(8,128)(2,1)}, u32[]{:S(2)}, u32[]{:S(2)}) %collective-permute-start) | collective-permute-done | bytes 393248 | tf_op jit(solution)/shard_map/ppermute | solution.py:34
  33.7 4.3 collective-permute-start.18
  39.1 3.2 collective-permute-done.18
  60.0 20.2 %shard_map.204 = (bf16[1024,768]{1,0:T(8,128)(2,1)}, bf16[1024,768]{1,0:T(8,128)(2,1)}, bf16[3,1024,192]{2,1,0:T(8,128)(2,1)}, bf16[3,768,192]{2,1,0:T(8,128)(2,...) custom-call(bf16[256,768]{1,0:T(8,128)(2,1)} %collective-permute-done.refs_0_, ...), custom_call_target="tpu_custom_call" | custom-call | flops 99999997952 | bytes 1000 | tf_op jit(solution)/shard_map/pallas_call | solution.py:178
  80.2 6.9 %collective-permute-start.13 = (bf16[512,384]{1,0:T(8,128)(2,1)}, bf16[512,384]{1,0:T(8,128)(2,1)S(1)}, u32[]{:S(2)}, u32[]{:S(2)}) collective-permute-start(bf16[512,384]{1,0:T(8,128)(2,1)} %get-tuple-element.140.refs_1_.own_ref), channel_id=1, source_target_pairs={{0,16},{1,17},{2,18},{3,19},{4,20},{5,21},{6,22},{7,23},{8,24},{9,... | collective-permute-start | bytes 1179656 | tf_op jit(solution)/shard_map/ppermute | solution.py:34
  91.6 3.5 collective-permute-done.13.refs_2_
  99.0 7.8 %shard_map.205 = (f32[1024,768]{1,0:T(8,128)S(1)}, bf16[1024,768]{1,0:T(8,128)(2,1)S(1)}, f32[1024,1]{1,0:T(8,128)S(1)}, bf16[320,384]{1,0:T(8,128)(2,1)S(1)}, b...) custom-call(bf16[1024,768]{1,0:T(8,128)(2,1)S(1)} %copy-done.3, ...), custom_call_target="tpu_custom_call" | custom-call | flops 1000000000 | bytes 1000 | tf_op jit(solution)/shard_map/pallas_call | solution.py:178
  113.9 7.3 %collective-permute-done.21.refs_1_ = bf16[320,384]{1,0:T(8,128)(2,1)S(1)} collective-permute-done((bf16[320,384]{1,0:T(8,128)(2,1)S(1)}, bf16[320,384]{1,0:T(8,128)(2,1)S(1)}, u32[]{:S(2)}, u32[]{:S(2)}) %collective-permute-start.21) | collective-permute-done | bytes 245792 | tf_op jit(solution)/shard_map/ppermute | solution.py:34
  121.8 5.7 collective-permute-done.23.refs_3_
  128.3 4.0 collective-permute-start.32
  132.3 8.0 %shard_map.206 = (bf16[1280,768]{1,0:T(8,128)(2,1)S(1)}, bf16[1280,768]{1,0:T(8,128)(2,1)S(1)}, bf16[640,384]{1,0:T(8,128)(2,1)S(1)}, bf16[640,384]{1,0:T(8,128)...) custom-call(bf16[320,384]{1,0:T(8,128)(2,1)S(1)} %get-tuple-element.143.refs_0_, ...), custom_call_target="tpu_custom_call" | custom-call | flops 1000000000 | bytes 1000 | tf_op jit(solution)/shard_map/pallas_call | solution.py:178
  153.1 7.9 %collective-permute-done.38 = bf16[640,384]{1,0:T(8,128)(2,1)} collective-permute-done((bf16[640,384]{1,0:T(8,128)(2,1)}, bf16[640,384]{1,0:T(8,128)(2,1)}, u32[]{:S(2)}, u32[]{:S(2)}) %collective-permute-start.38) | collective-permute-done | bytes 491552 | tf_op jit(solution)/shard_map/ppermute | solution.py:34
  165.8 5.4 collective-permute-done.30
  174.0 3.4 collective-permute-start.40
  178.2 3.6 collective-permute-start.41
  181.9 2.9 shard_map.207.refs_2_
  184.8 3.7 collective-permute-done.41
  190.0 6.4 collective-permute-done.49
  196.6 3.8 collective-permute-start.45
  201.3 22.1 %shard_map.208 = (bf16[1024,768]{1,0:T(8,128)(2,1)}, bf16[1024,768]{1,0:T(8,128)(2,1)}, bf16[3,1024,192]{2,1,0:T(8,128)(2,1)}, bf16[3,768,192]{2,1,0:T(8,128)(2,...) custom-call(f32[1024,768]{1,0:T(8,128)} %copy-done.30, f32[1024,1]{1,0:T(8,128)} %copy-done.84, ...), custom_call_target="tpu_custom_call" | custom-call | flops 99999997952 | bytes 1000 | tf_op jit(solution)/shard_map/pallas_call | solution.py:178
  226.4 3.1 collective-permute-start.47
  229.5 3.3 collective-permute-done.46.refs_2_
  238.4 7.8 %shard_map.209 = (f32[1024,768]{1,0:T(8,128)S(1)}, bf16[1024,768]{1,0:T(8,128)(2,1)S(1)}, f32[1024,1]{1,0:T(8,128)S(1)}, bf16[320,384]{1,0:T(8,128)(2,1)S(1)}, b...) custom-call(bf16[1024,768]{1,0:T(8,128)(2,1)S(1)} %copy-done, ...), custom_call_target="tpu_custom_call" | custom-call | flops 1000000000 | bytes 1000 | tf_op jit(solution)/shard_map/pallas_call | solution.py:178
  253.3 5.3 collective-permute-done.51.refs_1_
  259.2 4.3 collective-permute-done.53.refs_3_
  265.0 7.4 %shard_map.210 = (bf16[1280,768]{1,0:T(8,128)(2,1)S(1)}, bf16[1280,768]{1,0:T(8,128)(2,1)S(1)}, bf16[640,384]{1,0:T(8,128)(2,1)S(1)}, bf16[640,384]{1,0:T(8,128)...) custom-call(bf16[320,384]{1,0:T(8,128)(2,1)S(1)} %get-tuple-element.161.refs_0_, ...), custom_call_target="tpu_custom_call" | custom-call | flops 1000000000 | bytes 1000 | tf_op jit(solution)/shard_map/pallas_call | solution.py:178
  281.9 6.8 %collective-permute-done.59 = bf16[640,384]{1,0:T(8,128)(2,1)S(1)} collective-permute-done((bf16[640,384]{1,0:T(8,128)(2,1)S(1)}, bf16[640,384]{1,0:T(8,128)(2,1)S(1)}, u32[]{:S(2)}, u32[]{:S(2)}) %collective-permute-start.59) | collective-permute-done | bytes 491552 | tf_op jit(solution)/shard_map/ppermute | solution.py:34
  291.2 7.6 %collective-permute-done.64 = bf16[640,384]{1,0:T(8,128)(2,1)S(1)} collective-permute-done((bf16[640,384]{1,0:T(8,128)(2,1)S(1)}, bf16[640,384]{1,0:T(8,128)(2,1)S(1)}, u32[]{:S(2)}, u32[]{:S(2)}) %collective-permute-start.64) | collective-permute-done | bytes 491552 | tf_op jit(solution)/shard_map/ppermute | solution.py:34
  304.2 4.3 collective-permute-done.66.refs_4_
  308.5 5.2 collective-permute-done.65.refs_3_
  316.6 4.9 shard_map.211.refs_2_
  325.7 6.5 shard_map.212
  337.6 5.3 collective-permute-done.72.refs_1_.refs_9_
  342.8 5.7 collective-permute-done.73.refs_2_.refs_10_
  350.4 6.7 %shard_map.213 = (bf16[1280,768]{1,0:T(8,128)(2,1)S(1)}, bf16[640,384]{1,0:T(8,128)(2,1)S(1)}, bf16[640,384]{1,0:T(8,128)(2,1)S(1)}, bf16[640,384]{1,0:T(8,128)(2,1)S(1)}, bf16[640,384]{1,0:T(8,128)(2,1)S(1)}) custom-call(bf16[320,384]{1,0:T(8,128)(2,1)S(1)} %get-tuple-element.174.refs_0_.refs_8_, ...), custom_call_target="tpu_custom_call" | custom-call | flops 1000000000 | bytes 1000 | tf_op jit(solution)/shard_map/pallas_call | solution.py:178
  362.8 8.8 %shard_map.214 = (bf16[768,768]{1,0:T(8,128)(2,1)}, bf16[768,768]{1,0:T(8,128)(2,1)}) custom-call(bf16[320,384]{1,0:T(8,128)(2,1)} %copy-done.56, bf16[320,384]{1,0:T(8,128)(2,1)} %copy-done.57, bf16[320,384]{1,0:T(8,128)(2,1)} %copy-done.58, bf16[320,384]{1,0:T(8,128)(2,1)} %copy-done.59, bf16[320,384]{1,0:T(8,128)(2,1)} %copy-done.60, ...), custom_call_target="tpu_custom_call" | custom-call | flops 1000000000 | bytes 1000 | tf_op jit(solution)/shard_map/pallas_call | solution.py:178
  371.6 3.1 collective-permute-done.80
  375.4 9.1 %collective-permute-done.83 = bf16[640,384]{1,0:T(8,128)(2,1)S(1)} collective-permute-done((bf16[640,384]{1,0:T(8,128)(2,1)S(1)}, bf16[640,384]{1,0:T(8,128)(2,1)S(1)}, u32[]{:S(2)}, u32[]{:S(2)}) %collective-permute-start.83) | collective-permute-done | bytes 491552 | tf_op jit(solution)/shard_map/ppermute | solution.py:34
  386.5 6.2 collective-permute-done.85.refs_4_
  392.8 4.8 collective-permute-done.84.refs_3_
  397.5 2.9 shard_map.215.refs_0_
  400.5 2.9 collective-permute-start.87
  404.3 26.2 %shard_map.216 = (f32[1024,768]{1,0:T(8,128)}, bf16[1024,768]{1,0:T(8,128)(2,1)}, f32[1,768]{1,0:T(1,128)}, bf16[3,1024,192]{2,1,0:T(8,128)(2,1)}, f32[3,2048]{1...) custom-call(bf16[1024,384]{1,0:T(8,128)(2,1)} %copy-done.105, bf16[1024,384]{1,0:T(8,128)(2,1)} %copy-done.148, ...), custom_call_target="tpu_custom_call" | custom-call | flops 99999997952 | bytes 1000 | tf_op jit(solution)/shard_map/pallas_call | solution.py:178
  430.6 5.6 shard_map.217
  444.0 8.1 %collective-permute-done.70 = bf16[256,768]{1,0:T(8,128)(2,1)S(1)} collective-permute-done((bf16[256,768]{1,0:T(8,128)(2,1)S(1)}, bf16[256,768]{1,0:T(8,128)(2,1)S(1)}, u32[]{:S(2)}, u32[]{:S(2)}) %collective-permute-start.70) | collective-permute-done | bytes 393248 | tf_op jit(solution)/shard_map/ppermute | solution.py:34
  452.2 6.3 collective-permute-done.71
  464.5 4.6 shard_map.219
  469.9 4.0 collective-permute-start.92
  475.4 5.3 collective-permute-done.92.refs_1_.refs_9_
  480.6 6.2 collective-permute-done.93.refs_2_.refs_10_
  488.7 6.5 shard_map.220
  496.5 3.6 collective-permute-start.99
  501.8 8.8 %shard_map.221 = (bf16[768,768]{1,0:T(8,128)(2,1)}, bf16[768,768]{1,0:T(8,128)(2,1)}) custom-call(bf16[320,384]{1,0:T(8,128)(2,1)} %copy-done.48, bf16[320,384]{1,0:T(8,128)(2,1)} %copy-done.49, bf16[320,384]{1,0:T(8,128)(2,1)} %copy-done.50, bf16[320,384]{1,0:T(8,128)(2,1)} %copy-done.51, bf16[320,384]{1,0:T(8,128)(2,1)} %copy-done.52, ...), custom_call_target="tpu_custom_call" | custom-call | flops 1000000000 | bytes 1000 | tf_op jit(solution)/shard_map/pallas_call | solution.py:178
  517.2 7.5 %collective-permute-done.100 = bf16[640,384]{1,0:T(8,128)(2,1)S(1)} collective-permute-done((bf16[640,384]{1,0:T(8,128)(2,1)S(1)}, bf16[640,384]{1,0:T(8,128)(2,1)S(1)}, u32[]{:S(2)}, u32[]{:S(2)}) %collective-permute-start.100) | collective-permute-done | bytes 491552 | tf_op jit(solution)/shard_map/ppermute | solution.py:34
  525.9 2.8 collective-permute-done.105.refs_3_
  528.6 3.0 collective-permute-done.102.refs_2_
  531.6 2.8 shard_map.222.refs_0_
  537.0 26.4 %shard_map.223 = (f32[1024,768]{1,0:T(8,128)}, bf16[1024,768]{1,0:T(8,128)(2,1)}, f32[1,768]{1,0:T(1,128)}, bf16[3,1024,192]{2,1,0:T(8,128)(2,1)}, f32[3,2048]{1...) custom-call(bf16[1024,384]{1,0:T(8,128)(2,1)} %copy-done.104, ...), custom_call_target="tpu_custom_call" | custom-call | flops 99999997952 | bytes 1000 | tf_op jit(solution)/shard_map/pallas_call | solution.py:178
  571.0 5.7 shard_map.224
  583.8 13.9 %collective-permute-done.110 = bf16[1024,384]{1,0:T(8,128)(2,1)} collective-permute-done((bf16[1024,384]{1,0:T(8,128)(2,1)S(1)}, bf16[1024,384]{1,0:T(8,128)(2,1)}, u32[]{:S(2)}, u32[]{:S(2)}) %collective-permute-start.110) | collective-permute-done | bytes 786464 | tf_op jit(solution)/shard_map/ppermute | solution.py:34
  600.9 3.6 fusion.2
  612.6 23.7 %collective-permute-start.120 = (f32[2,4992]{1,0:T(2,128)S(1)}, f32[2,4992]{1,0:T(2,128)S(1)}, u32[]{:S(2)}, u32[]{:S(2)}) collective-permute-start(f32[2,4992]{1,0:T(2,128)S(1)} %pad_maximum_fusion.15), channel_id=1, source_target_pairs={{0,2},{1,3},{2,0},{3,1},{4,6},{5,7},{6,4},{7,5},{8,10},{9,11},{10,... | collective-permute-start | bytes 119816 | tf_op jit(solution)/shard_map/ppermute | solution.py:34
  636.3 3.5 collective-permute-start.121
  654.8 5.9 collective-permute-done.124
  (711 shorter events, 226.2 us)
Async XLA Ops:
  2.3 13.3 %collective-permute-start.10 = (bf16[2052]{0:T(1024)(128)(2,1)S(1)}, bf16[2052]{0:T(1024)(128)(2,1)S(1)}, u32[]{:S(2)}, u32[]{:S(2)}) collective-permute-start(bf16[2052]{0:T(1024)(128)(2,1)S(1)} %concatenate.83), channel_id=1, source_target_pairs={{0,4},{1,5},{2,6},{3,7},{4,0},{5,1},{6,2},{7,3},{8,12},{9,13},{10,... | collective-permute-start | bytes 12320 | tf_op jit(solution)/shard_map/ppermute | solution.py:34
  6.3 16.5 %collective-permute-start.4 = (bf16[192,768]{1,0:T(8,128)(2,1)}, bf16[192,768]{1,0:T(8,128)(2,1)}, u32[]{:S(2)}, u32[]{:S(2)}) collective-permute-start(bf16[192,768]{1,0:T(8,128)(2,1)} %pad_maximum_fusion.11), channel_id=1, source_target_pairs={{0,16},{1,17},{2,18},{3,19},{4,20},{5,21},{6,22},{7,23},{8,24},{9,... | collective-permute-start | bytes 884744 | tf_op jit(solution)/shard_map/ppermute | solution.py:34
  9.7 13.8 %collective-permute-start.1 = (bf16[256,768]{1,0:T(8,128)(2,1)}, bf16[256,768]{1,0:T(8,128)(2,1)}, u32[]{:S(2)}, u32[]{:S(2)}) collective-permute-start(bf16[256,768]{1,0:T(8,128)(2,1)} %get-tuple-element.326), channel_id=1, source_target_pairs={{0,5},{1,4},{2,1},{3,0},{4,7},{5,6},{6,3},{7,2},{8,13},{9,12},{10,... | collective-permute-start | bytes 1179656 | tf_op jit(solution)/shard_map/ppermute | solution.py:34
  11.1 20.3 %collective-permute-start = (bf16[256,768]{1,0:T(8,128)(2,1)}, bf16[256,768]{1,0:T(8,128)(2,1)}, u32[]{:S(2)}, u32[]{:S(2)}) collective-permute-start(bf16[256,768]{1,0:T(8,128)(2,1)} %get-tuple-element.327), channel_id=1, source_target_pairs={{0,4},{1,5},{2,0},{3,1},{4,6},{5,7},{6,2},{7,3},{8,12},{9,13},{10,... | collective-permute-start | bytes 1179656 | tf_op jit(solution)/shard_map/ppermute | solution.py:34
  22.8 30.0 %collective-permute-start.5 = (bf16[768,768]{1,0:T(8,128)(2,1)}, bf16[768,768]{1,0:T(8,128)(2,1)S(1)}, u32[]{:S(2)}, u32[]{:S(2)}) collective-permute-start(bf16[768,768]{1,0:T(8,128)(2,1)} %broadcast_select_fusion.4), channel_id=1, source_target_pairs={{0,16},{1,17},{2,18},{3,19},{4,20},{5,21},{6,22},{7,23},{8,24},{9,... | collective-permute-start | bytes 3538952 | tf_op jit(solution)/shard_map/ppermute | solution.py:34
  44.6 12.3 %collective-permute-start.3 = (bf16[256,768]{1,0:T(8,128)(2,1)}, bf16[256,768]{1,0:T(8,128)(2,1)S(1)}, u32[]{:S(2)}, u32[]{:S(2)}) collective-permute-start(bf16[256,768]{1,0:T(8,128)(2,1)} %collective-permute-done.1.refs_1_), channel_id=1, source_target_pairs={{0,4},{1,5},{2,6},{3,7},{4,0},{5,1},{6,2},{7,3},{8,12},{9,13},{10,... | collective-permute-start | bytes 1179656 | tf_op jit(solution)/shard_map/ppermute | solution.py:34
  45.1 11.8 %collective-permute-start.2 = (bf16[256,768]{1,0:T(8,128)(2,1)}, bf16[256,768]{1,0:T(8,128)(2,1)S(1)}, u32[]{:S(2)}, u32[]{:S(2)}) collective-permute-start(bf16[256,768]{1,0:T(8,128)(2,1)} %collective-permute-done.refs_0_), channel_id=1, source_target_pairs={{0,4},{1,5},{2,6},{3,7},{4,0},{5,1},{6,2},{7,3},{8,12},{9,13},{10,... | collective-permute-start | bytes 1179656 | tf_op jit(solution)/shard_map/ppermute | solution.py:34
  52.9 42.2 %collective-permute-start.20 = (bf16[4,2,96,384]{3,2,0,1:T(8,128)(2,1)}, bf16[4,2,96,384]{3,2,0,1:T(8,128)(2,1)}, u32[]{:S(2)}, u32[]{:S(2)}) collective-permute-start(bf16[4,2,96,384]{3,2,0,1:T(8,128)(2,1)} %pad_maximum_fusion.9), channel_id=1, source_target_pairs={{0,4},{1,5},{2,6},{3,7},{4,0},{5,1},{6,2},{7,3},{8,12},{9,13},{10,... | collective-permute-start | bytes 1769480 | tf_op jit(solution)/shard_map/ppermute | solution.py:34
  56.8 23.4 %collective-permute-start.12 = (bf16[768,768]{1,0:T(8,128)(2,1)}, bf16[768,768]{1,0:T(8,128)(2,1)S(1)}, u32[]{:S(2)}, u32[]{:S(2)}) collective-permute-start(bf16[768,768]{1,0:T(8,128)(2,1)} %get-tuple-element.279), channel_id=1, source_target_pairs={{0,4},{1,0},{2,6},{3,2},{4,7},{5,3},{6,5},{7,1},{8,12},{9,8},{10,1... | collective-permute-start | bytes 3538952 | tf_op jit(solution)/shard_map/ppermute | solution.py:34
  80.2 14.8 %collective-permute-start.13 = (bf16[512,384]{1,0:T(8,128)(2,1)}, bf16[512,384]{1,0:T(8,128)(2,1)S(1)}, u32[]{:S(2)}, u32[]{:S(2)}) collective-permute-start(bf16[512,384]{1,0:T(8,128)(2,1)} %get-tuple-element.140.refs_1_.own_ref), channel_id=1, source_target_pairs={{0,16},{1,17},{2,18},{3,19},{4,20},{5,21},{6,22},{7,23},{8,24},{9,... | collective-permute-start | bytes 1179656 | tf_op jit(solution)/shard_map/ppermute | solution.py:34
  88.0 39.5 %collective-permute-start.28 = (bf16[768,768]{1,0:T(8,128)(2,1)}, bf16[768,768]{1,0:T(8,128)(2,1)S(1)}, u32[]{:S(2)}, u32[]{:S(2)}) collective-permute-start(bf16[768,768]{1,0:T(8,128)(2,1)} %get-tuple-element.279), channel_id=1, source_target_pairs={{0,6},{1,2},{2,4},{3,0},{4,5},{5,1},{6,7},{7,3},{8,14},{9,10},{10,... | collective-permute-start | bytes 3538952 | tf_op jit(solution)/shard_map/ppermute | solution.py:34
  113.7 13.7 %collective-permute-start.23 = (bf16[320,384]{1,0:T(8,128)(2,1)S(1)}, bf16[320,384]{1,0:T(8,128)(2,1)S(1)}, u32[]{:S(2)}, u32[]{:S(2)}) collective-permute-start(bf16[320,384]{1,0:T(8,128)(2,1)S(1)} %get-tuple-element.146), channel_id=1, source_target_pairs={{0,9},{1,8},{2,11},{3,10},{4,13},{5,12},{6,15},{7,14},{8,1},{9,0},... | collective-permute-start | bytes 737288 | tf_op jit(solution)/shard_map/ppermute | solution.py:34
  113.9 14.3 %collective-permute-start.24 = (bf16[320,384]{1,0:T(8,128)(2,1)S(1)}, bf16[320,384]{1,0:T(8,128)(2,1)S(1)}, u32[]{:S(2)}, u32[]{:S(2)}) collective-permute-start(bf16[320,384]{1,0:T(8,128)(2,1)S(1)} %get-tuple-element.143.refs_0_), channel_id=1, source_target_pairs={{0,4},{1,5},{2,6},{3,7},{4,0},{5,1},{6,2},{7,3},{8,12},{9,13},{10,... | collective-permute-start | bytes 737288 | tf_op jit(solution)/shard_map/ppermute | solution.py:34
  127.6 15.9 %collective-permute-start.31 = (bf16[192,576]{1,0:T(8,128)(2,1)S(1)}, bf16[192,576]{1,0:T(8,128)(2,1)S(1)}, u32[]{:S(2)}, u32[]{:S(2)}) collective-permute-start(bf16[192,576]{1,0:T(8,128)(2,1)S(1)} %slice.387), channel_id=1, source_target_pairs={{4,6},{5,7},{6,4},{7,5},{12,14},{13,15},{14,12},{15,13},{16,17},{1... | collective-permute-start | bytes 663560 | tf_op jit(solution)/shard_map/ppermute | solution.py:34
  128.3 15.9 %collective-permute-start.32 = (bf16[192,576]{1,0:T(8,128)(2,1)S(1)}, bf16[192,576]{1,0:T(8,128)(2,1)S(1)}, u32[]{:S(2)}, u32[]{:S(2)}) collective-permute-start(bf16[192,576]{1,0:T(8,128)(2,1)S(1)} %slice.387), channel_id=1, source_target_pairs={{0,6},{1,7},{2,4},{3,5},{4,0},{5,1},{6,2},{7,3},{8,14},{9,15},{10,... | collective-permute-start | bytes 663560 | tf_op jit(solution)/shard_map/ppermute | solution.py:34
  144.2 27.1 %collective-permute-start.35 = (bf16[768,768]{1,0:T(8,128)(2,1)}, bf16[768,768]{1,0:T(8,128)(2,1)S(1)}, u32[]{:S(2)}, u32[]{:S(2)}) collective-permute-start(bf16[768,768]{1,0:T(8,128)(2,1)} %get-tuple-element.157), channel_id=1, source_target_pairs={{0,4},{1,0},{2,6},{3,2},{4,7},{5,3},{6,5},{7,1},{8,12},{9,8},{10,1... | collective-permute-start | bytes 3538952 | tf_op jit(solution)/shard_map/ppermute | solution.py:34
  146.6 14.4 %collective-permute-start.38 = (bf16[640,384]{1,0:T(8,128)(2,1)}, bf16[640,384]{1,0:T(8,128)(2,1)}, u32[]{:S(2)}, u32[]{:S(2)}) collective-permute-start(bf16[640,384]{1,0:T(8,128)(2,1)} %add.241), channel_id=1, source_target_pairs={{0,16},{1,17},{2,18},{3,19},{4,20},{5,21},{6,22},{7,23},{8,24},{9,... | collective-permute-start | bytes 1474568 | tf_op jit(solution)/shard_map/ppermute | solution.py:34
  148.5 22.8 %collective-permute-start.30 = (bf16[640,384]{1,0:T(8,128)(2,1)S(1)}, bf16[640,384]{1,0:T(8,128)(2,1)S(1)}, u32[]{:S(2)}, u32[]{:S(2)}) collective-permute-start(bf16[640,384]{1,0:T(8,128)(2,1)S(1)} %add.239), channel_id=1, source_target_pairs={{0,16},{1,17},{2,18},{3,19},{4,20},{5,21},{6,22},{7,23},{8,24},{9,... | collective-permute-start | bytes 1474568 | tf_op jit(solution)/shard_map/ppermute | solution.py:34
  151.0 14.8 %collective-permute-start.33 = (bf16[192,576]{1,0:T(8,128)(2,1)}, bf16[192,576]{1,0:T(8,128)(2,1)S(1)}, u32[]{:S(2)}, u32[]{:S(2)}) collective-permute-start(bf16[192,576]{1,0:T(8,128)(2,1)} %broadcast_select_fusion.20.refs_4_), channel_id=1, source_target_pairs={{0,8},{1,9},{2,10},{3,11},{4,12},{5,13},{6,14},{7,15},{8,0},{9,1},... | collective-permute-start | bytes 663560 | tf_op jit(solution)/shard_map/ppermute | solution.py:34
  151.6 13.1 %collective-permute-start.34 = (bf16[192,576]{1,0:T(8,128)(2,1)}, bf16[192,576]{1,0:T(8,128)(2,1)S(1)}, u32[]{:S(2)}, u32[]{:S(2)}) collective-permute-start(bf16[192,576]{1,0:T(8,128)(2,1)} %copy-done.151), channel_id=1, source_target_pairs={{0,8},{1,9},{2,10},{3,11},{4,12},{5,13},{6,14},{7,15},{8,0},{9,1},... | collective-permute-start | bytes 663560 | tf_op jit(solution)/shard_map/ppermute | solution.py:34
  162.4 15.8 %collective-permute-start.43 = (bf16[320,384]{1,0:T(8,128)(2,1)S(1)}, bf16[320,384]{1,0:T(8,128)(2,1)S(1)}, u32[]{:S(2)}, u32[]{:S(2)}) collective-permute-start(bf16[320,384]{1,0:T(8,128)(2,1)S(1)} %get-tuple-element.318), channel_id=1, source_target_pairs={{0,9},{1,8},{2,11},{3,10},{4,13},{5,12},{6,15},{7,14},{8,1},{9,0},... | collective-permute-start | bytes 737288 | tf_op jit(solution)/shard_map/ppermute | solution.py:34
  164.7 17.1 %collective-permute-start.42 = (bf16[320,384]{1,0:T(8,128)(2,1)S(1)}, bf16[320,384]{1,0:T(8,128)(2,1)S(1)}, u32[]{:S(2)}, u32[]{:S(2)}) collective-permute-start(bf16[320,384]{1,0:T(8,128)(2,1)S(1)} %get-tuple-element.319), channel_id=1, source_target_pairs={{0,8},{1,9},{2,10},{3,11},{4,12},{5,13},{6,14},{7,15},{8,0},{9,1},... | collective-permute-start | bytes 737288 | tf_op jit(solution)/shard_map/ppermute | solution.py:34
  184.7 15.7 %collective-permute-start.44 = (bf16[1024,384]{1,0:T(8,128)(2,1)S(1)}, bf16[1024,384]{1,0:T(8,128)(2,1)S(1)}, u32[]{:S(2)}, u32[]{:S(2)}) collective-permute-start(bf16[1024,384]{1,0:T(8,128)(2,1)S(1)} %shard_map.207.refs_2_), channel_id=1, source_target_pairs={{0,4},{1,5},{2,6},{3,7},{4,0},{5,1},{6,2},{7,3},{8,12},{9,13},{10,... | collective-permute-start | bytes 2359304 | tf_op jit(solution)/shard_map/ppermute | solution.py:34
  196.6 39.0 %collective-permute-start.50 = (bf16[4,2,96,384]{3,2,0,1:T(8,128)(2,1)S(1)}, bf16[4,2,96,384]{3,2,0,1:T(8,128)(2,1)S(1)}, u32[]{:S(2)}, u32[]{:S(2)}) collective-permute-start(bf16[4,2,96,384]{3,2,0,1:T(8,128)(2,1)S(1)} %pad_maximum_fusion.10), channel_id=1, source_target_pairs={{0,4},{1,5},{2,6},{3,7},{4,0},{5,1},{6,2},{7,3},{8,12},{9,13},{10,... | collective-permute-start | bytes 1769480 | tf_op jit(solution)/shard_map/ppermute | solution.py:34
  196.6 26.8 %collective-permute-start.45 = (bf16[768,768]{1,0:T(8,128)(2,1)}, bf16[768,768]{1,0:T(8,128)(2,1)S(1)}, u32[]{:S(2)}, u32[]{:S(2)}) collective-permute-start(bf16[768,768]{1,0:T(8,128)(2,1)} %get-tuple-element.157), channel_id=1, source_target_pairs={{0,6},{1,2},{2,4},{3,0},{4,5},{5,1},{6,7},{7,3},{8,14},{9,10},{10,... | collective-permute-start | bytes 3538952 | tf_op jit(solution)/shard_map/ppermute | solution.py:34
  250.9 12.6 %collective-permute-start.53 = (bf16[320,384]{1,0:T(8,128)(2,1)S(1)}, bf16[320,384]{1,0:T(8,128)(2,1)S(1)}, u32[]{:S(2)}, u32[]{:S(2)}) collective-permute-start(bf16[320,384]{1,0:T(8,128)(2,1)S(1)} %get-tuple-element.164), channel_id=1, source_target_pairs={{0,9},{1,8},{2,11},{3,10},{4,13},{5,12},{6,15},{7,14},{8,1},{9,0},... | collective-permute-start | bytes 737288 | tf_op jit(solution)/shard_map/ppermute | solution.py:34
  274.6 14.1 %collective-permute-start.59 = (bf16[640,384]{1,0:T(8,128)(2,1)S(1)}, bf16[640,384]{1,0:T(8,128)(2,1)S(1)}, u32[]{:S(2)}, u32[]{:S(2)}) collective-permute-start(bf16[640,384]{1,0:T(8,128)(2,1)S(1)} %add.245), channel_id=1, source_target_pairs={{0,16},{1,17},{2,18},{3,19},{4,20},{5,21},{6,22},{7,23},{8,24},{9,... | collective-permute-start | bytes 1474568 | tf_op jit(solution)/shard_map/ppermute | solution.py:34
  276.8 21.9 %collective-permute-start.64 = (bf16[640,384]{1,0:T(8,128)(2,1)S(1)}, bf16[640,384]{1,0:T(8,128)(2,1)S(1)}, u32[]{:S(2)}, u32[]{:S(2)}) collective-permute-start(bf16[640,384]{1,0:T(8,128)(2,1)S(1)} %add.247), channel_id=1, source_target_pairs={{0,16},{1,17},{2,18},{3,19},{4,20},{5,21},{6,22},{7,23},{8,24},{9,... | collective-permute-start | bytes 1474568 | tf_op jit(solution)/shard_map/ppermute | solution.py:34
  278.4 25.3 %collective-permute-start.61 = (bf16[256,768]{1,0:T(8,128)(2,1)}, bf16[256,768]{1,0:T(8,128)(2,1)}, u32[]{:S(2)}, u32[]{:S(2)}) collective-permute-start(bf16[256,768]{1,0:T(8,128)(2,1)} %get-tuple-element.324), channel_id=1, source_target_pairs={{0,5},{1,4},{2,1},{3,0},{4,7},{5,6},{6,3},{7,2},{8,13},{9,12},{10,... | collective-permute-start | bytes 1179656 | tf_op jit(solution)/shard_map/ppermute | solution.py:34
  279.4 24.3 %collective-permute-start.60 = (bf16[256,768]{1,0:T(8,128)(2,1)}, bf16[256,768]{1,0:T(8,128)(2,1)}, u32[]{:S(2)}, u32[]{:S(2)}) collective-permute-start(bf16[256,768]{1,0:T(8,128)(2,1)} %get-tuple-element.325), channel_id=1, source_target_pairs={{0,4},{1,5},{2,0},{3,1},{4,6},{5,7},{6,2},{7,3},{8,12},{9,13},{10,... | collective-permute-start | bytes 1179656 | tf_op jit(solution)/shard_map/ppermute | solution.py:34
  289.6 14.6 %collective-permute-start.62 = (bf16[320,384]{1,0:T(8,128)(2,1)}, bf16[320,384]{1,0:T(8,128)(2,1)}, u32[]{:S(2)}, u32[]{:S(2)}) collective-permute-start(bf16[320,384]{1,0:T(8,128)(2,1)} %get-tuple-element.344), channel_id=1, source_target_pairs={{0,1},{1,0},{2,3},{3,2},{4,5},{5,4},{6,7},{7,6},{8,9},{9,8},{10,11... | collective-permute-start | bytes 737288 | tf_op jit(solution)/shard_map/ppermute | solution.py:34
  301.8 11.9 %collective-permute-start.65 = (bf16[320,384]{1,0:T(8,128)(2,1)}, bf16[320,384]{1,0:T(8,128)(2,1)}, u32[]{:S(2)}, u32[]{:S(2)}) collective-permute-start(bf16[320,384]{1,0:T(8,128)(2,1)} %get-tuple-element.317), channel_id=1, source_target_pairs={{0,8},{1,9},{2,10},{3,11},{4,12},{5,13},{6,14},{7,15},{8,0},{9,1},... | collective-permute-start | bytes 737288 | tf_op jit(solution)/shard_map/ppermute | solution.py:34
  303.7 17.8 %collective-permute-start.69 = (bf16[256,768]{1,0:T(8,128)(2,1)}, bf16[256,768]{1,0:T(8,128)(2,1)}, u32[]{:S(2)}, u32[]{:S(2)}) collective-permute-start(bf16[256,768]{1,0:T(8,128)(2,1)} %collective-permute-done.61), channel_id=1, source_target_pairs={{0,4},{1,5},{2,6},{3,7},{4,0},{5,1},{6,2},{7,3},{8,12},{9,13},{10,... | collective-permute-start | bytes 1179656 | tf_op jit(solution)/shard_map/ppermute | solution.py:34
  303.7 17.8 %collective-permute-start.68 = (bf16[256,768]{1,0:T(8,128)(2,1)}, bf16[256,768]{1,0:T(8,128)(2,1)}, u32[]{:S(2)}, u32[]{:S(2)}) collective-permute-start(bf16[256,768]{1,0:T(8,128)(2,1)} %collective-permute-done.60), channel_id=1, source_target_pairs={{0,4},{1,5},{2,6},{3,7},{4,0},{5,1},{6,2},{7,3},{8,12},{9,13},{10,... | collective-permute-start | bytes 1179656 | tf_op jit(solution)/shard_map/ppermute | solution.py:34
  335.2 13.4 %collective-permute-start.73 = (bf16[320,384]{1,0:T(8,128)(2,1)S(1)}, bf16[320,384]{1,0:T(8,128)(2,1)S(1)}, u32[]{:S(2)}, u32[]{:S(2)}) collective-permute-start(bf16[320,384]{1,0:T(8,128)(2,1)S(1)} %get-tuple-element.176), channel_id=1, source_target_pairs={{0,8},{1,9},{2,10},{3,11},{4,12},{5,13},{6,14},{7,15},{8,0},{9,1},... | collective-permute-start | bytes 737288 | tf_op jit(solution)/shard_map/ppermute | solution.py:34
  336.4 12.2 %collective-permute-start.74 = (bf16[320,384]{1,0:T(8,128)(2,1)S(1)}, bf16[320,384]{1,0:T(8,128)(2,1)S(1)}, u32[]{:S(2)}, u32[]{:S(2)}) collective-permute-start(bf16[320,384]{1,0:T(8,128)(2,1)S(1)} %get-tuple-element.177), channel_id=1, source_target_pairs={{0,9},{1,8},{2,11},{3,10},{4,13},{5,12},{6,15},{7,14},{8,1},{9,0},... | collective-permute-start | bytes 737288 | tf_op jit(solution)/shard_map/ppermute | solution.py:34
  360.6 14.1 %collective-permute-start.80 = (bf16[640,384]{1,0:T(8,128)(2,1)S(1)}, bf16[640,384]{1,0:T(8,128)(2,1)S(1)}, u32[]{:S(2)}, u32[]{:S(2)}) collective-permute-start(bf16[640,384]{1,0:T(8,128)(2,1)S(1)} %add.257), channel_id=1, source_target_pairs={{0,16},{1,17},{2,18},{3,19},{4,20},{5,21},{6,22},{7,23},{8,24},{9,... | collective-permute-start | bytes 1474568 | tf_op jit(solution)/shard_map/ppermute | solution.py:34
  362.2 22.2 %collective-permute-start.83 = (bf16[640,384]{1,0:T(8,128)(2,1)S(1)}, bf16[640,384]{1,0:T(8,128)(2,1)S(1)}, u32[]{:S(2)}, u32[]{:S(2)}) collective-permute-start(bf16[640,384]{1,0:T(8,128)(2,1)S(1)} %add.259), channel_id=1, source_target_pairs={{0,16},{1,17},{2,18},{3,19},{4,20},{5,21},{6,22},{7,23},{8,24},{9,... | collective-permute-start | bytes 1474568 | tf_op jit(solution)/shard_map/ppermute | solution.py:34
  374.8 11.8 %collective-permute-start.81 = (bf16[320,384]{1,0:T(8,128)(2,1)S(1)}, bf16[320,384]{1,0:T(8,128)(2,1)S(1)}, u32[]{:S(2)}, u32[]{:S(2)}) collective-permute-start(bf16[320,384]{1,0:T(8,128)(2,1)S(1)} %get-tuple-element.341), channel_id=1, source_target_pairs={{0,1},{1,0},{2,3},{3,2},{4,5},{5,4},{6,7},{7,6},{8,9},{9,8},{10,11... | collective-permute-start | bytes 737288 | tf_op jit(solution)/shard_map/ppermute | solution.py:34
  385.4 12.2 %collective-permute-start.84 = (bf16[320,384]{1,0:T(8,128)(2,1)S(1)}, bf16[320,384]{1,0:T(8,128)(2,1)S(1)}, u32[]{:S(2)}, u32[]{:S(2)}) collective-permute-start(bf16[320,384]{1,0:T(8,128)(2,1)S(1)} %get-tuple-element.315), channel_id=1, source_target_pairs={{0,8},{1,9},{2,10},{3,11},{4,12},{5,13},{6,14},{7,15},{8,0},{9,1},... | collective-permute-start | bytes 737288 | tf_op jit(solution)/shard_map/ppermute | solution.py:34
  400.5 30.0 %collective-permute-start.87 = (bf16[768,768]{1,0:T(8,128)(2,1)S(1)}, bf16[768,768]{1,0:T(8,128)(2,1)}, u32[]{:S(2)}, u32[]{:S(2)}) collective-permute-start(bf16[768,768]{1,0:T(8,128)(2,1)S(1)} %copy-done.147), channel_id=1, source_target_pairs={{0,3},{1,5},{2,1},{3,7},{4,2},{5,4},{6,0},{7,6},{8,11},{9,13},{10,... | collective-permute-start | bytes 3538952 | tf_op jit(solution)/shard_map/ppermute | solution.py:34
  437.7 20.8 %collective-permute-start.90 = (bf16[1,2,192,768]{3,2,1,0:T(8,128)(2,1)S(1)}, bf16[1,2,192,768]{3,2,1,0:T(8,128)(2,1)S(1)}, u32[]{:S(2)}, u32[]{:S(2)}) collective-permute-start(bf16[1,2,192,768]{3,2,1,0:T(8,128)(2,1)S(1)} %bitcast.148), channel_id=1, source_target_pairs={{0,8},{1,9},{2,10},{3,11},{4,12},{5,13},{6,14},{7,15},{8,0},{9,1},... | collective-permute-start | bytes 1769480 | tf_op jit(solution)/shard_map/ppermute | solution.py:34
  438.9 20.4 %collective-permute-start.89 = (bf16[1024,384]{1,0:T(8,128)(2,1)S(1)}, bf16[1024,384]{1,0:T(8,128)(2,1)S(1)}, u32[]{:S(2)}, u32[]{:S(2)}) collective-permute-start(bf16[1024,384]{1,0:T(8,128)(2,1)S(1)} %add.262), channel_id=1, source_target_pairs={{0,16},{1,17},{2,18},{3,19},{4,20},{5,21},{6,22},{7,23},{8,24},{9,... | collective-permute-start | bytes 2359304 | tf_op jit(solution)/shard_map/ppermute | solution.py:34
  443.3 15.2 %collective-permute-start.71 = (bf16[256,768]{1,0:T(8,128)(2,1)S(1)}, bf16[256,768]{1,0:T(8,128)(2,1)S(1)}, u32[]{:S(2)}, u32[]{:S(2)}) collective-permute-start(bf16[256,768]{1,0:T(8,128)(2,1)S(1)} %get-tuple-element.287), channel_id=1, source_target_pairs={{0,3},{1,2},{2,7},{3,6},{4,1},{5,0},{6,5},{7,4},{8,11},{9,10},{10,... | collective-permute-start | bytes 1179656 | tf_op jit(solution)/shard_map/ppermute | solution.py:34
  473.9 13.0 %collective-permute-start.93 = (bf16[320,384]{1,0:T(8,128)(2,1)S(1)}, bf16[320,384]{1,0:T(8,128)(2,1)S(1)}, u32[]{:S(2)}, u32[]{:S(2)}) collective-permute-start(bf16[320,384]{1,0:T(8,128)(2,1)S(1)} %get-tuple-element.211), channel_id=1, source_target_pairs={{0,8},{1,9},{2,10},{3,11},{4,12},{5,13},{6,14},{7,15},{8,0},{9,1},... | collective-permute-start | bytes 737288 | tf_op jit(solution)/shard_map/ppermute | solution.py:34
  474.8 12.0 %collective-permute-start.94 = (bf16[320,384]{1,0:T(8,128)(2,1)S(1)}, bf16[320,384]{1,0:T(8,128)(2,1)S(1)}, u32[]{:S(2)}, u32[]{:S(2)}) collective-permute-start(bf16[320,384]{1,0:T(8,128)(2,1)S(1)} %get-tuple-element.212), channel_id=1, source_target_pairs={{0,9},{1,8},{2,11},{3,10},{4,13},{5,12},{6,15},{7,14},{8,1},{9,0},... | collective-permute-start | bytes 737288 | tf_op jit(solution)/shard_map/ppermute | solution.py:34
  475.4 12.0 %collective-permute-start.95 = (bf16[320,384]{1,0:T(8,128)(2,1)S(1)}, bf16[320,384]{1,0:T(8,128)(2,1)S(1)}, u32[]{:S(2)}, u32[]{:S(2)}) collective-permute-start(bf16[320,384]{1,0:T(8,128)(2,1)S(1)} %get-tuple-element.209.refs_0_.refs_8_), channel_id=1, source_target_pairs={{0,4},{1,5},{2,6},{3,7},{4,0},{5,1},{6,2},{7,3},{8,12},{9,13},{10,... | collective-permute-start | bytes 737288 | tf_op jit(solution)/shard_map/ppermute | solution.py:34
  495.6 16.7 %collective-permute-start.101 = (bf16[2,192,768]{2,1,0:T(8,128)(2,1)S(1)}, bf16[2,192,768]{2,1,0:T(8,128)(2,1)S(1)}, u32[]{:S(2)}, u32[]{:S(2)}) collective-permute-start(bf16[2,192,768]{2,1,0:T(8,128)(2,1)S(1)} %add_bitcast_fusion.1), channel_id=1, source_target_pairs={{4,6},{5,7},{6,4},{7,5},{12,14},{13,15},{14,12},{15,13},{16,17},{1... | collective-permute-start | bytes 1769480 | tf_op jit(solution)/shard_map/ppermute | solution.py:34
  496.5 14.1 %collective-permute-start.99 = (bf16[640,384]{1,0:T(8,128)(2,1)S(1)}, bf16[640,384]{1,0:T(8,128)(2,1)}, u32[]{:S(2)}, u32[]{:S(2)}) collective-permute-start(bf16[640,384]{1,0:T(8,128)(2,1)S(1)} %get-tuple-element.215), channel_id=1, source_target_pairs={{0,4},{1,5},{2,6},{3,7},{4,0},{5,1},{6,2},{7,3},{8,12},{9,13},{10,... | collective-permute-start | bytes 1474568 | tf_op jit(solution)/shard_map/ppermute | solution.py:34
  500.2 13.2 %collective-permute-start.104 = (bf16[640,384]{1,0:T(8,128)(2,1)S(1)}, bf16[640,384]{1,0:T(8,128)(2,1)S(1)}, u32[]{:S(2)}, u32[]{:S(2)}) collective-permute-start(bf16[640,384]{1,0:T(8,128)(2,1)S(1)} %add.267), channel_id=1, source_target_pairs={{0,16},{1,17},{2,18},{3,19},{4,20},{5,21},{6,22},{7,23},{8,24},{9,... | collective-permute-start | bytes 1474568 | tf_op jit(solution)/shard_map/ppermute | solution.py:34
  511.8 12.9 %collective-permute-start.100 = (bf16[640,384]{1,0:T(8,128)(2,1)S(1)}, bf16[640,384]{1,0:T(8,128)(2,1)S(1)}, u32[]{:S(2)}, u32[]{:S(2)}) collective-permute-start(bf16[640,384]{1,0:T(8,128)(2,1)S(1)} %add.264), channel_id=1, source_target_pairs={{0,16},{1,17},{2,18},{3,19},{4,20},{5,21},{6,22},{7,23},{8,24},{9,... | collective-permute-start | bytes 1474568 | tf_op jit(solution)/shard_map/ppermute | solution.py:34
  513.6 12.3 %collective-permute-start.106 = (bf16[320,384]{1,0:T(8,128)(2,1)S(1)}, bf16[320,384]{1,0:T(8,128)(2,1)S(1)}, u32[]{:S(2)}, u32[]{:S(2)}) collective-permute-start(bf16[320,384]{1,0:T(8,128)(2,1)S(1)} %get-tuple-element.312), channel_id=1, source_target_pairs={{0,9},{1,8},{2,11},{3,10},{4,13},{5,12},{6,15},{7,14},{8,1},{9,0},... | collective-permute-start | bytes 737288 | tf_op jit(solution)/shard_map/ppermute | solution.py:34
  516.1 12.5 %collective-permute-start.105 = (bf16[320,384]{1,0:T(8,128)(2,1)S(1)}, bf16[320,384]{1,0:T(8,128)(2,1)S(1)}, u32[]{:S(2)}, u32[]{:S(2)}) collective-permute-start(bf16[320,384]{1,0:T(8,128)(2,1)S(1)} %get-tuple-element.313), channel_id=1, source_target_pairs={{0,8},{1,9},{2,10},{3,11},{4,12},{5,13},{6,14},{7,15},{8,0},{9,1},... | collective-permute-start | bytes 737288 | tf_op jit(solution)/shard_map/ppermute | solution.py:34
  535.4 28.8 %collective-permute-start.108 = (bf16[768,768]{1,0:T(8,128)(2,1)}, bf16[768,768]{1,0:T(8,128)(2,1)S(1)}, u32[]{:S(2)}, u32[]{:S(2)}) collective-permute-start(bf16[768,768]{1,0:T(8,128)(2,1)} %get-tuple-element.236), channel_id=1, source_target_pairs={{0,3},{1,5},{2,1},{3,7},{4,2},{5,4},{6,0},{7,6},{8,11},{9,13},{10,... | collective-permute-start | bytes 3538952 | tf_op jit(solution)/shard_map/ppermute | solution.py:34
  564.1 15.7 %collective-permute-start.109 = (bf16[1024,384]{1,0:T(8,128)(2,1)}, bf16[1024,384]{1,0:T(8,128)(2,1)S(1)}, u32[]{:S(2)}, u32[]{:S(2)}) collective-permute-start(bf16[1024,384]{1,0:T(8,128)(2,1)} %get-tuple-element.238), channel_id=1, source_target_pairs={{0,4},{1,5},{2,6},{3,7},{4,0},{5,1},{6,2},{7,3},{8,12},{9,13},{10,... | collective-permute-start | bytes 2359304 | tf_op jit(solution)/shard_map/ppermute | solution.py:34
  565.4 35.5 %collective-permute-start.126 = (bf16[768,768]{1,0:T(8,128)(2,1)}, bf16[768,768]{1,0:T(8,128)(2,1)}, u32[]{:S(2)}, u32[]{:S(2)}) collective-permute-start(bf16[768,768]{1,0:T(8,128)(2,1)} %get-tuple-element.185), channel_id=1, source_target_pairs={{0,1},{1,7},{2,3},{3,5},{4,0},{5,6},{6,2},{7,4},{8,9},{9,15},{10,1... | collective-permute-start | bytes 3538952 | tf_op jit(solution)/shard_map/ppermute | solution.py:34
  568.3 32.6 %collective-permute-start.125 = (bf16[768,768]{1,0:T(8,128)(2,1)}, bf16[768,768]{1,0:T(8,128)(2,1)}, u32[]{:S(2)}, u32[]{:S(2)}) collective-permute-start(bf16[768,768]{1,0:T(8,128)(2,1)} %get-tuple-element.222), channel_id=1, source_target_pairs={{0,1},{1,7},{2,3},{3,5},{4,0},{5,6},{6,2},{7,4},{8,9},{9,15},{10,1... | collective-permute-start | bytes 3538952 | tf_op jit(solution)/shard_map/ppermute | solution.py:34
  579.0 20.1 %collective-permute-start.114 = (bf16[1,2,192,768]{3,2,1,0:T(8,128)(2,1)}, bf16[1,2,192,768]{3,2,1,0:T(8,128)(2,1)}, u32[]{:S(2)}, u32[]{:S(2)}) collective-permute-start(bf16[1,2,192,768]{3,2,1,0:T(8,128)(2,1)} %bitcast.53), channel_id=1, source_target_pairs={{0,8},{1,9},{2,10},{3,11},{4,12},{5,13},{6,14},{7,15},{8,0},{9,1},... | collective-permute-start | bytes 1769480 | tf_op jit(solution)/shard_map/ppermute | solution.py:34
  580.1 17.5 %collective-permute-start.110 = (bf16[1024,384]{1,0:T(8,128)(2,1)S(1)}, bf16[1024,384]{1,0:T(8,128)(2,1)}, u32[]{:S(2)}, u32[]{:S(2)}) collective-permute-start(bf16[1024,384]{1,0:T(8,128)(2,1)S(1)} %add.270), channel_id=1, source_target_pairs={{0,16},{1,17},{2,18},{3,19},{4,20},{5,21},{6,22},{7,23},{8,24},{9,... | collective-permute-start | bytes 2359304 | tf_op jit(solution)/shard_map/ppermute | solution.py:34
  582.3 67.7 %collective-permute-start.117 = (bf16[192,768]{1,0:T(8,128)(2,1)}, bf16[192,768]{1,0:T(8,128)(2,1)S(1)}, u32[]{:S(2)}, u32[]{:S(2)}) collective-permute-start(bf16[192,768]{1,0:T(8,128)(2,1)} %select_bitcast_fusion.8), channel_id=1, source_target_pairs={{0,4},{1,5},{2,6},{3,7},{4,0},{5,1},{6,2},{7,3},{8,12},{9,13},{10,... | collective-permute-start | bytes 884744 | tf_op jit(solution)/shard_map/ppermute | solution.py:34
  604.6 60.0 %collective-permute-start.127 = (bf16[768,768]{1,0:T(8,128)(2,1)}, bf16[768,768]{1,0:T(8,128)(2,1)}, u32[]{:S(2)}, u32[]{:S(2)}) collective-permute-start(bf16[768,768]{1,0:T(8,128)(2,1)} %get-tuple-element.277), channel_id=1, source_target_pairs={{0,16},{1,17},{2,18},{3,19},{4,20},{5,21},{6,22},{7,23},{8,24},{9,... | collective-permute-start | bytes 3538952 | tf_op jit(solution)/shard_map/ppermute | solution.py:34
  612.6 27.4 %collective-permute-start.120 = (f32[2,4992]{1,0:T(2,128)S(1)}, f32[2,4992]{1,0:T(2,128)S(1)}, u32[]{:S(2)}, u32[]{:S(2)}) collective-permute-start(f32[2,4992]{1,0:T(2,128)S(1)} %pad_maximum_fusion.15), channel_id=1, source_target_pairs={{0,2},{1,3},{2,0},{3,1},{4,6},{5,7},{6,4},{7,5},{8,10},{9,11},{10,... | collective-permute-start | bytes 119816 | tf_op jit(solution)/shard_map/ppermute | solution.py:34
  644.8 21.9 %collective-permute-start.112 = (bf16[256,768]{1,0:T(8,128)(2,1)S(1)}, bf16[256,768]{1,0:T(8,128)(2,1)S(1)}, u32[]{:S(2)}, u32[]{:S(2)}) collective-permute-start(bf16[256,768]{1,0:T(8,128)(2,1)S(1)} %get-tuple-element.284), channel_id=1, source_target_pairs={{0,2},{1,3},{2,6},{3,7},{4,0},{5,1},{6,4},{7,5},{8,10},{9,11},{10,... | collective-permute-start | bytes 1179656 | tf_op jit(solution)/shard_map/ppermute | solution.py:34
  647.9 18.9 %collective-permute-start.113 = (bf16[256,768]{1,0:T(8,128)(2,1)S(1)}, bf16[256,768]{1,0:T(8,128)(2,1)}, u32[]{:S(2)}, u32[]{:S(2)}) collective-permute-start(bf16[256,768]{1,0:T(8,128)(2,1)S(1)} %get-tuple-element.285), channel_id=1, source_target_pairs={{0,3},{1,2},{2,7},{3,6},{4,1},{5,0},{6,5},{7,4},{8,11},{9,10},{10,... | collective-permute-start | bytes 1179656 | tf_op jit(solution)/shard_map/ppermute | solution.py:34
  (224 other events, 2095.4 us)
